TPU v7x, 128 devices: a whole 4x4x4 slice. The times are simulated.
128 devices in a mesh: blk: 32 (over y, x_hi, z), head: 4 (over x_lo, core).
Axes of the slice: x: 4 (x_hi: 2, x_lo: 2; x = x_hi * 2 + x_lo), y: 4, z: 4, core: 2. Of those that a mesh axis runs over, the one named last changes fastest.
Arguments:
- layer_input: bfloat16 [16384, 1024], P(('blk', 'head')), may hold values from -6 to 6
- attn_gain: float32 [1024], replicated, may hold values from 0.5 to 1.5
- w_query: bfloat16 [1024, 1024], P('blk', 'head'), may hold values from -0.1875 to 0.1875
- key_weight: bfloat16 [1024, 512], P('blk', 'head'), may hold values from -0.1875 to 0.1875
- value_weight: bfloat16 [1024, 512], P('blk', 'head'), may hold values from -0.1875 to 0.1875
- w_output: bfloat16 [1024, 1024], P('blk', 'head'), may hold values from -1.5 to 1.5
- query_gain: float32 [64], replicated, may hold values from 0.1 to 1.9
- key_gain: float32 [64], replicated, may hold values from 0.1 to 1.9
- ffn_gain: float32 [1024], replicated, may hold values from 0.5 to 1.5
- router: float32 [1024, 32], replicated, may hold values from -0.09375 to 0.09375
- w_gate: bfloat16 [32, 1024, 512], P('blk'), may hold values from -0.1875 to 0.1875
- w_up: bfloat16 [32, 1024, 512], P('blk'), may hold values from -0.1875 to 0.1875
- w_down: bfloat16 [32, 512, 1024], P('blk'), may hold values from -1 to 1
- routes: int32 [16384, 8], P(('blk', 'head')), may hold values from 0 to 31, all different within a row; in each aligned block of 128 rows (0 to 127, 128 to 255, ...) at most 40 rows name the same one
- doc_lengths: int32 [3], replicated, may hold values from 1 to 16382, as said below
- cotangent: bfloat16 [16384, 1024], P(('blk', 'head')), may hold values from -6 to 6
Outputs:
- layer_output: bfloat16 [16384, 1024], P(('blk', 'head'))
- input_grad: bfloat16 [16384, 1024], P(('blk', 'head'))
- attn_gain_grad: float32 [1024], replicated
- w_query_grad: float32 [1024, 1024], P('blk', 'head')
- w_key_grad: float32 [1024, 512], P('blk', 'head')
- w_value_grad: float32 [1024, 512], P('blk', 'head')
- w_output_grad: float32 [1024, 1024], P('blk', 'head')
- query_gain_grad: float32 [64], replicated
- key_gain_grad: float32 [64], replicated
- ffn_gain_grad: float32 [1024], replicated
- router_grad: float32 [1024, 32], replicated
- w_gate_grad: float32 [32, 1024, 512], P('blk')
- w_up_grad: float32 [32, 1024, 512], P('blk')
- w_down_grad: float32 [32, 512, 1024], P('blk')
Inputs may be any that keep to these rules, and one draw needn't show every extreme that they name: `routes`: in the rows of one device (its 128 tokens) no expert is named more than 40 times, and in some devices' rows one expert is named exactly 40 times; a token names 8 different experts. `doc_lengths`: the lengths sum to 16384; the first and the last are at most 256, so that the middle document begins within the first 512 positions and ends within the last 512.
All inputs are finite; a program needn't handle non-finite values.
Results may differ from a plain program's by a relative error of at most 0.035.
Values may be sent and summed in bfloat16 or wider, within the bound.
A program may use at most 128 MiB of HBM per device.

v0:
```python
import functools

import jax
import jax.numpy as jnp
from jax import lax
from jax.sharding import PartitionSpec as P

QUERY_HEADS = 16
KEY_VALUE_HEADS = 8
HEAD_SIZE = 64
TOPK = 8
EXP_DEV = 1
BLOCK = 256


EPSILON = 1e-06
ROPE_BASE = 10000.0
PRECISE = lax.Precision.HIGHEST


def side_by_side(arrays, axis, dim, along):
    ends, at = ([], 0)
    for a in arrays[:-1]:
        at += a.shape[along]
        ends.append(at)
    both = jnp.concatenate(arrays, axis=along)
    return tuple(jnp.split(lax.all_gather(both, axis, axis=dim, tiled=True), ends, axis=along))


def from_behind(block, axis, distance):
    devices = range(lax.axis_size(axis))
    route = [((i - distance) % len(devices), i) for i in devices]
    return lax.ppermute(block, axis, route)


def rms_scale(values, gain_row):
    return (
        values * lax.rsqrt(jnp.mean(values * values, axis=-1, keepdims=True) + EPSILON) * gain_row
    )


def position_tables(where_at, doc_lengths):
    endings = jnp.cumsum(doc_lengths)
    openings = endings - doc_lengths
    document = jnp.sum((where_at[:, None] >= endings[None, :]).astype(jnp.int32), axis=1)
    numbers = jnp.arange(doc_lengths.shape[0], dtype=jnp.int32)
    opening = jnp.sum(
        jnp.where(document[:, None] == numbers[None, :], openings[None, :], 0), axis=1
    )
    inside = where_at - opening
    return (document, inside, inside // BLOCK)


def rotary(values, inside):
    half_dim = values.shape[-1] // 2
    frequency = jnp.power(
        ROPE_BASE, -2.0 * jnp.arange(half_dim, dtype=jnp.float32) / values.shape[-1]
    )
    angles = inside.astype(jnp.float32)[:, None] * frequency[None, :]
    cosine_table = jnp.cos(angles)[:, None, :]
    sine_table = jnp.sin(angles)[:, None, :]
    first_half = values[..., :half_dim]
    second_half = values[..., half_dim:]
    return jnp.concatenate(
        [
            first_half * cosine_table - second_half * sine_table,
            second_half * cosine_table + first_half * sine_table,
        ],
        axis=-1,
    )


def head_prep(raw_heads, gain_row, inside):
    count_of_tokens = raw_heads.shape[0]
    split_heads = raw_heads.reshape(count_of_tokens, raw_heads.shape[1] // HEAD_SIZE, HEAD_SIZE)
    return rotary(rms_scale(split_heads, gain_row), inside).reshape(
        count_of_tokens, raw_heads.shape[1]
    )


def rebuild(gathered, shard_shape, blk_count, count_of_heads):
    blocks = gathered.reshape(blk_count, count_of_heads, shard_shape[0], shard_shape[1])
    return blocks.transpose(0, 2, 1, 3).reshape(
        blk_count * shard_shape[0], count_of_heads * shard_shape[1]
    )


def dismantle(whole, blk_count, count_of_heads):
    shard_rows = whole.shape[0] // blk_count
    shard_cols = whole.shape[1] // count_of_heads
    blocks = whole.reshape(blk_count, shard_rows, count_of_heads, shard_cols)
    return blocks.transpose(0, 2, 1, 3).reshape(blk_count * count_of_heads, shard_rows * shard_cols)


def to_heads(value):
    return lax.all_to_all(value, "head", split_axis=1, concat_axis=0, tiled=True)


def to_tokens(value):
    return lax.all_to_all(value, "head", split_axis=0, concat_axis=1, tiled=True)


def to_experts(value):
    return lax.all_to_all(value, "blk", split_axis=0, concat_axis=0, tiled=True)


def in_steps(one_step, carried, pieces, step_width):
    piece_rows = pieces[0].shape[0]
    step_count = piece_rows // step_width
    stacked = tuple(
        (
            piece_item.reshape((step_count, step_width) + piece_item.shape[1:])
            for piece_item in pieces
        )
    )

    def advance(inner, scan_item):
        step_index, parts = scan_item
        return (one_step(inner, parts, step_index * step_width), None)

    carried, unused_tail = lax.scan(
        advance, carried, (jnp.arange(step_count, dtype=jnp.int32), stacked)
    )
    return carried


def body(
    layer_input,
    attn_gain,
    w_query,
    key_weight,
    value_weight,
    w_output,
    query_gain,
    key_gain,
    ffn_gain,
    router,
    w_gate,
    w_up,
    w_down,
    routes,
    doc_lengths,
    cotangent,
):
    blk_count = lax.axis_size("blk")
    count_of_heads = lax.axis_size("head")
    blk_index = lax.axis_index("blk")
    head_index = lax.axis_index("head")
    count_of_tokens = layer_input.shape[0]
    model_width = layer_input.shape[1]
    query_count = count_of_tokens * count_of_heads
    local_query = QUERY_HEADS // count_of_heads
    local_key_value = KEY_VALUE_HEADS // count_of_heads
    group_factor = QUERY_HEADS // KEY_VALUE_HEADS
    query_width = local_query * HEAD_SIZE
    key_value_width = local_key_value * HEAD_SIZE
    scaling = HEAD_SIZE ** (-0.5)
    expert_count = EXP_DEV * blk_count
    capacity = min(count_of_tokens, 5 * count_of_tokens * TOPK // (4 * expert_count))
    pair_count = count_of_tokens * TOPK
    token_pos = (blk_index * count_of_heads + head_index) * count_of_tokens + jnp.arange(
        count_of_tokens, dtype=jnp.int32
    )
    token_inside = position_tables(token_pos, doc_lengths)[1]
    query_pos = blk_index * query_count + jnp.arange(query_count, dtype=jnp.int32)
    query_tables = position_tables(query_pos, doc_lengths)
    query_doc = query_tables[0]
    query_order = query_tables[2]
    gathered = (
        lax.all_gather(w_query.reshape(1, -1), ("blk", "head"), axis=0, tiled=True),
        lax.all_gather(key_weight.reshape(1, -1), ("blk", "head"), axis=0, tiled=True),
        lax.all_gather(value_weight.reshape(1, -1), ("blk", "head"), axis=0, tiled=True),
        lax.all_gather(w_output.reshape(1, -1), ("blk", "head"), axis=0, tiled=True),
    )
    query_full = rebuild(gathered[0], w_query.shape, blk_count, count_of_heads)
    key_full = rebuild(gathered[1], key_weight.shape, blk_count, count_of_heads)
    value_full = rebuild(gathered[2], value_weight.shape, blk_count, count_of_heads)
    output_full = rebuild(gathered[3], w_output.shape, blk_count, count_of_heads)
    source = layer_input.astype(jnp.float32)
    normed_wide, attn_pull = jax.vjp(rms_scale, source, attn_gain)
    normed = normed_wide.astype(jnp.bfloat16)
    query_raw = jnp.dot(normed, query_full, preferred_element_type=jnp.float32)
    key_raw = jnp.dot(normed, key_full, preferred_element_type=jnp.float32)
    value_raw = jnp.dot(normed, value_full, preferred_element_type=jnp.float32)
    query_prep, query_pull = jax.vjp(
        functools.partial(head_prep, inside=token_inside), query_raw, query_gain
    )
    key_prep, key_pull = jax.vjp(
        functools.partial(head_prep, inside=token_inside), key_raw, key_gain
    )
    packed = jnp.concatenate(
        [
            query_prep.reshape(count_of_tokens, count_of_heads, query_width),
            key_prep.reshape(count_of_tokens, count_of_heads, key_value_width),
            value_raw.reshape(count_of_tokens, count_of_heads, key_value_width),
        ],
        axis=2,
    )
    head_side = to_heads(
        packed.reshape(
            count_of_tokens, count_of_heads * (query_width + 2 * key_value_width)
        ).astype(jnp.bfloat16)
    )
    query_h = head_side[:, :query_width]
    key_h = head_side[:, query_width : query_width + key_value_width]
    value_h = head_side[:, query_width + key_value_width :]
    query_four = query_h.reshape(query_count, local_key_value, group_factor, HEAD_SIZE)

    def exponents(key_piece, begin_at):
        piece_rows = key_piece.shape[0]
        key_pos = begin_at + jnp.arange(piece_rows, dtype=jnp.int32)
        key_tables = position_tables(key_pos, doc_lengths)
        allowed = (query_doc[:, None] == key_tables[0][None, :]) & (
            key_tables[2][None, :] <= query_order[:, None]
        )
        key_three = key_piece.reshape(piece_rows, local_key_value, HEAD_SIZE)
        raw_scores = jnp.einsum(
            "qhgd,khd->hgqk", query_four, key_three, preferred_element_type=jnp.float32
        )
        exponent = jnp.where(allowed[None, None], jnp.exp(raw_scores * scaling), 0.0)
        return (exponent, key_three)

    def forward_step(carried, pieces, begin_at):
        numerator, totals = carried
        exponent, key_three = exponents(pieces[0], begin_at)
        value_three = pieces[1].reshape(pieces[1].shape[0], local_key_value, HEAD_SIZE)
        numerator = numerator + jnp.einsum(
            "hgqk,khd->qhgd",
            exponent.astype(jnp.bfloat16),
            value_three,
            preferred_element_type=jnp.float32,
        )
        return (numerator, totals + jnp.sum(exponent, axis=-1))

    start_numer = jnp.zeros((query_count, local_key_value, group_factor, HEAD_SIZE), jnp.float32)
    start_totals = jnp.zeros((local_key_value, group_factor, query_count), jnp.float32)
    numerator, totals = in_steps(
        forward_step,
        (start_numer, start_totals),
        side_by_side((key_h, value_h), "blk", 0, 1),
        query_count,
    )
    totals_query = totals.transpose(2, 0, 1)
    context_wide = numerator / totals_query[..., None]
    context_h = context_wide.reshape(query_count, query_width).astype(jnp.bfloat16)
    context_tok = to_tokens(context_h)
    middle = source + jnp.dot(context_tok, output_full, preferred_element_type=jnp.float32)
    mixed_wide, ffn_pull = jax.vjp(rms_scale, middle, ffn_gain)
    mixed_in = mixed_wide.astype(jnp.bfloat16)
    logits = jnp.dot(mixed_in.astype(jnp.float32), router, precision=PRECISE)
    numbers = jnp.arange(expert_count, dtype=jnp.int32)
    chosen = routes[:, :, None] == numbers[None, None, :]
    picked = jnp.sum(jnp.where(chosen, logits[:, None, :], 0.0), axis=2)
    gates = jax.nn.softmax(picked, axis=1)
    hit_table = chosen.reshape(pair_count, expert_count).astype(jnp.int32)
    placed = jnp.sum(jnp.cumsum(hit_table, axis=0) * hit_table, axis=1) - 1
    slot_index = routes.reshape(pair_count) * capacity + placed
    slot_owner = (
        jnp.zeros((expert_count * capacity,), jnp.int32)
        .at[slot_index]
        .set(jnp.arange(pair_count, dtype=jnp.int32))
    )
    slot_live = jnp.zeros((expert_count * capacity,), jnp.bool_).at[slot_index].set(True)
    outgoing = jnp.where(
        slot_live[:, None], mixed_in[slot_owner // TOPK], jnp.zeros((), jnp.bfloat16)
    )
    arrived = to_experts(outgoing.reshape(expert_count, capacity, model_width))
    expert_in = (
        arrived.reshape(blk_count, EXP_DEV, capacity, model_width)
        .transpose(1, 0, 2, 3)
        .reshape(EXP_DEV, blk_count * capacity, model_width)
    )
    gate_pre = jnp.einsum("erd,edf->erf", expert_in, w_gate, preferred_element_type=jnp.float32)
    up_pre = jnp.einsum("erd,edf->erf", expert_in, w_up, preferred_element_type=jnp.float32)
    sigmoid_gate = jax.nn.sigmoid(gate_pre)
    activated = gate_pre * sigmoid_gate
    hidden = (activated * up_pre).astype(jnp.bfloat16)
    expert_out = jnp.einsum(
        "erf,efd->erd", hidden, w_down, preferred_element_type=jnp.float32
    ).astype(jnp.bfloat16)
    returning = to_experts(
        expert_out.reshape(EXP_DEV, blk_count, capacity, model_width)
        .transpose(1, 0, 2, 3)
        .reshape(blk_count * EXP_DEV, capacity, model_width)
    )
    returned_rows = returning.reshape(expert_count * capacity, model_width)[slot_index].reshape(
        count_of_tokens, TOPK, model_width
    )
    mixture = jnp.sum(gates[:, :, None] * returned_rows.astype(jnp.float32), axis=1)
    layer_output = (middle + mixture).astype(jnp.bfloat16)
    upstream = cotangent.astype(jnp.float32)
    gate_grad = jnp.sum(upstream[:, None, :] * returned_rows.astype(jnp.float32), axis=2)
    out_grad = (
        (gates[:, :, None] * upstream[:, None, :])
        .astype(jnp.bfloat16)
        .reshape(pair_count, model_width)
    )
    grads_out = jnp.where(slot_live[:, None], out_grad[slot_owner], jnp.zeros((), jnp.bfloat16))
    grads_in = to_experts(grads_out.reshape(expert_count, capacity, model_width))
    grads_rows = (
        grads_in.reshape(blk_count, EXP_DEV, capacity, model_width)
        .transpose(1, 0, 2, 3)
        .reshape(EXP_DEV, blk_count * capacity, model_width)
    )
    hidden_grad = jnp.einsum("erd,efd->erf", grads_rows, w_down, preferred_element_type=jnp.float32)
    gate_back = (
        hidden_grad * up_pre * sigmoid_gate * (1.0 + gate_pre * (1.0 - sigmoid_gate))
    ).astype(jnp.bfloat16)
    up_back = (hidden_grad * activated).astype(jnp.bfloat16)
    rows_grad = jnp.einsum(
        "erf,edf->erd", gate_back, w_gate, preferred_element_type=jnp.float32
    ) + jnp.einsum("erf,edf->erd", up_back, w_up, preferred_element_type=jnp.float32)
    down_w_grad = jnp.einsum("erf,erd->efd", hidden, grads_rows, preferred_element_type=jnp.float32)
    gate_w_grad = jnp.einsum(
        "erd,erf->edf", expert_in, gate_back, preferred_element_type=jnp.float32
    )
    up_w_grad = jnp.einsum("erd,erf->edf", expert_in, up_back, preferred_element_type=jnp.float32)
    sent_back = lax.all_to_all(
        rows_grad.reshape(EXP_DEV, blk_count, capacity, model_width)
        .transpose(1, 0, 2, 3)
        .reshape(blk_count * EXP_DEV, capacity, model_width)
        .astype(jnp.bfloat16),
        "blk",
        split_axis=0,
        concat_axis=0,
        tiled=True,
    ).astype(jnp.float32)
    input_rows = sent_back.reshape(expert_count * capacity, model_width)[slot_index].reshape(
        count_of_tokens, TOPK, model_width
    )
    pick_grad = gates * (gate_grad - jnp.sum(gates * gate_grad, axis=1, keepdims=True))
    logit_grad = jnp.sum(jnp.where(chosen, pick_grad[:, :, None], 0.0), axis=1)
    router_grad = jnp.dot(mixed_in.astype(jnp.float32).T, logit_grad, precision=PRECISE)
    mixed_grad = jnp.sum(input_rows, axis=1) + jnp.dot(logit_grad, router.T, precision=PRECISE)
    middle_norm_grad, ffn_gain_grad = ffn_pull(mixed_grad)
    middle_grad = upstream + middle_norm_grad
    attn_grad = middle_grad.astype(jnp.bfloat16)
    output_w_grad = jnp.dot(context_tok.T, attn_grad, preferred_element_type=jnp.float32)
    context_grad = jnp.dot(attn_grad, output_full.T, preferred_element_type=jnp.float32).astype(
        jnp.bfloat16
    )
    context_grad_h = to_heads(context_grad)
    grad_wide = context_grad_h.astype(jnp.float32).reshape(
        query_count, local_key_value, group_factor, HEAD_SIZE
    )
    dot_term = jnp.sum(grad_wide * context_wide, axis=-1).transpose(1, 2, 0) / totals
    scaled_grad = (grad_wide / totals_query[..., None]).astype(jnp.bfloat16)

    def backward_terms(key_piece, value_piece, begin_at):
        exponent, key_three = exponents(key_piece, begin_at)
        value_three = value_piece.reshape(value_piece.shape[0], local_key_value, HEAD_SIZE)
        prob_grad = jnp.einsum(
            "qhgd,khd->hgqk", scaled_grad, value_three, preferred_element_type=jnp.float32
        )
        score_grad = (exponent * (prob_grad - dot_term[..., None])).astype(jnp.bfloat16)
        query_part = (
            jnp.einsum("hgqk,khd->qhgd", score_grad, key_three, preferred_element_type=jnp.float32)
            * scaling
        )
        key_part = (
            jnp.einsum("hgqk,qhgd->khd", score_grad, query_four, preferred_element_type=jnp.float32)
            * scaling
        )
        value_part = jnp.einsum(
            "hgqk,qhgd->khd",
            exponent.astype(jnp.bfloat16),
            scaled_grad,
            preferred_element_type=jnp.float32,
        )
        return (
            query_part,
            key_part.reshape(key_piece.shape[0], key_value_width),
            value_part.reshape(key_piece.shape[0], key_value_width),
        )

    zero_query = jnp.zeros((query_count, local_key_value, group_factor, HEAD_SIZE), jnp.float32)

    def cycle_turn(step_index, cycle_state):
        query_acc, key_now, value_now, key_acc, value_acc = cycle_state
        owner_index = (blk_index - step_index) % blk_count
        query_part, key_part, value_part = backward_terms(
            key_now, value_now, owner_index * query_count
        )
        moved_pairs = from_behind((key_now, value_now), "blk", 1)
        moved_grads = (
            from_behind((key_acc + key_part).astype(jnp.bfloat16), "blk", 1).astype(jnp.float32),
            from_behind((value_acc + value_part).astype(jnp.bfloat16), "blk", 1).astype(
                jnp.float32
            ),
        )
        return (
            query_acc + query_part,
            moved_pairs[0],
            moved_pairs[1],
            moved_grads[0],
            moved_grads[1],
        )

    zero_kv = jnp.zeros((query_count, key_value_width), jnp.float32)
    cycle_state = lax.fori_loop(
        0, blk_count, cycle_turn, (zero_query, key_h, value_h, zero_kv, zero_kv)
    )
    query_grad_h = cycle_state[0]
    key_grad_h = cycle_state[3]
    value_grad_h = cycle_state[4]
    back_packed = jnp.concatenate(
        [query_grad_h.reshape(query_count, query_width), key_grad_h, value_grad_h], axis=1
    ).astype(jnp.bfloat16)
    token_gradient_rows = to_tokens(back_packed).reshape(
        count_of_tokens, count_of_heads, query_width + 2 * key_value_width
    )
    query_tok_grad = token_gradient_rows[:, :, :query_width].reshape(
        count_of_tokens, QUERY_HEADS * HEAD_SIZE
    )
    key_token_gradient = token_gradient_rows[
        :, :, query_width : query_width + key_value_width
    ].reshape(count_of_tokens, KEY_VALUE_HEADS * HEAD_SIZE)
    value_token_gradient = token_gradient_rows[:, :, query_width + key_value_width :].reshape(
        count_of_tokens, KEY_VALUE_HEADS * HEAD_SIZE
    )
    query_raw_grad, query_gain_grad = query_pull(query_tok_grad.astype(jnp.float32))
    key_raw_grad, key_gain_grad = key_pull(key_token_gradient.astype(jnp.float32))
    query_raw_low = query_raw_grad.astype(jnp.bfloat16)
    key_raw_low = key_raw_grad.astype(jnp.bfloat16)
    normed_grad = jnp.dot(query_raw_low, query_full.T, preferred_element_type=jnp.float32)
    normed_grad = normed_grad + jnp.dot(key_raw_low, key_full.T, preferred_element_type=jnp.float32)
    normed_grad = normed_grad + jnp.dot(
        value_token_gradient, value_full.T, preferred_element_type=jnp.float32
    )
    source_norm_grad, attn_gain_grad = attn_pull(normed_grad)
    input_grad = (middle_grad + source_norm_grad).astype(jnp.bfloat16)
    query_w_grad = jnp.dot(normed.T, query_raw_low, preferred_element_type=jnp.float32)
    key_w_grad = jnp.dot(normed.T, key_raw_low, preferred_element_type=jnp.float32)
    value_w_grad = jnp.dot(normed.T, value_token_gradient, preferred_element_type=jnp.float32)
    shard_grads = (
        lax.psum_scatter(
            dismantle(query_w_grad, blk_count, count_of_heads),
            ("blk", "head"),
            scatter_dimension=0,
            tiled=True,
        ),
        lax.psum_scatter(
            dismantle(key_w_grad, blk_count, count_of_heads),
            ("blk", "head"),
            scatter_dimension=0,
            tiled=True,
        ),
        lax.psum_scatter(
            dismantle(value_w_grad, blk_count, count_of_heads),
            ("blk", "head"),
            scatter_dimension=0,
            tiled=True,
        ),
        lax.psum_scatter(
            dismantle(output_w_grad, blk_count, count_of_heads),
            ("blk", "head"),
            scatter_dimension=0,
            tiled=True,
        ),
    )
    query_shard = shard_grads[0].reshape(w_query.shape)
    key_shard = shard_grads[1].reshape(key_weight.shape)
    value_shard = shard_grads[2].reshape(value_weight.shape)
    output_shard = shard_grads[3].reshape(w_output.shape)
    expert_sums = (
        lax.psum(gate_w_grad.astype(jnp.bfloat16), "head").astype(jnp.float32),
        lax.psum(up_w_grad.astype(jnp.bfloat16), "head").astype(jnp.float32),
        lax.psum(down_w_grad.astype(jnp.bfloat16), "head").astype(jnp.float32),
    )
    small_sums = lax.psum(
        (attn_gain_grad, query_gain_grad, key_gain_grad, ffn_gain_grad, router_grad),
        ("blk", "head"),
    )
    return (
        layer_output,
        input_grad,
        small_sums[0],
        query_shard,
        key_shard,
        value_shard,
        output_shard,
        small_sums[1],
        small_sums[2],
        small_sums[3],
        small_sums[4],
        expert_sums[0],
        expert_sums[1],
        expert_sums[2],
    )


def solution(mesh):
    placed = (
        P(("blk", "head"), None),
        P(),
        P("blk", "head"),
        P("blk", "head"),
        P("blk", "head"),
        P("blk", "head"),
        P(),
        P(),
        P(),
        P(),
        P("blk", None, None),
        P("blk", None, None),
        P("blk", None, None),
        P(("blk", "head"), None),
        P(),
        P(("blk", "head"), None),
    )
    return jax.shard_map(
        body,
        mesh=mesh,
        in_specs=placed,
        out_specs=(
            P(("blk", "head"), None),
            P(("blk", "head"), None),
            P(),
            P("blk", "head"),
            P("blk", "head"),
            P("blk", "head"),
            P("blk", "head"),
            P(),
            P(),
            P(),
            P(),
            P("blk", None, None),
            P("blk", None, None),
            P("blk", None, None),
        ),
        check_vma=False,
    )
```

profile of v0, /device:TPU:4, one launch (start us, length us, event | category | flops | bytes accessed | tf_op | source)
XLA Modules:
  0.0 2161.4 jit_solution(17715184266600640756)
XLA Ops:
  14.9 191.4 %all-gather.14.cloned.1.call-done = bf16[128,1,4096]{2,1,0:T(2,128)(2,1)} async-done(((bf16[1,1,4096]{2,1,0:T(2,128)(2,1)}), bf16[128,1,4096]{2,1,0:T(2,128)(2,1)}) %all-gather.14.cloned.1.call-update) | async-done | bytes 1048592 | tf_op jit(solution)/shard_map/all_gather | solution.py:171
  206.2 7.7 reduce.5
  216.7 184.6 %all-gather.16.cloned.1.call-done = bf16[128,1,4096]{2,1,0:T(2,128)(2,1)} async-done(((bf16[1,1,4096]{2,1,0:T(2,128)(2,1)}), bf16[128,1,4096]{2,1,0:T(2,128)(2,1)}) %all-gather.16.cloned.1.call-update) | async-done | bytes 1048592 | tf_op jit(solution)/shard_map/all_gather | solution.py:172
  401.4 7.7 reduce.6
  416.8 183.4 %all-gather.12.cloned.1.call-done = bf16[128,1,8192]{2,1,0:T(2,128)(2,1)} async-done(((bf16[1,1,8192]{2,1,0:T(2,128)(2,1)}), bf16[128,1,8192]{2,1,0:T(2,128)(2,1)}) %all-gather.12.cloned.1.call-update) | async-done | bytes 2097168 | tf_op jit(solution)/shard_map/all_gather | solution.py:170
  600.2 13.0 reduce.4
  622.5 11.2 all_to_all.78
  635.9 9.0 reduce-window.24
  650.0 96.9 %all-gather.10.cloned.1.call-done = bf16[16384,256]{0,1:T(8,128)(2,1)} async-done(((bf16[512,256]{0,1:T(8,128)(2,1)}), bf16[16384,256]{0,1:T(8,128)(2,1)}) %all-gather.10.cloned.1.call-update) | async-done | bytes 8388624 | tf_op jit(solution)/shard_map/all_gather | solution.py:27
  755.1 287.7 %while.39 = (s32[]{:T(128)}, f32[512,2,2,64]{0,3,2,1:T(8,128)S(1)}, f32[2,2,512]{2,1,0:T(2,128)S(1)}, bf16[32,512,128]{1,2,0:T(8,128)(2,1)}, s32[512]{0:T(512)S(...) while((s32[]{:T(128)}, f32[512,2,2,64]{0,3,2,1:T(8,128)S(1)}, ...), condition=%wide.region_12.13_spmd.clone, body=%wide.region_8.12_spmd.clone.sunk | while | flops 275794944 | bytes 11327692 | solution.py:121
  1054.5 13.9 reduce.7
  1077.2 5.2 gather_fusion
  1083.9 5.1 gather_fusion.2
  1092.8 43.2 %all_to_all.79 = bf16[32,40,1024]{2,1,0:T(8,128)(2,1)} all-to-all(bf16[32,40,1024]{2,1,0:T(8,128)(2,1)S(1)} %get-tuple-element.725), channel_id=1, replica_groups=mesh['blk'=32,'head'=4] {'blk'}, dimensions={0} | all-to-all | bytes 5242880 | tf_op jit(solution)/shard_map/all_to_all | solution.py:104
  1136.0 7.5 all-to-all-start.4
  1143.6 4.9 fusion.45
  1151.5 24.6 %all-to-all-done.4 = bf16[32,40,1024]{2,1,0:T(8,128)(2,1)} async-done(((bf16[32,40,1024]{2,1,0:T(8,128)(2,1)}), bf16[32,40,1024]{2,1,0:T(8,128)(2,1)}, u32[]{:S(2)}, u32[]{:S(2)}) %all-to-all-start.4) | async-done | bytes 2621472 | tf_op jit(solution)/shard_map/all_to_all | solution.py:104
  1176.1 7.1 multiply_convert_fusion
  1186.3 9.4 all-to-all-start.3
  1202.1 26.5 %all-to-all-done.3 = bf16[32,40,1024]{2,1,0:T(8,128)(2,1)} async-done(((bf16[32,40,1024]{2,1,0:T(8,128)(2,1)}), bf16[32,40,1024]{2,1,0:T(8,128)(2,1)}, u32[]{:S(2)}, u32[]{:S(2)}) %all-to-all-start.3) | async-done | bytes 2621472 | tf_op jit(solution)/shard_map/all_to_all | solution.py:104
  1228.6 9.2 all-to-all-start.5
  1237.8 4.9 fusion.38
  1245.3 8.1 gather_fusion.1
  1257.6 11.8 all-to-all-done.5
  1269.5 4.7 bitcast_convert_fusion
  1274.2 8.9 gather_fusion.3
  1306.1 628.2 %while.40 = (s32[]{:T(128)}, f32[512,2,2,64]{0,3,2,1:T(8,128)S(1)}, bf16[512,128]{0,1:T(8,128)(2,1)S(1)}, bf16[512,128]{0,1:T(8,128)(2,1)S(1)}, f32[512,128]{0,1...) while((s32[]{:T(128)}, f32[512,2,2,64]{0,3,2,1:T(8,128)S(1)}, ...), condition=%wide.region_32.33_spmd.clone, body=%wide.region_29.32_spmd.clone.sunk | while | flops 681264128 | bytes 27425276 | solution.py:400
  1320.9 9.2 collective-permute-done.2
  1330.2 5.2 collective-permute-done.3
  1343.6 7.1 collective-permute-start.3
  1351.2 6.0 collective-permute-done.2
  1366.9 7.1 collective-permute-start.3
  1374.5 8.6 collective-permute-done.2
  1396.6 7.1 collective-permute-start.3
  1404.2 7.4 collective-permute-done.2
  1421.6 7.1 collective-permute-start.3
  1441.1 5.3 collective-permute-start.3
  1458.8 5.3 collective-permute-start.3
  1476.6 5.2 collective-permute-start.3
  1501.1 4.7 collective-permute-done.3
  1548.9 5.0 collective-permute-start.3
  1567.2 6.2 collective-permute-start.3
  1585.3 6.2 collective-permute-start.3
  1604.5 5.2 collective-permute-start.3
  1623.5 5.3 collective-permute-start.3
  1642.3 5.3 collective-permute-start.3
  1661.1 5.3 collective-permute-start.3
  1698.8 5.2 collective-permute-start.3
  1717.9 5.2 collective-permute-start.3
  1736.6 4.9 collective-permute-start.3
  1755.5 5.2 collective-permute-start.3
  1774.6 5.2 collective-permute-start.3
  1793.3 4.9 collective-permute-start.3
  1812.2 5.2 collective-permute-start.3
  1831.3 5.2 collective-permute-start.3
  1850.0 4.9 collective-permute-start.3
  1868.9 5.2 collective-permute-start.3
  1888.0 5.2 collective-permute-start.3
  1906.7 4.9 collective-permute-start.3
  1925.6 5.2 collective-permute-start.3
  1940.8 5.3 copy.232
  1960.2 5.5 copy.229
  1965.7 77.3 %all-reduce.8 = (f32[1024]{0:T(1024)}, f32[64]{0:T(128)}, f32[64]{0:T(128)}, f32[1024]{0:T(1024)}) all-reduce(f32[1024]{0:T(1024)S(1)} %get-tuple-element.626, f32[64]{0:T(128)S(1)} %get-tuple-element.624, f32[64]{0:T(128)S(1)} %get-tuple-element.628, f32[1024]{0:T(1024)S(1)} %get-tuple-element.622), channel_id=1, replica_groups=mesh['blk'=32,'head'=4] {'blk','head'}, use_global_device_ids=true, to_apply=%region_37.38 | all-reduce | flops 2176 | bytes 17408 | tf_op jit(solution)/shard_map/psum | solution.py:470
  2049.2 97.0 %all-reduce.14.cloned.1.call-done = (f32[128,8192]{1,0:T(8,128)}, f32[128,4096]{1,0:T(8,128)}, f32[128,4096]{1,0:T(8,128)}, f32[128,8192]{1,0:T(8,128)}, f32[1024,32]{0,1:T(8,128)}) async-done(((f32[128,8192]{1,0:T(8,128)}, f32[128,4096]{1,0:T(8,128)}, f32[128,4096]{1,0:T(8,128)}, f32[128,8192]{1,0:T(8,128)}, f32[1024,32]{0,1:T(8,128)}), (f32[128,8192]{1,0:T(8,128)}, f32[128,4096]{1,0:T(8,128)}, ...) | async-done | bytes 12714000
  (1419 shorter events, 843.8 us)
Async XLA Ops:
  7.2 199.0 %all-gather.14.cloned.1.call-start = ((), (), s32[]{:S(2)}) async-start(), calls=%async_computation.10 | async-start | bytes 2113536 | tf_op jit(solution)/shard_map/all_gather | solution.py:171
  8.7 392.7 %all-gather.16.cloned.1.call-start = ((), (), s32[]{:S(2)}) async-start(), calls=%async_computation.11 | async-start | bytes 2113536 | tf_op jit(solution)/shard_map/all_gather | solution.py:172
  10.0 590.2 %all-gather.12.cloned.1.call-start = ((), (), s32[]{:S(2)}) async-start(), calls=%async_computation.9 | async-start | bytes 4227072 | tf_op jit(solution)/shard_map/all_gather | solution.py:170
  11.5 735.4 %all-gather.10.cloned.1.call-start = ((), (), s32[]{:S(2)}) async-start(), calls=%async_computation.8 | async-start | bytes 8650752 | tf_op jit(solution)/shard_map/all_gather | solution.py:27
  634.7 419.9 %all-gather.18.cloned.1.call-start = ((), (), s32[]{:S(2)}) async-start(), calls=%async_computation.12 | async-start | bytes 4227072 | tf_op jit(solution)/shard_map/all_gather | solution.py:173
  1043.8 29.3 %all-to-all-start.1 = ((bf16[4,128,256]{1,2,0:T(8,128)(2,1)}), bf16[4,128,256]{1,2,0:T(8,128)(2,1)}, u32[]{:S(2)}, u32[]{:S(2)}) async-start(bf16[4,128,256]{1,2,0:T(8,128)(2,1)} %copy.183), calls=%async_computation.1 | async-start | bytes 524288 | tf_op jit(solution)/shard_map/all_to_all | solution.py:100
  1136.0 40.2 %all-to-all-start.4 = ((bf16[32,40,1024]{2,1,0:T(8,128)(2,1)}), bf16[32,40,1024]{2,1,0:T(8,128)(2,1)}, u32[]{:S(2)}, u32[]{:S(2)}) async-start(bf16[32,40,1024]{2,1,0:T(8,128)(2,1)} %get-tuple-element.724), calls=%async_computation.4 | async-start | bytes 5242880 | tf_op jit(solution)/shard_map/all_to_all | solution.py:104
  1186.3 42.3 %all-to-all-start.3 = ((bf16[32,40,1024]{2,1,0:T(8,128)(2,1)}), bf16[32,40,1024]{2,1,0:T(8,128)(2,1)}, u32[]{:S(2)}, u32[]{:S(2)}) async-start(bf16[32,40,1024]{2,1,0:T(8,128)(2,1)} %bitcast.482), calls=%async_computation.3 | async-start | bytes 5242880 | tf_op jit(solution)/shard_map/all_to_all | solution.py:104
  1228.6 40.9 %all-to-all-start.5 = ((bf16[32,40,1024]{2,1,0:T(8,128)(2,1)}), bf16[32,40,1024]{2,1,0:T(8,128)(2,1)}, u32[]{:S(2)}, u32[]{:S(2)}) async-start(bf16[32,40,1024]{2,1,0:T(8,128)(2,1)} %bitcast.444), calls=%async_computation.5 | async-start | bytes 5242880 | tf_op jit(solution)/shard_map/all_to_all | solution.py:318
  1293.3 749.7 %all-reduce.16.cloned.1.call-start = ((), (), s32[]{:S(2)}) async-start(), calls=%async_computation.14 | async-start | bytes 6291456 | tf_op jit(solution)/shard_map/psum | solution.py:466
  1306.2 29.3 %collective-permute-start = (bf16[512,128]{0,1:T(8,128)(2,1)S(1)}, bf16[512,128]{0,1:T(8,128)(2,1)S(1)}, u32[]{:S(2)}, u32[]{:S(2)}) collective-permute-start(bf16[512,128]{0,1:T(8,128)(2,1)S(1)} %copy.276), channel_id=1, source_target_pairs={{124,0},{0,4},{4,8},{8,12},{12,16},{16,20},{20,24},{24,28},{28,32}... | collective-permute-start | bytes 393224 | tf_op jit(solution)/shard_map/while/body/eval_jaxpr/ppermute | solution.py:33
  1307.9 27.6 %collective-permute-start.1 = (bf16[512,128]{0,1:T(8,128)(2,1)S(1)}, bf16[512,128]{0,1:T(8,128)(2,1)S(1)}, u32[]{:S(2)}, u32[]{:S(2)}) collective-permute-start(bf16[512,128]{0,1:T(8,128)(2,1)S(1)} %copy.277), channel_id=1, source_target_pairs={{124,0},{0,4},{4,8},{8,12},{12,16},{16,20},{20,24},{24,28},{28,32}... | collective-permute-start | bytes 393224 | tf_op jit(solution)/shard_map/while/body/eval_jaxpr/ppermute | solution.py:33
  1316.9 18.5 collective-permute-start.3
  1335.5 23.9 %collective-permute-start = (bf16[512,128]{0,1:T(8,128)(2,1)S(1)}, bf16[512,128]{0,1:T(8,128)(2,1)S(1)}, u32[]{:S(2)}, u32[]{:S(2)}) collective-permute-start(bf16[512,128]{0,1:T(8,128)(2,1)S(1)} %copy.276), channel_id=1, source_target_pairs={{124,0},{0,4},{4,8},{8,12},{12,16},{16,20},{20,24},{24,28},{28,32}... | collective-permute-start | bytes 393224 | tf_op jit(solution)/shard_map/while/body/eval_jaxpr/ppermute | solution.py:33
  1335.6 23.8 %collective-permute-start.1 = (bf16[512,128]{0,1:T(8,128)(2,1)S(1)}, bf16[512,128]{0,1:T(8,128)(2,1)S(1)}, u32[]{:S(2)}, u32[]{:S(2)}) collective-permute-start(bf16[512,128]{0,1:T(8,128)(2,1)S(1)} %copy.277), channel_id=1, source_target_pairs={{124,0},{0,4},{4,8},{8,12},{12,16},{16,20},{20,24},{24,28},{28,32}... | collective-permute-start | bytes 393224 | tf_op jit(solution)/shard_map/while/body/eval_jaxpr/ppermute | solution.py:33
  1359.4 28.2 %collective-permute-start = (bf16[512,128]{0,1:T(8,128)(2,1)S(1)}, bf16[512,128]{0,1:T(8,128)(2,1)S(1)}, u32[]{:S(2)}, u32[]{:S(2)}) collective-permute-start(bf16[512,128]{0,1:T(8,128)(2,1)S(1)} %copy.276), channel_id=1, source_target_pairs={{124,0},{0,4},{4,8},{8,12},{12,16},{16,20},{20,24},{24,28},{28,32}... | collective-permute-start | bytes 393224 | tf_op jit(solution)/shard_map/while/body/eval_jaxpr/ppermute | solution.py:33
  1359.5 28.1 %collective-permute-start.1 = (bf16[512,128]{0,1:T(8,128)(2,1)S(1)}, bf16[512,128]{0,1:T(8,128)(2,1)S(1)}, u32[]{:S(2)}, u32[]{:S(2)}) collective-permute-start(bf16[512,128]{0,1:T(8,128)(2,1)S(1)} %copy.277), channel_id=1, source_target_pairs={{124,0},{0,4},{4,8},{8,12},{12,16},{16,20},{20,24},{24,28},{28,32}... | collective-permute-start | bytes 393224 | tf_op jit(solution)/shard_map/while/body/eval_jaxpr/ppermute | solution.py:33
  1364.0 19.1 collective-permute-start.2
  1366.9 20.6 collective-permute-start.3
  1387.6 25.5 %collective-permute-start = (bf16[512,128]{0,1:T(8,128)(2,1)S(1)}, bf16[512,128]{0,1:T(8,128)(2,1)S(1)}, u32[]{:S(2)}, u32[]{:S(2)}) collective-permute-start(bf16[512,128]{0,1:T(8,128)(2,1)S(1)} %copy.276), channel_id=1, source_target_pairs={{124,0},{0,4},{4,8},{8,12},{12,16},{16,20},{20,24},{24,28},{28,32}... | collective-permute-start | bytes 393224 | tf_op jit(solution)/shard_map/while/body/eval_jaxpr/ppermute | solution.py:33
  1387.7 25.4 %collective-permute-start.1 = (bf16[512,128]{0,1:T(8,128)(2,1)S(1)}, bf16[512,128]{0,1:T(8,128)(2,1)S(1)}, u32[]{:S(2)}, u32[]{:S(2)}) collective-permute-start(bf16[512,128]{0,1:T(8,128)(2,1)S(1)} %copy.277), channel_id=1, source_target_pairs={{124,0},{0,4},{4,8},{8,12},{12,16},{16,20},{20,24},{24,28},{28,32}... | collective-permute-start | bytes 393224 | tf_op jit(solution)/shard_map/while/body/eval_jaxpr/ppermute | solution.py:33
  1392.3 19.3 collective-permute-start.2
  1413.2 18.1 collective-permute-start
  1413.3 18.0 collective-permute-start.1
  1431.3 18.5 collective-permute-start
  1485.4 20.5 collective-permute-start
  1487.9 18.0 collective-permute-start.1
  1521.9 18.5 collective-permute-start
  1540.4 18.5 collective-permute-start
  1541.0 18.0 collective-permute-start.1
  1576.9 18.4 collective-permute-start
  1595.4 18.5 collective-permute-start
  1614.0 19.7 collective-permute-start
  1614.8 18.8 collective-permute-start.1
  1633.7 18.1 collective-permute-start
  1651.8 19.4 collective-permute-start
  1652.7 18.5 collective-permute-start.1
  1671.3 18.8 collective-permute-start
  1671.6 18.6 collective-permute-start.1
  1690.2 18.5 collective-permute-start
  1690.3 18.4 collective-permute-start.1
  1708.7 19.4 collective-permute-start
  1709.2 18.9 collective-permute-start.1
  1728.1 18.4 collective-permute-start
  1728.3 18.3 collective-permute-start.1
  1746.6 19.1 collective-permute-start
  1746.7 19.0 collective-permute-start.1
  1765.7 18.8 collective-permute-start
  1765.9 18.6 collective-permute-start.1
  1784.6 18.9 collective-permute-start
  1785.0 18.5 collective-permute-start.1
  1803.5 18.6 collective-permute-start
  1803.6 18.5 collective-permute-start.1
  1822.1 19.3 collective-permute-start
  1822.6 18.9 collective-permute-start.1
  1841.5 18.4 collective-permute-start
  1841.7 18.3 collective-permute-start.1
  1860.0 19.1 collective-permute-start
  1860.1 19.0 collective-permute-start.1
  1879.1 18.8 collective-permute-start
  1879.3 18.6 collective-permute-start.1
  1897.9 18.9 collective-permute-start
  1898.3 18.5 collective-permute-start.1
  1938.8 207.4 %all-reduce.14.cloned.1.call-start = ((), (), s32[]{:S(2)}) async-start(), calls=%async_computation.13 | async-start | bytes 25427968
  (168 other events, 4643.3 us)
Sparse Core Ops, SparseCore 0:
  10.3 195.8 all-gather.13
  208.5 192.7 all-gather.15
  403.7 196.5 all-gather.11
  634.8 112.0 all-gather.9
  749.1 198.7 all-gather.17
  1298.1 91.8 all-reduce.15
  1965.8 180.3 all-reduce.13
where the time goes:
time: 2170 us; the launch traced here: 2160 us
  waiting for transfers between devices  972 us (45%)
  matrix products  450 us (21%)
  starting transfers between devices  289 us (13%)
  local copies, waits for them, and re-layouts  156 us (7%)
  blocking collectives  132 us (6%)
  other arithmetic  121 us (6%)
  loops' own time  26 us (1%)
    ppermute x128, starting transfers between devices, from_behind(): return lax.ppermute(block, axis, route)  251 us
    all_gather x1, waiting for transfers between devices, body(): lax.all_gather(key_weight.reshape(1, -1), ('blk', 'head'), axis=0, tiled=...  191 us
    all_gather x1, waiting for transfers between devices, body(): lax.all_gather(value_weight.reshape(1, -1), ('blk', 'head'), axis=0, tile...  185 us
    all_gather x1, waiting for transfers between devices, body(): lax.all_gather(w_query.reshape(1, -1), ('blk', 'head'), axis=0, tiled=True)  183 us
    ppermute x128, waiting for transfers between devices, from_behind(): return lax.ppermute(block, axis, route)  154 us
    dot_general x64, matrix products, exponents(): jnp.einsum('qhgd,khd->hgqk', query_four, key_three, preferred_element_typ...  122 us
    dot_general x32, matrix products, forward_step(): jnp.einsum('hgqk,khd->qhgd', exponent.astype(jnp.bfloat16), value_three,...  101 us
    unnamed x8, waiting for transfers between devices  97.2 us
  transfers between devices with their start and end apart: 141, of which 71 were waited for; matrix products, arithmetic and copies ran while one was open for 30% of the time, Pallas kernels for 0%

commit v1 on v0

v1 whole, which is shorter than its diff:
```python
import functools

import jax
import jax.numpy as jnp
from jax import lax
from jax.experimental import pallas as pl
from jax.experimental.pallas import tpu as pltpu
from jax.sharding import PartitionSpec as P

HEAD_SIZE = 64
TOPK = 8
BLOCK = 256
EPSILON = 1e-06
ROPE_BASE = 10000.0
PRECISE = lax.Precision.HIGHEST
SCALE = HEAD_SIZE ** (-0.5)

NB = 32
GROUP = 4
MESH_ID = pl.DeviceIdType.MESH
F32 = jnp.float32
BF16 = jnp.bfloat16
NT = (((1,), (1,)), ((), ()))
NN = (((1,), (0,)), ((), ()))
TN = (((0,), (0,)), ((), ()))


def place():
    b = lax.axis_index("blk")
    h = lax.axis_index("head")
    y = b // 8
    r = lax.rem(b, 8)
    m = jnp.where(lax.rem(y, 2) == 0, r, 7 - r)
    return b, h // 2, lax.rem(h, 2), y, m


def member(m, j):
    return 8 * j + m + lax.rem(j, 2) * (7 - 2 * m)


def times(start, n, body):
    def step(i, carry):
        body(i)
        return carry

    lax.fori_loop(start, n, step, 0)


def signal(sem, blk, head):
    pl.semaphore_signal(sem, inc=1, device_id=(blk, head), device_id_type=MESH_ID)


def rows(start, size):
    return pl.ds(pl.multiple_of(start, size), size)


def exchange(kernel, collective_id, out_shapes, sems, *operands):
    anyspec = pl.BlockSpec(memory_space=pl.ANY)
    return pl.pallas_call(
        kernel,
        out_shape=out_shapes,
        in_specs=[anyspec] * len(operands),
        out_specs=[anyspec] * len(out_shapes),
        scratch_shapes=[pltpu.SemaphoreType.DMA(s) for s in sems],
        compiler_params=pltpu.CompilerParams(collective_id=collective_id, has_side_effects=True),
    )(*operands)


def to(src, dst, send, recv, blk, head):
    return pltpu.make_async_remote_copy(
        src, dst, send, recv, device_id=(blk, head), device_id_type=MESH_ID
    )


def weights_kernel(ws, wo, li, w_out, wo_out, li_out, s1, r1, s2, r2, s3, r3, s4, r4, sx, rx, ls):
    b, xl, c, _, _ = place()
    h = 2 * xl + c
    sib = 2 * xl + 1 - c
    over = 2 * (1 - xl) + c
    bar = pltpu.get_barrier_semaphore()
    times(1, NB, lambda d: signal(bar, lax.rem(b + d, NB), h))
    times(0, NB, lambda d: signal(bar, lax.rem(b + d, NB), over))
    signal(bar, b, sib)
    pl.semaphore_wait(bar, 2 * NB)

    def first(d):
        return to(ws, w_out.at[c, rows(b * 32, 32)], s1.at[d], r1.at[d], lax.rem(b + d, NB), h)

    def second(d):
        src = lax.rem(b + NB - d, NB)
        part = w_out.at[c, rows(src * 32, 32)]
        return to(part, part, s2.at[d], r2.at[d], b, sib)

    def third(e):
        d, x2 = lax.rem(e, NB), lax.rem(xl + e // NB, 2)
        part = wo_out.at[h, rows(b * 32, 32)]
        return to(wo, part, s3.at[e], r3.at[e], lax.rem(b + d, NB), 2 * x2 + c)

    def fourth(e):
        d, x2 = lax.rem(e, NB), lax.rem(xl + e // NB, 2)
        part = wo_out.at[2 * x2 + c, rows(lax.rem(b + NB - d, NB) * 32, 32)]
        return to(part, part, s4.at[e], r4.at[e], b, sib)

    cross = to(li, li_out.at[xl], sx, rx, b, over)
    cross.start()
    times(1, NB, lambda d: first(d).start())
    times(1, 2 * NB, lambda e: third(e).start())
    own_w = pltpu.make_async_copy(ws, w_out.at[c, rows(b * 32, 32)], ls.at[0])
    own_w.start()
    own_li = pltpu.make_async_copy(li, li_out.at[xl], ls.at[1])
    own_li.start()
    own_wo = pltpu.make_async_copy(wo, wo_out.at[h, rows(b * 32, 32)], ls.at[2])
    own_wo.start()
    to_sib = to(ws, w_out.at[c, rows(b * 32, 32)], s2.at[0], r2.at[0], b, sib)
    to_sib.start()
    wo_sib = to(wo, wo_out.at[h, rows(b * 32, 32)], s4.at[0], r4.at[0], b, sib)
    wo_sib.start()

    def relay(d):
        first(d).wait_recv()
        second(d).start()

    def relay_wo(e):
        third(e).wait_recv()
        fourth(e).start()

    times(1, NB, relay)
    times(1, 2 * NB, relay_wo)
    times(1, NB, lambda d: first(d).wait_send())
    times(1, 2 * NB, lambda e: third(e).wait_send())
    to_sib.wait()
    wo_sib.wait()
    times(1, NB, lambda d: second(d).wait())
    times(1, 2 * NB, lambda e: fourth(e).wait())
    cross.wait()
    own_w.wait()
    own_li.wait()
    own_wo.wait()


def qkv_kernel(q, kv, q_out, kv_out, s1, r1, s2, r2, ls):
    b, xl, c, y, m = place()
    h = 2 * xl + c
    bar = pltpu.get_barrier_semaphore()
    times(1, NB, lambda d: signal(bar, lax.rem(b + d, NB), h))
    for dj in range(GROUP):
        signal(bar, member(m, lax.rem(y + dj, GROUP)), 2 * xl + 1 - c)
    pl.semaphore_wait(bar, NB - 1 + GROUP)

    def big(d):
        peer = lax.rem(b + d, NB)
        cols = pl.ds(pl.multiple_of((peer // 8) * 128, 128), 128)
        return to(kv.at[:, cols], kv_out.at[b], s1.at[d], r1.at[d], peer, h)

    def small(dj, dc):
        j = lax.rem(y + dj, GROUP)
        c2 = lax.rem(c + dc, 2)
        cols = pl.ds(pl.multiple_of(j * 128, 128), 128)
        k = 2 * dj + dc
        src, dst = q.at[:, cols], q_out.at[y, rows(c * 256, 256)]
        if k == 0:
            return pltpu.make_async_copy(src, dst, ls.at[0])
        return to(src, dst, s2.at[k], r2.at[k], member(m, j), 2 * xl + c2)

    smalls = [small(dj, dc) for dj in range(GROUP) for dc in range(2)]
    for item in smalls:
        item.start()
    own_cols = pl.ds(pl.multiple_of(y * 128, 128), 128)
    own = pltpu.make_async_copy(kv.at[:, own_cols], kv_out.at[b], ls.at[1])
    own.start()
    times(1, NB, lambda d: big(d).start())
    for item in smalls:
        item.wait()
    own.wait()
    times(1, NB, lambda d: big(d).wait())


def context_kernel(ctx, out, s1, r1, ls):
    b, xl, c, y, m = place()
    bar = pltpu.get_barrier_semaphore()

    def copies(make):
        done = []
        for dj in range(GROUP):
            for dx in range(2):
                done.append(make(dj, dx))
        return done

    def greet(dj, dx):
        if dj + dx > 0:
            x2 = lax.rem(xl + dx, 2)
            signal(bar, member(m, lax.rem(y + dj, GROUP)), 2 * x2 + c)

    copies(greet)
    pl.semaphore_wait(bar, 2 * GROUP - 1)

    def piece(dj, dx):
        j = lax.rem(y + dj, GROUP)
        x2 = lax.rem(xl + dx, 2)
        cols = pl.ds(pl.multiple_of((4 * xl + y) * 128, 128), 128)
        src, dst = ctx.at[j, rows(c * 256 + x2 * 128, 128)], out.at[:, cols]
        k = 2 * dj + dx
        if k == 0:
            return pltpu.make_async_copy(src, dst, ls)
        return to(src, dst, s1.at[k], r1.at[k], member(m, j), 2 * x2 + c)

    parts = copies(piece)
    for item in parts:
        item.start()
    for item in parts:
        item.wait()


def context_grad_kernel(cg, out, s1, r1, ls):
    b, xl, c, y, m = place()
    bar = pltpu.get_barrier_semaphore()
    turns = [(dj, dx, dc) for dj in range(GROUP) for dx in range(2) for dc in range(2)]

    def where(dj, dx, dc):
        j = lax.rem(y + dj, GROUP)
        x2 = lax.rem(xl + dx, 2)
        return j, x2, member(m, j), 2 * x2 + lax.rem(c + dc, 2)

    for turn in turns[1:]:
        _, _, blk, head = where(*turn)
        signal(bar, blk, head)
    pl.semaphore_wait(bar, len(turns) - 1)

    parts = []
    for k, turn in enumerate(turns):
        j, x2, blk, head = where(*turn)
        cols = pl.ds(pl.multiple_of((4 * x2 + j) * 128, 128), 128)
        src, dst = cg.at[:, cols], out.at[y, rows(c * 256 + xl * 128, 128)]
        if k == 0:
            parts.append(pltpu.make_async_copy(src, dst, ls))
        else:
            parts.append(to(src, dst, s1.at[k], r1.at[k], blk, head))
    for item in parts:
        item.start()
    for item in parts:
        item.wait()


def qkv_grad_kernel(dq, dkv, dq_out, dkv_out, s1, r1, s2, r2, ls):
    b, xl, c, y, m = place()
    h = 2 * xl + c
    bar = pltpu.get_barrier_semaphore()
    times(1, NB, lambda d: signal(bar, lax.rem(b + d, NB), h))
    for dj in range(GROUP):
        signal(bar, member(m, lax.rem(y + dj, GROUP)), 2 * xl + 1 - c)
    pl.semaphore_wait(bar, NB - 1 + GROUP)

    def big(d):
        peer = lax.rem(b + d, NB)
        return to(dkv.at[peer], dkv_out.at[b], s1.at[d], r1.at[d], peer, h)

    def small(dj, dc):
        j = lax.rem(y + dj, GROUP)
        c2 = lax.rem(c + dc, 2)
        cols = pl.ds(pl.multiple_of(y * 128, 128), 128)
        src, dst = dq.at[j, rows(c2 * 256, 256)], dq_out.at[c, :, cols]
        k = 2 * dj + dc
        if k == 0:
            return pltpu.make_async_copy(src, dst, ls.at[0])
        return to(src, dst, s2.at[k], r2.at[k], member(m, j), 2 * xl + c2)

    smalls = [small(dj, dc) for dj in range(GROUP) for dc in range(2)]
    for item in smalls:
        item.start()
    own = pltpu.make_async_copy(dkv.at[b], dkv_out.at[b], ls.at[1])
    own.start()
    times(1, NB, lambda d: big(d).start())
    for item in smalls:
        item.wait()
    own.wait()
    times(1, NB, lambda d: big(d).wait())


def scatter_kernel(parts, out, s1, r1, ls):
    b, xl, c, _, _ = place()
    h = 2 * xl + c
    bar = pltpu.get_barrier_semaphore()
    times(1, NB, lambda d: signal(bar, lax.rem(b + d, NB), h))
    pl.semaphore_wait(bar, NB - 1)

    def big(d):
        peer = lax.rem(b + d, NB)
        return to(parts.at[peer], out.at[b], s1.at[d], r1.at[d], peer, h)

    own = pltpu.make_async_copy(parts.at[b], out.at[b], ls)
    own.start()
    times(1, NB, lambda d: big(d).start())
    own.wait()
    times(1, NB, lambda d: big(d).wait())


def small_sum_kernel(x, out, four, many, s1, r1, s2, r2):
    b = lax.axis_index("blk")
    h = lax.axis_index("head")
    bar = pltpu.get_barrier_semaphore()
    for d in range(1, 4):
        signal(bar, b, lax.rem(h + d, 4))
    times(1, NB, lambda d: signal(bar, lax.rem(b + d, NB), h))
    pl.semaphore_wait(bar, NB + 2)
    four[h] = x[...]
    near = [
        to(x, four.at[h], s1.at[d], r1.at[d], b, lax.rem(h + d, 4)) for d in range(1, 4)
    ]
    for item in near:
        item.start()
    for item in near:
        item.wait()
    many[b] = four[0] + four[1] + four[2] + four[3]

    def far(d):
        return to(many.at[b], many.at[b], s2.at[d], r2.at[d], lax.rem(b + d, NB), h)

    times(1, NB, lambda d: far(d).start())
    times(1, NB, lambda d: far(d).wait())
    total = many[0]
    for i in range(1, NB):
        total = total + many[i]
    out[...] = total


def small_sum(x):
    vm = pl.BlockSpec(memory_space=pltpu.VMEM)
    dma = pltpu.SemaphoreType.DMA
    return pl.pallas_call(
        small_sum_kernel,
        out_shape=jax.ShapeDtypeStruct(x.shape, x.dtype),
        in_specs=[vm],
        out_specs=vm,
        scratch_shapes=[
            pltpu.VMEM((4,) + x.shape, x.dtype),
            pltpu.VMEM((NB,) + x.shape, x.dtype),
            dma((4,)),
            dma((4,)),
            dma((NB,)),
            dma((NB,)),
        ],
        compiler_params=pltpu.CompilerParams(collective_id=6, has_side_effects=True),
    )(x)


def limits(pos, e0, e1, total):
    low = jnp.where(pos < e0, 0, jnp.where(pos < e1, e0, e1))
    end = jnp.where(pos < e0, e0, jnp.where(pos < e1, e1, total))
    reach = low + ((pos - low) // BLOCK + 1) * BLOCK
    return low, jnp.minimum(end, reach)


def query_positions(shape, axis, qb):
    r = lax.broadcasted_iota(jnp.int32, shape, axis)
    r = lax.rem(r, 512)
    return 512 * qb + 256 * lax.rem(r // 128, 2) + 128 * (r // 256) + lax.rem(r, 128)


def key_positions(shape, axis, kb, core):
    r = lax.broadcasted_iota(jnp.int32, shape, axis)
    return 512 * kb + 256 * (r // 128) + 128 * core + lax.rem(r, 128)


def over_keys(info, i, body):
    e0, e1, total, core = info[0], info[1], info[2], info[3]
    qb = info[4 + i]
    first_low, first_high = limits(512 * qb, e0, e1, total)
    last_low, last_high = limits(512 * qb + 511, e0, e1, total)

    def step(kb, carry):
        start = 512 * kb
        reached = last_high > start + 128 * core
        whole = (last_low <= start) & (first_high > start + 511)
        pl.when(whole)(lambda: body(kb, False))
        pl.when(reached & jnp.logical_not(whole))(lambda: body(kb, True))
        return carry

    lax.fori_loop(0, jnp.minimum(qb + 2, NB), step, 0)


def forward_kernel(info, q_ref, kv_ref, out_ref, qp, vx, acc):
    e0, e1, total, core = info[0], info[1], info[2], info[3]
    left = lax.broadcasted_iota(jnp.int32, (256, 128), 1) < 64
    left_q = lax.broadcasted_iota(jnp.int32, (512, 128), 1) < 64

    def ones(kb, carry):
        vx[kb] = jnp.where(left, 1.0, kv_ref[kb].astype(F32)).astype(BF16)
        return carry

    lax.fori_loop(0, NB, ones, 0)
    for i in range(GROUP):
        qb = info[4 + i]
        both = q_ref[i].astype(F32)
        qp[0:512] = jnp.where(left_q, both, 0.0).astype(BF16)
        qp[512:1024] = jnp.where(left_q, pltpu.roll(both, 64, 1), 0.0).astype(BF16)
        acc[...] = jnp.zeros_like(acc)

        def body(kb, masked):
            keys = kv_ref[kb]
            scores = lax.dot_general(qp[...], keys, NT, preferred_element_type=F32)
            expo = jnp.exp(scores)
            if masked:
                low, high = limits(query_positions((1024, 1), 0, qb), e0, e1, total)
                kpos = key_positions((1, 256), 1, kb, core)
                expo = jnp.where((kpos >= low) & (kpos < high), expo, 0.0)
            acc[...] += jnp.dot(expo.astype(BF16), vx[kb], preferred_element_type=F32)

        over_keys(info, i, body)
        out_ref[i, 0] = acc[0:512]
        out_ref[i, 1] = acc[512:1024]


def combine_kernel(a_ref, b_ref, ctx_ref, wide_ref, inv_ref):
    left = lax.broadcasted_iota(jnp.int32, (512, 128), 1) < 64
    for i in range(GROUP):
        one = a_ref[i, 0] + b_ref[i, 0]
        two = a_ref[i, 1] + b_ref[i, 1]
        totals = jnp.where(left, one, pltpu.roll(two, 64, 1))
        numer = jnp.where(left, pltpu.roll(one, 64, 1), two)
        wide = numer / totals
        wide_ref[i] = wide
        inv_ref[i] = 1.0 / totals
        ctx_ref[i] = wide.astype(BF16)


def backward_kernel(info, q_ref, kv_ref, cg_ref, wide_ref, inv_ref, dq_ref, dkv_ref, qp, gp, kt, dot_ref, dq_acc, dkv_acc):
    e0, e1, total, core = info[0], info[1], info[2], info[3]
    left_q = lax.broadcasted_iota(jnp.int32, (512, 128), 1) < 64

    def prepare(kb, carry):
        kt[kb] = kv_ref[kb].astype(F32).T[0:64].astype(BF16)
        dkv_acc[kb] = jnp.zeros((256, 128), F32)
        return carry

    lax.fori_loop(0, NB, prepare, 0)
    for i in range(GROUP):
        qb = info[4 + i]
        both = q_ref[i].astype(F32)
        qp[0:512] = jnp.where(left_q, both, 0.0).astype(BF16)
        qp[512:1024] = jnp.where(left_q, pltpu.roll(both, 64, 1), 0.0).astype(BF16)
        grad = cg_ref[i].astype(F32)
        inv = inv_ref[i]
        scaled = grad * inv
        gp[0:512] = jnp.where(left_q, 0.0, pltpu.roll(scaled, 64, 1)).astype(BF16)
        gp[512:1024] = jnp.where(left_q, 0.0, scaled).astype(BF16)
        terms = (scaled * wide_ref[i]).T
        dot_ref[:, 0:512] = jnp.sum(terms[0:64], axis=0, keepdims=True)
        dot_ref[:, 512:1024] = jnp.sum(terms[64:128], axis=0, keepdims=True)
        dq_acc[...] = jnp.zeros_like(dq_acc)

        def body(kb, masked):
            keys = kv_ref[kb]
            scores = lax.dot_general(keys, qp[...], NT, preferred_element_type=F32)
            expo = jnp.exp(scores)
            if masked:
                low, high = limits(query_positions((1, 1024), 1, qb), e0, e1, total)
                kpos = key_positions((256, 1), 0, kb, core)
                expo = jnp.where((kpos >= low) & (kpos < high), expo, 0.0)
            prob = lax.dot_general(keys, gp[...], NT, preferred_element_type=F32)
            score_grad = (expo * (prob - dot_ref[...])).astype(BF16)
            dkv_acc[kb] += jnp.dot(score_grad, qp[...], preferred_element_type=F32) + jnp.dot(
                expo.astype(BF16), gp[...], preferred_element_type=F32
            )
            dq_acc[...] += jnp.dot(kt[kb], score_grad, preferred_element_type=F32)

        over_keys(info, i, body)
        flat = jnp.concatenate([dq_acc[:, 0:512], dq_acc[:, 512:1024]], axis=0)
        dq_ref[i] = (flat.T * SCALE).astype(BF16)

    def finish(kb, carry):
        dkv_ref[kb] = dkv_acc[kb].astype(BF16)
        return carry

    lax.fori_loop(0, NB, finish, 0)


VM = pl.BlockSpec(memory_space=pltpu.VMEM)
SM = pl.BlockSpec(memory_space=pltpu.SMEM)
BIG = pltpu.CompilerParams(vmem_limit_bytes=56 * 1024 * 1024)


def cost(flops, size, exps):
    return pl.CostEstimate(flops=flops, bytes_accessed=size, transcendentals=exps)


def attend(info, q, kv):
    return pl.pallas_call(
        forward_kernel,
        out_shape=jax.ShapeDtypeStruct((GROUP, 2, 512, 128), F32),
        in_specs=[SM, VM, VM],
        out_specs=VM,
        scratch_shapes=[
            pltpu.VMEM((1024, 128), BF16),
            pltpu.VMEM((NB, 256, 128), BF16),
            pltpu.VMEM((1024, 128), F32),
        ],
        compiler_params=BIG,
        cost_estimate=cost(18_000_000_000, 6_000_000, 18_000_000),
    )(info, q, kv)


def combine(a, b):
    return pl.pallas_call(
        combine_kernel,
        out_shape=(
            jax.ShapeDtypeStruct((GROUP, 512, 128), BF16),
            jax.ShapeDtypeStruct((GROUP, 512, 128), F32),
            jax.ShapeDtypeStruct((GROUP, 512, 128), F32),
        ),
        in_specs=[VM, VM],
        out_specs=(VM, VM, VM),
        compiler_params=BIG,
    )(a, b)


def attend_back(info, q, kv, cg, wide, inv):
    return pl.pallas_call(
        backward_kernel,
        out_shape=(
            jax.ShapeDtypeStruct((GROUP, 512, 128), BF16),
            jax.ShapeDtypeStruct((NB, 256, 128), BF16),
        ),
        in_specs=[SM] + [VM] * 5,
        out_specs=(VM, VM),
        scratch_shapes=[
            pltpu.VMEM((1024, 128), BF16),
            pltpu.VMEM((1024, 128), BF16),
            pltpu.VMEM((NB, 64, 256), BF16),
            pltpu.VMEM((1, 1024), F32),
            pltpu.VMEM((64, 1024), F32),
            pltpu.VMEM((NB, 256, 128), F32),
        ],
        compiler_params=BIG,
        cost_estimate=cost(45_000_000_000, 8_000_000, 18_000_000),
    )(info, q, kv, cg, wide, inv)


def rms_scale(values, gain_row):
    return (
        values * lax.rsqrt(jnp.mean(values * values, axis=-1, keepdims=True) + EPSILON) * gain_row
    )


def rotary(values, inside):
    half = values.shape[-1] // 2
    frequency = jnp.power(ROPE_BASE, -2.0 * jnp.arange(half, dtype=F32) / values.shape[-1])
    angles = inside.astype(F32)[:, None] * frequency[None, :]
    cosine, sine = jnp.cos(angles)[:, None, :], jnp.sin(angles)[:, None, :]
    first, second = values[..., :half], values[..., half:]
    return jnp.concatenate(
        [first * cosine - second * sine, second * cosine + first * sine], axis=-1
    )


def head_prep(raw_heads, gain_row, inside):
    return rotary(rms_scale(raw_heads, gain_row), inside)


def from_head(value, bit):
    return lax.ppermute(value, "head", [(i, i ^ bit) for i in range(4)])


def body(
    layer_input,
    attn_gain,
    w_query,
    key_weight,
    value_weight,
    w_output,
    query_gain,
    key_gain,
    ffn_gain,
    router,
    w_gate,
    w_up,
    w_down,
    routes,
    doc_lengths,
    cotangent,
):
    b, xl, c, y, m = place()
    tokens, width = layer_input.shape
    total = tokens * 4 * NB
    experts = NB
    capacity = min(tokens, 5 * tokens * TOPK // (4 * experts))
    ends = jnp.cumsum(doc_lengths)
    info = jnp.stack(
        [ends[0], ends[1], jnp.int32(total), c] + [member(m, jnp.int32(j)) for j in range(GROUP)]
    ).astype(jnp.int32)

    chosen = jnp.any(routes[:, :, None] == jnp.arange(experts, dtype=jnp.int32), axis=1)
    before = jnp.tril(jnp.ones((tokens, tokens), BF16), -1)
    rank = jnp.dot(before, chosen.astype(BF16), preferred_element_type=F32).astype(jnp.int32)
    slot = jnp.arange(capacity, dtype=jnp.int32)
    at_slot = chosen.T[:, None, :] & (rank.T[:, None, :] == slot[None, :, None])
    pick = at_slot.astype(BF16).reshape(experts * capacity, tokens)

    def to_experts(value):
        return lax.all_to_all(value, "blk", split_axis=0, concat_axis=0, tiled=True)

    def dispatch(value):
        picked = jnp.dot(pick, value, preferred_element_type=F32).astype(BF16)
        return to_experts(picked.reshape(experts, capacity, width))

    shard = jnp.concatenate(
        [
            w_query,
            key_weight[:, :64],
            value_weight[:, :64],
            key_weight[:, 64:],
            value_weight[:, 64:],
        ],
        axis=1,
    )
    w_full, out_full, both_inputs = exchange(
        weights_kernel,
        0,
        [
            jax.ShapeDtypeStruct((2, width, 512), BF16),
            jax.ShapeDtypeStruct((4, width, width // 4), BF16),
            jax.ShapeDtypeStruct((2, tokens, width), BF16),
        ],
        [(NB,)] * 4 + [(2 * NB,)] * 4 + [(), (), (3,)],
        shard,
        w_output,
        layer_input,
    )
    source2 = both_inputs.reshape(2 * tokens, width).astype(F32)
    normed_wide, attn_pull = jax.vjp(rms_scale, source2, attn_gain)
    normed = normed_wide.astype(BF16)
    raw = [jnp.dot(normed, w_full[i], preferred_element_type=F32) for i in range(2)]
    query_raw = jnp.concatenate([raw[0][:, :256], raw[1][:, :256]], axis=1).reshape(-1, 8, 64)
    kv_raw = jnp.concatenate([raw[0][:, 256:], raw[1][:, 256:]], axis=1).reshape(-1, 4, 2, 64)
    t = jnp.arange(2 * tokens, dtype=jnp.int32)
    pos = 512 * b + 256 * (t // 128) + 128 * c + t % 128
    opening = jnp.where(pos < ends[0], 0, jnp.where(pos < ends[1], ends[0], ends[1]))
    inside = pos - opening
    prep = functools.partial(head_prep, inside=inside)
    query_prep, query_pull = jax.vjp(prep, query_raw, query_gain)
    key_prep, key_pull = jax.vjp(prep, kv_raw[:, :, 0], key_gain)
    query = (query_prep.astype(BF16) * SCALE).astype(BF16).reshape(2 * tokens, 512)
    keyval = (
        jnp.stack([key_prep, kv_raw[:, :, 1]], axis=2).astype(BF16).reshape(2 * tokens, 512)
    )
    q_group, kv_all = exchange(
        qkv_kernel,
        1,
        [
            jax.ShapeDtypeStruct((GROUP, 512, 128), BF16),
            jax.ShapeDtypeStruct((NB, 256, 128), BF16),
        ],
        [(NB,), (NB,), (8,), (8,), (2,)],
        query,
        keyval,
    )
    late_cotangent, _ = lax.optimization_barrier((cotangent, q_group))
    up_rows = dispatch(late_cotangent).reshape(experts * capacity, width)
    partial = attend(info, q_group, kv_all)
    ctx, ctx_wide, ctx_inv = combine(partial, from_head(partial, 1))
    (context,) = exchange(
        context_kernel,
        2,
        [jax.ShapeDtypeStruct((tokens, width), BF16)],
        [(8,), (8,), ()],
        ctx,
    )

    source = layer_input.astype(F32)
    projected = [jnp.dot(context, out_full[i], preferred_element_type=F32) for i in range(4)]
    middle = source + jnp.concatenate(projected, axis=1)
    mixed_wide, ffn_pull = jax.vjp(rms_scale, middle, ffn_gain)
    mixed_in = mixed_wide.astype(BF16)
    expert_in = dispatch(mixed_in).reshape(experts * capacity, width)
    logits = jnp.dot(mixed_in.astype(F32), router, precision=PRECISE)
    top = jnp.max(jnp.where(chosen, logits, -jnp.inf), axis=1, keepdims=True)
    weight = jnp.where(chosen, jnp.exp(logits - top), 0.0)
    gates = weight / jnp.sum(weight, axis=1, keepdims=True)
    slot_gates = jnp.where(at_slot, gates.T[:, None, :], 0.0)
    sent_gates = jnp.sum(slot_gates, axis=2)
    gate_rows = to_experts(sent_gates[:, None, :]).reshape(experts * capacity, 1)

    gate_w, up_w, down_w = w_gate[0], w_up[0], w_down[0]
    gate_pre = jnp.dot(expert_in, gate_w, preferred_element_type=F32)
    up_pre = jnp.dot(expert_in, up_w, preferred_element_type=F32)
    sig = jax.nn.sigmoid(gate_pre)
    activated = gate_pre * sig
    hidden = (activated * up_pre).astype(BF16)
    expert_out = jnp.dot(hidden, down_w, preferred_element_type=F32).astype(BF16)
    upstream_rows = up_rows.astype(F32)
    gate_back_rows = jnp.sum(upstream_rows * expert_out.astype(F32), axis=1)
    gate_grad_slots = to_experts(gate_back_rows.reshape(experts, 1, capacity))[:, 0]
    out_grad = (gate_rows * upstream_rows).astype(BF16)
    hidden_grad = lax.dot_general(out_grad, down_w, NT, preferred_element_type=F32)
    gate_back = (hidden_grad * up_pre * sig * (1.0 + gate_pre * (1.0 - sig))).astype(BF16)
    up_back = (hidden_grad * activated).astype(BF16)
    rows_grad = lax.dot_general(
        gate_back, gate_w, NT, preferred_element_type=F32
    ) + lax.dot_general(up_back, up_w, NT, preferred_element_type=F32)
    grads_home = to_experts(rows_grad.astype(BF16).reshape(experts, capacity, width))
    down_w_grad = lax.dot_general(hidden, out_grad, TN, preferred_element_type=F32)
    gate_w_grad = lax.dot_general(expert_in, gate_back, TN, preferred_element_type=F32)
    up_w_grad = lax.dot_general(expert_in, up_back, TN, preferred_element_type=F32)

    gate_grad = jnp.sum(
        jnp.where(at_slot, gate_grad_slots[:, :, None], 0.0), axis=1
    ).T
    logit_grad = gates * (gate_grad - jnp.sum(gates * gate_grad, axis=1, keepdims=True))
    router_grad = jnp.dot(mixed_in.astype(F32).T, logit_grad, precision=PRECISE)
    mixed_grad = lax.dot_general(
        pick, grads_home.reshape(experts * capacity, width), TN, preferred_element_type=F32
    ) + jnp.dot(logit_grad, router.T, precision=PRECISE)
    middle_norm_grad, ffn_gain_grad = ffn_pull(mixed_grad)
    upstream = cotangent.astype(F32)
    middle_grad = upstream + middle_norm_grad
    attn_grad = middle_grad.astype(BF16)
    context_grad = sum(
        lax.dot_general(
            attn_grad[:, 256 * i : 256 * i + 256], out_full[i], NT, preferred_element_type=F32
        )
        for i in range(4)
    ).astype(BF16)
    (cg_group,) = exchange(
        context_grad_kernel,
        3,
        [jax.ShapeDtypeStruct((GROUP, 512, 128), BF16)],
        [(16,), (16,), ()],
        context_grad,
    )
    late, _ = lax.optimization_barrier(
        ((expert_out, gate_w_grad, up_w_grad, down_w_grad), cg_group)
    )
    rows_home = to_experts(late[0].reshape(experts, capacity, width))
    slot_gates = slot_gates.reshape(experts * capacity, tokens)
    gates_high = slot_gates.astype(BF16)
    gates_low = (slot_gates - gates_high.astype(F32)).astype(BF16)
    rows_home = rows_home.reshape(experts * capacity, width)
    mixture = lax.dot_general(
        gates_high, rows_home, TN, preferred_element_type=F32
    ) + lax.dot_general(gates_low, rows_home, TN, preferred_element_type=F32)
    layer_output = (middle + mixture).astype(BF16)
    def shared_sum(grad):
        low = grad.astype(BF16).reshape(2, grad.shape[0] // 2, grad.shape[1])
        mine = jnp.where(c == 0, low[0], low[1])
        other = jnp.where(c == 0, low[1], low[0])
        chip = (mine.astype(F32) + from_head(other, 1).astype(F32)).astype(BF16)
        both = (chip.astype(F32) + from_head(chip, 2).astype(F32)).astype(BF16)
        back = from_head(both, 1)
        return jnp.where(
            c == 0, jnp.concatenate([both, back]), jnp.concatenate([back, both])
        ).astype(F32)

    expert_sums = [shared_sum(g) for g in late[1:]]

    out_w_parts = jnp.stack(
        [
            lax.dot_general(
                context, attn_grad[:, 256 * i : 256 * i + 256], TN, preferred_element_type=F32
            )
            for i in range(4)
        ]
    ).astype(BF16)
    out_w_parts = lax.all_to_all(
        out_w_parts.reshape(4 * NB, width // NB, width // 4),
        ("head", "blk"),
        split_axis=0,
        concat_axis=0,
        tiled=True,
    )
    w_output_grad = jnp.sum(out_w_parts.astype(F32), axis=0)
    router_grad = lax.psum(router_grad, ("blk", "head"))

    dq, dkv = attend_back(info, q_group, kv_all, cg_group, ctx_wide, ctx_inv)
    dq_parts, dkv_parts = exchange(
        qkv_grad_kernel,
        4,
        [
            jax.ShapeDtypeStruct((2, 2 * tokens, 512), BF16),
            jax.ShapeDtypeStruct((NB, 256, 128), BF16),
        ],
        [(NB,), (NB,), (8,), (8,), (2,)],
        dq,
        dkv,
    )
    query_grad = (dq_parts[0].astype(F32) + dq_parts[1].astype(F32)).astype(BF16)
    dkv_sum = jnp.sum(dkv_parts.reshape(GROUP, 8, 256, 128).astype(F32), axis=1).astype(BF16)
    dkv_sum = dkv_sum.transpose(1, 0, 2).reshape(2 * tokens, 4, 2, 64)
    query_raw_grad, query_gain_grad = query_pull(query_grad.astype(F32).reshape(-1, 8, 64))
    key_raw_grad, key_gain_grad = key_pull(dkv_sum[:, :, 0].astype(F32))
    query_low = query_raw_grad.astype(BF16).reshape(2 * tokens, 512)
    kv_low = jnp.stack([key_raw_grad.astype(BF16), dkv_sum[:, :, 1]], axis=2).reshape(
        2 * tokens, 512
    )
    lows = [
        jnp.concatenate(
            [query_low[:, 256 * i : 256 * i + 256], kv_low[:, 256 * i : 256 * i + 256]], axis=1
        )
        for i in range(2)
    ]
    w_parts = [
        lax.dot_general(normed, lows[i], TN, preferred_element_type=F32).astype(BF16)
        for i in range(2)
    ]
    mine = jnp.where(c == 0, w_parts[0], w_parts[1])
    other = jnp.where(c == 0, w_parts[1], w_parts[0])
    chip_w = (mine.astype(F32) + from_head(other, 1).astype(F32)).astype(BF16)
    normed_grad = sum(
        lax.dot_general(lows[i], w_full[i], NT, preferred_element_type=F32) for i in range(2)
    )
    norm_back, attn_gain_grad = attn_pull(normed_grad)
    halves = norm_back.reshape(2, tokens, width)
    mine = jnp.where(xl == 0, halves[0], halves[1])
    other = jnp.where(xl == 0, halves[1], halves[0])
    input_grad = (middle_grad + mine + from_head(other, 2)).astype(BF16)
    (w_shards,) = exchange(
        scatter_kernel,
        5,
        [jax.ShapeDtypeStruct((NB, width // NB, 512), BF16)],
        [(NB,), (NB,), ()],
        chip_w.reshape(NB, width // NB, 512),
    )
    w_shard = jnp.sum(w_shards.astype(F32), axis=0)
    smalls = jnp.concatenate(
        [attn_gain_grad, ffn_gain_grad, query_gain_grad, key_gain_grad, jnp.zeros((896,), F32)]
    ).reshape(24, 128)
    smalls = small_sum(smalls).reshape(-1)
    return (
        layer_output,
        input_grad,
        smalls[:1024],
        w_shard[:, :256],
        jnp.concatenate([w_shard[:, 256:320], w_shard[:, 384:448]], axis=1),
        jnp.concatenate([w_shard[:, 320:384], w_shard[:, 448:512]], axis=1),
        w_output_grad,
        smalls[2048:2112],
        smalls[2112:2176],
        smalls[1024:2048],
        router_grad,
        expert_sums[0][None],
        expert_sums[1][None],
        expert_sums[2][None],
    )


def solution(mesh):
    everyone = P(("blk", "head"), None)
    both = P("blk", "head")
    expert = P("blk", None, None)
    return jax.shard_map(
        body,
        mesh=mesh,
        in_specs=(everyone, P(), both, both, both, both, P(), P(), P(), P())
        + (expert, expert, expert, everyone, P(), everyone),
        out_specs=(everyone, everyone, P(), both, both, both, both, P(), P(), P(), P())
        + (expert, expert, expert),
        check_vma=False,
    )
```

time: 2170 us -> 700 us (0.32)
  waiting for transfers between devices: 972 us -> 39.3 us
  Pallas kernels: 0 us -> 390 us
  matrix products: 450 us -> 70.8 us
  starting transfers between devices: 289 us -> 82.4 us
  local copies, waits for them, and re-layouts: 156 us -> 28.4 us
  blocking collectives: 132 us -> 13.1 us
  other arithmetic: 121 us -> 47.8 us
  loops' own time: 26 us -> 0 us
    all_gather x5 -> x0, waiting for transfers between devices: 656 us -> none  [the longest x1 191 us: body(): lax.all_gather(key_weight.reshape(1, -1), ('blk', 'head'), axis=0, tiled=...]
    pallas_call x0 -> x10, Pallas kernels: none -> 390 us  [the longest x6 253 us: exchange(): pl.pallas_call(kernel, out_shape=out_shapes, in_specs=[anyspec] * len(ope...]
    dot_general x247 -> x35, matrix products: 449 us -> 69.5 us  [the longest x4 7.05 us: body(): lax.dot_general(attn_grad[:, 256 * i:256 * i + 256], out_full[i], NT, pre...]
    ppermute x128 -> x12, starting transfers between devices: 251 us -> 6.54 us  [from_head(): return lax.ppermute(value, 'head', [(i, i ^ bit) for i in range(4)])]
    ppermute x128 -> x12, waiting for transfers between devices: 154 us -> 0.03 us  [from_head(): return lax.ppermute(value, 'head', [(i, i ^ bit) for i in range(4)])]
    unnamed x8 -> x1, waiting for transfers between devices: 97.2 us -> 0.02 us
    psum x1 -> x0, blocking collectives: 77.3 us -> none  [body(): lax.psum((attn_gain_grad, query_gain_grad, key_gain_grad, ffn_gain_grad,...]
    dynamic_slice x64 -> x0, local copies, waits for them, and re-layouts: 50.6 us -> none  [in_steps(): lax.scan(advance, carried, (jnp.arange(step_count, dtype=jnp.int32), stac...]
  transfers between devices with their start and end apart: 141 -> 19, of which waited for: 71 -> 3; matrix products, arithmetic and copies ran while one was open for 30% -> 15% of each run, Pallas kernels for 0% -> 37%
where the time goes in v1:
time: 700 us; the launch traced here: 687 us
  Pallas kernels  390 us (56%)
  starting transfers between devices  82.4 us (12%)
  matrix products  70.8 us (10%)
  other arithmetic  47.8 us (7%)
  waiting for transfers between devices  39.3 us (6%)
  local copies, waits for them, and re-layouts  28.4 us (4%)
  between operations  16 us (2%)
  blocking collectives  13.1 us (2%)
    pallas_call x6, Pallas kernels, exchange(): pl.pallas_call(kernel, out_shape=out_shapes, in_specs=[anyspec] * len(ope...  253 us
    pallas_call x1, Pallas kernels, attend_back(): pl.pallas_call(backward_kernel, out_shape=(jax.ShapeDtypeStruct((GROUP, 5...  65.5 us
    all_to_all x5, starting transfers between devices, to_experts(): return lax.all_to_all(value, 'blk', split_axis=0, concat_axis=0, tiled=True)  58.7 us
    pallas_call x1, Pallas kernels, attend(): pl.pallas_call(forward_kernel, out_shape=jax.ShapeDtypeStruct((GROUP, 2,...  49.3 us
    all_to_all x5, waiting for transfers between devices, to_experts(): return lax.all_to_all(value, 'blk', split_axis=0, concat_axis=0, tiled=True)  39.2 us
    pallas_call x1, Pallas kernels, small_sum(): pl.pallas_call(small_sum_kernel, out_shape=jax.ShapeDtypeStruct(x.shape,...  17.7 us
  transfers between devices with their start and end apart: 19, of which 3 were waited for; matrix products, arithmetic and copies ran while one was open for 15% of the time, Pallas kernels for 37%

profile of v1, /device:TPU:4, one launch (start us, length us, event | category | flops | bytes accessed | tf_op | source)
XLA Modules:
  0.0 687.3 jit_solution(14894295290499214457)
XLA Ops:
  8.1 1.4 concatenate.107.ws
  9.6 43.3 %shard_map.263 = (bf16[2,1024,512]{2,1,0:T(8,128)(2,1)}, bf16[4,1024,256]{2,1,0:T(8,128)(2,1)}, bf16[2,128,1024]{2,1,0:T(8,128)(2,1)}) custom-call(bf16[32,512]{1,0:T(8,128)(2,1)} %concatenate.107.ws, bf16[32,256]{1,0:T(8,128)(2,1)} %wo.1, bf16[128,1024]{1,0:T(8,128)(2,1)} %li.1), custom_call_target="tpu_custom_call" | custom-call | tf_op jit(solution)/shard_map/pallas_call | solution.py:59
  55.5 1.7 fusion.33
  63.2 43.8 %shard_map.264 = (bf16[4,512,128]{2,1,0:T(8,128)(2,1)}, bf16[32,256,128]{2,1,0:T(8,128)(2,1)}) custom-call(bf16[256,512]{1,0:T(8,128)(2,1)} %copy.62.q, bf16[256,512]{1,0:T(8,128)(2,1)} %copy.63.kv), custom_call_target="tpu_custom_call" | custom-call | tf_op jit(solution)/shard_map/pallas_call | solution.py:59
  107.0 1.9 stack.57.info
  108.9 49.3 %shard_map.265.a_ref = f32[4,2,512,128]{3,2,1,0:T(8,128)} custom-call(s32[8]{0:T(128)} %stack.57.info, bf16[4,512,128]{2,1,0:T(8,128)(2,1)} %get-tuple-element.33.q_ref, bf16[32,256,128]{2,1,0:T(8,128)(2,1)} %get-tuple-element.34.kv_ref), custom_call_target="tpu_custom_call" | custom-call | flops 17999998976 | bytes 6000000 | tf_op jit(solution)/shard_map/pallas_call | solution.py:487
  159.1 2.3 convolution_convert_fusion
  161.4 24.6 %all-to-all-start.2 = ((bf16[32,40,1024]{2,1,0:T(8,128)(2,1)}), bf16[32,40,1024]{2,1,0:T(8,128)(2,1)}, u32[]{:S(2)}, u32[]{:S(2)}) async-start(bf16[32,40,1024]{2,1,0:T(8,128)(2,1)} %bitcast.239), calls=%async_computation.2 | async-start | bytes 5242880 | tf_op jit(solution)/shard_map/all_to_all | solution.py:599
  186.1 4.3 shard_map.266
  190.4 33.1 %shard_map.267 = bf16[128,1024]{1,0:T(8,128)(2,1)} custom-call(bf16[4,512,128]{2,1,0:T(8,128)(2,1)} %get-tuple-element.35.ctx), custom_call_target="tpu_custom_call" | custom-call | tf_op jit(solution)/shard_map/pallas_call | solution.py:59
  223.5 1.4 fusion.50
  229.2 2.4 convolution_convert_fusion.2
  231.7 8.7 %all-to-all-start = ((bf16[32,40,1024]{2,1,0:T(8,128)(2,1)}), bf16[32,40,1024]{2,1,0:T(8,128)(2,1)}, u32[]{:S(2)}, u32[]{:S(2)}) async-start(bf16[32,40,1024]{2,1,0:T(8,128)(2,1)} %bitcast.240), calls=%async_computation | async-start | bytes 5242880 | tf_op jit(solution)/shard_map/all_to_all | solution.py:599
  240.8 4.9 copy.64
  245.7 26.8 %all-to-all-done = bf16[32,40,1024]{2,1,0:T(8,128)(2,1)} async-done(((bf16[32,40,1024]{2,1,0:T(8,128)(2,1)}), bf16[32,40,1024]{2,1,0:T(8,128)(2,1)}, u32[]{:S(2)}, u32[]{:S(2)}) %all-to-all-start) | async-done | bytes 2621472 | tf_op jit(solution)/shard_map/all_to_all | solution.py:599
  272.6 3.7 fusion.30
  276.3 6.2 multiply_convert_fusion.5
  282.5 3.3 multiply_reduce_fusion
  286.5 8.9 %all-to-all-start.4 = ((f32[32,1,40]{2,1,0:T(1,128)}), f32[32,1,40]{2,1,0:T(1,128)S(1)}, u32[]{:S(2)}, u32[]{:S(2)}) async-start(f32[32,1,40]{2,1,0:T(1,128)} %reshape.542), calls=%async_computation.4 | async-start | bytes 32768 | tf_op jit(solution)/shard_map/all_to_all | solution.py:599
  295.4 7.0 %all-to-all-done.4 = f32[32,1,40]{2,1,0:T(1,128)S(1)} async-done(((f32[32,1,40]{2,1,0:T(1,128)}), f32[32,1,40]{2,1,0:T(1,128)S(1)}, u32[]{:S(2)}, u32[]{:S(2)}) %all-to-all-start.4) | async-done | bytes 5152 | tf_op jit(solution)/shard_map/all_to_all | solution.py:599
  302.9 13.1 %all_to_all.35 = f32[32,1,40]{2,1,0:T(1,128)S(1)} all-to-all(f32[32,1,40]{2,1,0:T(1,128)S(1)} %bitcast.271), channel_id=1, replica_groups=mesh['blk'=32,'head'=4] {'blk'}, dimensions={0} | all-to-all | bytes 10240 | tf_op jit(solution)/shard_map/all_to_all | solution.py:599
  316.0 2.4 multiply_convert_fusion.1
  319.3 2.4 multiply_convert_fusion.3
  321.8 1.6 fusion.28
  323.8 3.2 add_convert_fusion
  327.0 7.4 %all-to-all-start.3 = ((bf16[32,40,1024]{2,1,0:T(8,128)(2,1)}), bf16[32,40,1024]{2,1,0:T(8,128)(2,1)}, u32[]{:S(2)}, u32[]{:S(2)}) async-start(bf16[32,40,1024]{2,1,0:T(8,128)(2,1)} %bitcast.237), calls=%async_computation.3 | async-start | bytes 5242880 | tf_op jit(solution)/shard_map/all_to_all | solution.py:599
  334.3 8.7 %all-reduce.6.cloned.1.call-start = ((), (), s32[]{:S(2)}) async-start(), calls=%async_computation.7 | async-start | bytes 262144 | tf_op jit(solution)/shard_map/psum | solution.py:770
  345.9 4.7 fusion.142
  350.7 3.4 fusion.141
  354.1 4.8 fusion
  358.9 5.4 all-to-all-done.3
  364.3 2.4 convolution_bitcast_fusion
  369.7 2.1 fusion.58
  371.8 1.6 pad_maximum_fusion
  373.4 8.4 %all-to-all-start.6 = ((bf16[128,32,256]{2,1,0:T(8,128)(2,1)}), bf16[128,32,256]{2,1,0:T(8,128)(2,1)}, u32[]{:S(2)}, u32[]{:S(2)}) async-start(bf16[128,32,256]{2,1,0:T(8,128)(2,1)} %bitcast.241), calls=%async_computation.6 | async-start | bytes 4194304 | tf_op jit(solution)/shard_map/all_to_all | solution.py:762
  381.8 1.5 convolution_add_fusion.4
  384.7 2.1 fusion.10.cg
  386.8 29.2 %shard_map.268.cg_ref = bf16[4,512,128]{2,1,0:T(8,128)(2,1)} custom-call(bf16[128,1024]{1,0:T(8,128)(2,1)} %fusion.10.cg), custom_call_target="tpu_custom_call" | custom-call | tf_op jit(solution)/shard_map/pallas_call | solution.py:59
  415.9 65.5 %shard_map.269 = (bf16[4,512,128]{2,1,0:T(8,128)(2,1)}, bf16[32,256,128]{2,1,0:T(8,128)(2,1)}) custom-call(s32[8]{0:T(128)} %stack.57.info, bf16[4,512,128]{2,1,0:T(8,128)(2,1)} %get-tuple-element.33.q_ref, bf16[32,256,128]{2,1,0:T(8,128)(2,1)} %get-tuple-element.34.kv_ref, bf16[4,512,128]{2,1,0:T(8,128)(2,1)} %shard_map.268.cg_ref, ...), custom_call_target="tpu_custom_call" | custom-call | flops 44999999488 | bytes 8000000 | tf_op jit(solution)/shard_map/pallas_call | solution.py:517
  481.5 43.6 %shard_map.270 = (bf16[2,256,512]{2,1,0:T(8,128)(2,1)}, bf16[32,256,128]{2,1,0:T(8,128)(2,1)}) custom-call(bf16[4,512,128]{2,1,0:T(8,128)(2,1)} %get-tuple-element.41.dq, bf16[32,256,128]{2,1,0:T(8,128)(2,1)} %get-tuple-element.42.dkv), custom_call_target="tpu_custom_call" | custom-call | tf_op jit(solution)/shard_map/pallas_call | solution.py:59
  525.1 1.9 fusion.82
  527.0 2.0 copy.66
  538.0 1.5 fusion.16
  541.6 4.5 copy.65
  546.8 17.7 %shard_map.271 = f32[24,128]{1,0:T(8,128)} custom-call(f32[24,128]{1,0:T(8,128)} %bitcast.272), custom_call_target="tpu_custom_call" | custom-call | tf_op jit(solution)/shard_map/pallas_call | solution.py:329
  565.4 2.8 collective-permute-start.1
  569.5 1.5 convolution_convert_fusion.4
  571.1 3.0 broadcast_select_fusion
  574.7 2.2 add_convert_fusion.3
  576.9 2.1 add_convert_fusion.5
  579.0 2.0 collective-permute-start.7
  581.1 2.0 add_convert_fusion.7
  583.4 9.1 %all-to-all-start.5 = ((bf16[32,40,1024]{2,1,0:T(8,128)(2,1)}), bf16[32,40,1024]{2,1,0:T(8,128)(2,1)}, u32[]{:S(2)}, u32[]{:S(2)}) async-start(bf16[32,40,1024]{2,1,0:T(8,128)(2,1)} %bitcast.238), calls=%async_computation.5 | async-start | bytes 5242880 | tf_op jit(solution)/shard_map/all_to_all | solution.py:599
  592.6 2.1 add_convert_fusion.8
  594.7 2.6 add_convert_fusion.1
  597.3 59.7 %shard_map.272 = bf16[32,32,512]{2,1,0:T(8,128)(2,1)} custom-call(bf16[32,32,512]{2,1,0:T(8,128)(2,1)} %bitcast.247), custom_call_target="tpu_custom_call" | custom-call | tf_op jit(solution)/shard_map/pallas_call | solution.py:59
  662.4 1.4 add_convert_fusion.2
  665.3 1.7 fusion.11
  667.0 1.7 fusion.12
  668.6 1.8 fusion.13
  670.4 2.6 convert_reduce_fusion
  673.0 2.4 convolution_bitcast_fusion.1
  675.4 3.0 fusion.9
  678.4 1.6 copy.78
  (272 shorter events, 46.0 us)
Async XLA Ops:
  7.2 275.3 %copy-start = (bf16[1,512,1024]{2,1,0:T(8,128)(2,1)S(1)}, bf16[1,512,1024]{2,1,0:T(8,128)(2,1)}, u32[]{:S(2)}) copy-start(bf16[1,512,1024]{2,1,0:T(8,128)(2,1)} %param.28) | copy-start | bytes 3145732
  52.9 4.3 copy-start.27
  54.3 288.8 %copy-start.47 = (f32[2,128]{1,0:T(2,128)}, f32[2,128]{1,0:T(2,128)S(1)}, u32[]{:S(2)}) copy-start(f32[2,128]{1,0:T(2,128)S(1)} %fusion.18) | copy-start | bytes 3076
  60.6 468.4 %copy-start.23 = (f32[256,32]{0,1:T(8,128)}, f32[256,32]{0,1:T(8,128)S(1)}, u32[]{:S(2)}) copy-start(f32[256,32]{0,1:T(8,128)S(1)} %get-tuple-element.93) | copy-start | bytes 98308
  60.6 468.4 %copy-start.24 = (f32[256,32]{0,1:T(8,128)}, f32[256,32]{0,1:T(8,128)S(1)}, u32[]{:S(2)}) copy-start(f32[256,32]{0,1:T(8,128)S(1)} %get-tuple-element.94) | copy-start | bytes 98308
  62.1 96.2 %copy-start.35 = (f32[256,8]{0,1:T(8,128)}, f32[256,8]{0,1:T(8,128)S(1)}, u32[]{:S(2)}) copy-start(f32[256,8]{0,1:T(8,128)S(1)} %multiply_reduce_fusion.6) | copy-start | bytes 24580
  108.9 49.7 %copy-start.60 = (s32[128,8]{0,1:T(8,128)S(1)}, s32[128,8]{0,1:T(8,128)}, u32[]{:S(2)}) copy-start(s32[128,8]{0,1:T(8,128)} %param.29) | copy-start | bytes 12292
  108.9 50.2 %copy-start.11 = (bf16[128,1024]{1,0:T(8,128)(2,1)S(1)}, bf16[128,1024]{1,0:T(8,128)(2,1)}, u32[]{:S(2)}) copy-start(bf16[128,1024]{1,0:T(8,128)(2,1)} %param.31) | copy-start | bytes 786436
  158.3 27.8 %collective-permute-start = (f32[4,2,512,128]{3,2,1,0:T(8,128)}, f32[4,2,512,128]{3,2,1,0:T(8,128)}, u32[]{:S(2)}, u32[]{:S(2)}) collective-permute-start(f32[4,2,512,128]{3,2,1,0:T(8,128)} %shard_map.265.a_ref), channel_id=1, source_target_pairs={{0,1},{1,0},{2,3},{3,2},{4,5},{5,4},{6,7},{7,6},{8,9},{9,8},{10,11... | collective-permute-start | bytes 6291464 | tf_op jit(solution)/shard_map/ppermute | solution.py:560
  158.9 205.4 %copy-start.31 = (s32[32,128]{1,0:T(8,128)}, s32[32,128]{1,0:T(8,128)S(1)}, u32[]{:S(2)}) copy-start(s32[32,128]{1,0:T(8,128)S(1)} %convolution_convert_fusion.9) | copy-start | bytes 49156
  161.4 70.2 %all-to-all-start.2 = ((bf16[32,40,1024]{2,1,0:T(8,128)(2,1)}), bf16[32,40,1024]{2,1,0:T(8,128)(2,1)}, u32[]{:S(2)}, u32[]{:S(2)}) async-start(bf16[32,40,1024]{2,1,0:T(8,128)(2,1)} %bitcast.239), calls=%async_computation.2 | async-start | bytes 5242880 | tf_op jit(solution)/shard_map/all_to_all | solution.py:599
  190.4 38.5 %copy-start.22 = (bf16[128,1024]{1,0:T(8,128)(2,1)S(1)}, bf16[128,1024]{1,0:T(8,128)(2,1)}, u32[]{:S(2)}) copy-start(bf16[128,1024]{1,0:T(8,128)(2,1)} %li.1) | copy-start | bytes 786436
  223.5 4.2 copy-start.2
  224.9 4.2 copy-start.37
  231.7 8.7 %copy-start.25 = (f32[1024,32]{0,1:T(8,128)S(1)}, f32[1024,32]{0,1:T(8,128)}, u32[]{:S(2)}) copy-start(f32[1024,32]{0,1:T(8,128)} %param.25) | copy-start | bytes 393220
  231.7 40.9 %all-to-all-start = ((bf16[32,40,1024]{2,1,0:T(8,128)(2,1)}), bf16[32,40,1024]{2,1,0:T(8,128)(2,1)}, u32[]{:S(2)}, u32[]{:S(2)}) async-start(bf16[32,40,1024]{2,1,0:T(8,128)(2,1)} %bitcast.240), calls=%async_computation | async-start | bytes 5242880 | tf_op jit(solution)/shard_map/all_to_all | solution.py:599
  240.7 102.9 %copy-start.43 = (f32[128]{0:T(128)}, f32[128]{0:T(128)S(1)}, u32[]{:S(2)}) copy-start(f32[128]{0:T(128)S(1)} %get-tuple-element.101) | copy-start | bytes 1540
  240.8 102.9 %copy-start.49 = (f32[128]{0:T(128)}, f32[128]{0:T(128)S(1)}, u32[]{:S(2)}) copy-start(f32[128]{0:T(128)S(1)} %fusion.104) | copy-start | bytes 1540
  272.6 3.7 copy-start.20
  272.6 9.9 %slice-start = ((s8[5242880]{0:T(1024)(128)(4,1)}), s8[4194304]{0:T(1024)(128)(4,1)S(1)}, s32[]{:S(2)}) async-start(s8[5242880]{0:T(1024)(128)(4,1)} %bitcast.234), calls=%async_computation.8 | async-start | bytes 8388608
  276.3 6.2 copy-start.70
  276.3 6.2 slice-start.1
  282.5 3.3 copy-start.18
  286.5 15.9 %all-to-all-start.4 = ((f32[32,1,40]{2,1,0:T(1,128)}), f32[32,1,40]{2,1,0:T(1,128)S(1)}, u32[]{:S(2)}, u32[]{:S(2)}) async-start(f32[32,1,40]{2,1,0:T(1,128)} %reshape.542), calls=%async_computation.4 | async-start | bytes 32768 | tf_op jit(solution)/shard_map/all_to_all | solution.py:599
  295.4 23.0 %copy-start.33 = (f32[32,128]{1,0:T(8,128)}, f32[32,128]{1,0:T(8,128)S(1)}, u32[]{:S(2)}) copy-start(f32[32,128]{1,0:T(8,128)S(1)} %fusion.99) | copy-start | bytes 49156
  316.0 3.3 copy-start.72
  327.0 37.3 %all-to-all-start.3 = ((bf16[32,40,1024]{2,1,0:T(8,128)(2,1)}), bf16[32,40,1024]{2,1,0:T(8,128)(2,1)}, u32[]{:S(2)}, u32[]{:S(2)}) async-start(bf16[32,40,1024]{2,1,0:T(8,128)(2,1)} %bitcast.237), calls=%async_computation.3 | async-start | bytes 5242880 | tf_op jit(solution)/shard_map/all_to_all | solution.py:599
  334.3 344.1 %all-reduce.6.cloned.1.call-start = ((), (), s32[]{:S(2)}) async-start(), calls=%async_computation.7 | async-start | bytes 262144 | tf_op jit(solution)/shard_map/psum | solution.py:770
  345.9 4.7 copy-start.69
  350.7 3.4 copy-start.19
  354.1 181.0 %copy-start.4 = (bf16[1024,512]{1,0:T(8,128)(2,1)}, bf16[1024,512]{1,0:T(8,128)(2,1)S(1)}, u32[]{:S(2)}) copy-start(bf16[1024,512]{1,0:T(8,128)(2,1)S(1)} %fusion.141) | copy-start | bytes 3145732
  358.9 7.8 %copy-start.44 = (f32[128]{0:T(128)S(1)}, f32[128]{0:T(128)}, u32[]{:S(2)}) copy-start(f32[128]{0:T(128)} %copy-done.43) | copy-start | bytes 1540
  358.9 7.8 %copy-start.50 = (f32[128]{0:T(128)S(1)}, f32[128]{0:T(128)}, u32[]{:S(2)}) copy-start(f32[128]{0:T(128)} %copy-done.49) | copy-start | bytes 1540
  358.9 7.9 %copy-start.52 = (f32[128]{0:T(128)S(1)}, f32[128]{0:T(128)}, u32[]{:S(2)}) copy-start(f32[128]{0:T(128)} %copy-done.51) | copy-start | bytes 1540
  358.9 7.9 %copy-start.57 = (f32[128]{0:T(128)S(1)}, f32[128]{0:T(128)}, u32[]{:S(2)}) copy-start(f32[128]{0:T(128)} %copy-done.56) | copy-start | bytes 1540
  364.3 3.8 copy-start.65
  364.3 3.8 copy-start.12
  373.4 8.5 %copy-start.15 = (bf16[128,1024]{1,0:T(8,128)(2,1)S(1)}, bf16[128,1024]{1,0:T(8,128)(2,1)}, u32[]{:S(2)}) copy-start(bf16[128,1024]{1,0:T(8,128)(2,1)} %copy-done.14) | copy-start | bytes 786436
  373.4 210.0 %all-to-all-start.6 = ((bf16[128,32,256]{2,1,0:T(8,128)(2,1)}), bf16[128,32,256]{2,1,0:T(8,128)(2,1)}, u32[]{:S(2)}, u32[]{:S(2)}) async-start(bf16[128,32,256]{2,1,0:T(8,128)(2,1)} %bitcast.241), calls=%async_computation.6 | async-start | bytes 4194304 | tf_op jit(solution)/shard_map/all_to_all | solution.py:762
  525.1 5.2 copy-start.55
  527.0 4.0 copy-start.36
  536.9 40.0 %collective-permute-start.6 = (bf16[512,512]{1,0:T(8,128)(2,1)}, bf16[512,512]{1,0:T(8,128)(2,1)}, u32[]{:S(2)}, u32[]{:S(2)}) collective-permute-start(bf16[512,512]{1,0:T(8,128)(2,1)} %broadcast_select_fusion.2), channel_id=1, source_target_pairs={{0,1},{1,0},{2,3},{3,2},{4,5},{5,4},{6,7},{7,6},{8,9},{9,8},{10,11... | collective-permute-start | bytes 1572872 | tf_op jit(solution)/shard_map/ppermute | solution.py:560
  536.9 44.2 %collective-permute-start.3 = (bf16[512,512]{1,0:T(8,128)(2,1)}, bf16[512,512]{1,0:T(8,128)(2,1)}, u32[]{:S(2)}, u32[]{:S(2)}) collective-permute-start(bf16[512,512]{1,0:T(8,128)(2,1)} %broadcast_select_fusion.3), channel_id=1, source_target_pairs={{0,1},{1,0},{2,3},{3,2},{4,5},{5,4},{6,7},{7,6},{8,9},{9,8},{10,11... | collective-permute-start | bytes 1572872 | tf_op jit(solution)/shard_map/ppermute | solution.py:560
  541.6 4.5 copy-start.46
  541.6 4.5 copy-start.63
  546.1 28.6 %collective-permute-start.9 = (bf16[256,1024]{1,0:T(8,128)(2,1)}, bf16[256,1024]{1,0:T(8,128)(2,1)}, u32[]{:S(2)}, u32[]{:S(2)}) collective-permute-start(bf16[256,1024]{1,0:T(8,128)(2,1)} %broadcast_select_fusion.1), channel_id=1, source_target_pairs={{0,1},{1,0},{2,3},{3,2},{4,5},{5,4},{6,7},{7,6},{8,9},{9,8},{10,11... | collective-permute-start | bytes 1572872 | tf_op jit(solution)/shard_map/ppermute | solution.py:560
  565.4 27.1 %collective-permute-start.1 = (f32[128,1024]{1,0:T(8,128)}, f32[128,1024]{1,0:T(8,128)}, u32[]{:S(2)}, u32[]{:S(2)}) collective-permute-start(f32[128,1024]{1,0:T(8,128)} %slice_select_fusion), channel_id=1, source_target_pairs={{0,2},{1,3},{2,0},{3,1},{4,6},{5,7},{6,4},{7,5},{8,10},{9,11},{10,... | collective-permute-start | bytes 1572872 | tf_op jit(solution)/shard_map/ppermute | solution.py:560
  571.1 3.7 copy-start.9
  571.1 5.9 copy-start.7
  574.1 20.6 %collective-permute-start.2 = (bf16[1024,512]{1,0:T(8,128)(2,1)}, bf16[1024,512]{1,0:T(8,128)(2,1)}, u32[]{:S(2)}, u32[]{:S(2)}) collective-permute-start(bf16[1024,512]{1,0:T(8,128)(2,1)} %get-tuple-element.105), channel_id=1, source_target_pairs={{0,1},{1,0},{2,3},{3,2},{4,5},{5,4},{6,7},{7,6},{8,9},{9,8},{10,11... | collective-permute-start | bytes 3145736 | tf_op jit(solution)/shard_map/ppermute | solution.py:560
  574.7 6.3 copy-start.5
  576.9 85.5 %collective-permute-start.10 = (bf16[256,1024]{1,0:T(8,128)(2,1)}, bf16[256,1024]{1,0:T(8,128)(2,1)}, u32[]{:S(2)}, u32[]{:S(2)}) collective-permute-start(bf16[256,1024]{1,0:T(8,128)(2,1)} %add_convert_fusion.3), channel_id=1, source_target_pairs={{0,2},{1,3},{2,0},{3,1},{4,6},{5,7},{6,4},{7,5},{8,10},{9,11},{10,... | collective-permute-start | bytes 1572872 | tf_op jit(solution)/shard_map/ppermute | solution.py:560
  579.0 81.5 %collective-permute-start.7 = (bf16[512,512]{1,0:T(8,128)(2,1)}, bf16[512,512]{1,0:T(8,128)(2,1)}, u32[]{:S(2)}, u32[]{:S(2)}) collective-permute-start(bf16[512,512]{1,0:T(8,128)(2,1)} %add_convert_fusion.5), channel_id=1, source_target_pairs={{0,2},{1,3},{2,0},{3,1},{4,6},{5,7},{6,4},{7,5},{8,10},{9,11},{10,... | collective-permute-start | bytes 1572872 | tf_op jit(solution)/shard_map/ppermute | solution.py:560
  583.1 76.0 %collective-permute-start.4 = (bf16[512,512]{1,0:T(8,128)(2,1)}, bf16[512,512]{1,0:T(8,128)(2,1)}, u32[]{:S(2)}, u32[]{:S(2)}) collective-permute-start(bf16[512,512]{1,0:T(8,128)(2,1)} %add_convert_fusion.7), channel_id=1, source_target_pairs={{0,2},{1,3},{2,0},{3,1},{4,6},{5,7},{6,4},{7,5},{8,10},{9,11},{10,... | collective-permute-start | bytes 1572872 | tf_op jit(solution)/shard_map/ppermute | solution.py:560
  583.4 9.2 %copy-start.13 = (bf16[128,1024]{1,0:T(8,128)(2,1)S(1)}, bf16[128,1024]{1,0:T(8,128)(2,1)}, u32[]{:S(2)}) copy-start(bf16[128,1024]{1,0:T(8,128)(2,1)} %param.31) | copy-start | bytes 786436
  583.4 9.2 %copy-start.53 = (f32[128]{0:T(128)S(1)}, f32[128]{0:T(128)}, u32[]{:S(2)}) copy-start(f32[128]{0:T(128)} %copy-done.51) | copy-start | bytes 1540
  583.4 9.2 %copy-start.62 = (f32[128]{0:T(128)S(1)}, f32[128]{0:T(128)}, u32[]{:S(2)}) copy-start(f32[128]{0:T(128)} %copy-done.61) | copy-start | bytes 1540
  583.4 89.6 %all-to-all-start.5 = ((bf16[32,40,1024]{2,1,0:T(8,128)(2,1)}), bf16[32,40,1024]{2,1,0:T(8,128)(2,1)}, u32[]{:S(2)}, u32[]{:S(2)}) async-start(bf16[32,40,1024]{2,1,0:T(8,128)(2,1)} %bitcast.238), calls=%async_computation.5 | async-start | bytes 5242880 | tf_op jit(solution)/shard_map/all_to_all | solution.py:599
  660.4 4.9 collective-permute-start.5
  661.9 5.1 collective-permute-start.8
  663.8 4.8 collective-permute-start.11
  668.6 4.3 copy-start.32
  668.6 4.3 copy-start.34
  673.0 7.0 %copy-start.1 = (bf16[1,512,1024]{2,1,0:T(8,128)(2,1)S(1)}, bf16[1,512,1024]{2,1,0:T(8,128)(2,1)}, u32[]{:S(2)}) copy-start(bf16[1,512,1024]{2,1,0:T(8,128)(2,1)} %param.28) | copy-start | bytes 3145732
  (30 other events, 61.1 us)
Sparse Core Ops, SparseCore 0:
  344.7 177.5 all-reduce.5

commit v2 on v1

v2 whole, which is shorter than its diff:
```python
import functools

import jax
import jax.numpy as jnp
from jax import lax
from jax.experimental import pallas as pl
from jax.experimental.pallas import tpu as pltpu
from jax.sharding import PartitionSpec as P

HEAD_SIZE = 64
TOPK = 8
BLOCK = 256
EPSILON = 1e-06
ROPE_BASE = 10000.0
PRECISE = lax.Precision.HIGHEST
SCALE = HEAD_SIZE ** (-0.5)

NB = 32
SLOTS = 80
GROUP = 4
MESH_ID = pl.DeviceIdType.MESH
F32 = jnp.float32
BF16 = jnp.bfloat16
NT = (((1,), (1,)), ((), ()))
NN = (((1,), (0,)), ((), ()))
TN = (((0,), (0,)), ((), ()))


def place():
    b = lax.axis_index("blk")
    h = lax.axis_index("head")
    y = b // 8
    r = lax.rem(b, 8)
    m = jnp.where(lax.rem(y, 2) == 0, r, 7 - r)
    return b, h // 2, lax.rem(h, 2), y, m


def member(m, j):
    return 8 * j + m + lax.rem(j, 2) * (7 - 2 * m)


def times(start, n, body):
    def step(i, carry):
        body(i)
        return carry

    lax.fori_loop(start, n, step, 0)


def signal(sem, blk, head):
    pl.semaphore_signal(sem, inc=1, device_id=(blk, head), device_id_type=MESH_ID)


def rows(start, size):
    return pl.ds(pl.multiple_of(start, size), size)


def to(src, dst, send, recv, blk, head):
    return pltpu.make_async_remote_copy(
        src, dst, send, recv, device_id=(blk, head), device_id_type=MESH_ID
    )


def weights_kernel(
    ws, li, cot, routes, w_out, li_out, cot_out, routes_out, s1, r1, s2, r2, sx, rx, ls
):
    b, xl, c, _, _ = place()
    h = 2 * xl + c
    sib = 2 * xl + 1 - c
    over = 2 * (1 - xl) + c
    bar = pltpu.get_barrier_semaphore()
    times(1, NB, lambda d: signal(bar, lax.rem(b + d, NB), h))
    signal(bar, b, sib)
    signal(bar, b, over)
    pl.semaphore_wait(bar, NB + 1)

    def first(d):
        return to(ws, w_out.at[c, rows(b * 32, 32)], s1.at[d], r1.at[d], lax.rem(b + d, NB), h)

    def second(d):
        src = lax.rem(b + NB - d, NB)
        part = w_out.at[c, rows(src * 32, 32)]
        return to(part, part, s2.at[d], r2.at[d], b, sib)

    times(1, NB, lambda d: first(d).start())
    extra = [
        to(li, li_out.at[xl], sx.at[0], rx.at[0], b, over),
        to(ws, w_out.at[c, rows(b * 32, 32)], s2.at[0], r2.at[0], b, sib),
        to(cot, cot_out.at[c], sx.at[1], rx.at[1], b, sib),
        to(routes, routes_out.at[c], sx.at[2], rx.at[2], b, sib),
        pltpu.make_async_copy(ws, w_out.at[c, rows(b * 32, 32)], ls.at[0]),
        pltpu.make_async_copy(li, li_out.at[xl], ls.at[1]),
        pltpu.make_async_copy(cot, cot_out.at[c], ls.at[2]),
        pltpu.make_async_copy(routes, routes_out.at[c], ls.at[3]),
    ]
    for item in extra:
        item.start()

    def relay(d):
        first(d).wait_recv()
        second(d).start()

    times(1, NB, relay)
    times(1, NB, lambda d: first(d).wait_send())
    for item in extra:
        item.wait()
    times(1, NB, lambda d: second(d).wait())


def greet_all(bar, b, xl, c, y, m):
    h = 2 * xl + c
    times(1, NB, lambda d: signal(bar, lax.rem(b + d, NB), h))
    times(0, NB, lambda d: signal(bar, lax.rem(b + d, NB), 2 * (1 - xl) + c))
    for dj in range(GROUP):
        j = member(m, lax.rem(y + dj, GROUP))
        signal(bar, j, 2 * xl + 1 - c)
    pl.semaphore_wait(bar, 2 * NB - 1 + GROUP)


def pad_queries(both, qp, i):
    left = lax.broadcasted_iota(jnp.int32, (512, 128), 1) < 64
    qp[i, 0:512] = jnp.where(left, both, 0.0).astype(BF16)
    qp[i, 512:1024] = jnp.where(left, pltpu.roll(both, 64, 1), 0.0).astype(BF16)


def on_pair(p, m, inside, edge):
    def each(i):
        qb = member(m, i)
        whole = (p >= 1) & (2 * p + 1 <= qb - 1)
        pl.when(whole)(lambda: inside(i))
        pl.when(jnp.logical_not(whole) & (2 * p <= qb + 1))(lambda: edge(i, qb))

    times(0, GROUP, each)


def forward_kernel(
    info, query, keyval, wo, crows,
    q_out, kv_out, wo_out, c_out, ctx_out, wide_out, inv_out,
    qg, kvs, qp, vt, acc, accm, peer, ctx,
    s1, r1, s2, r2, s3, r3, s4, r4, s5, r5, s6, r6, s7, r7, ls,
):
    b, xl, c, y, m = place()
    h = 2 * xl + c
    sib = 2 * xl + 1 - c
    e0, e1, total = info[0], info[1], info[2]
    greet_all(pltpu.get_barrier_semaphore(), b, xl, c, y, m)

    def q_piece(dj, dc):
        j = lax.rem(y + dj, GROUP)
        cols = pl.ds(pl.multiple_of(j * 128, 128), 128)
        k = 2 * dj + dc
        src, dst = query.at[:, cols], qg.at[y, rows(c * 256, 256)]
        if k == 0:
            return pltpu.make_async_copy(src, dst, ls.at[0])
        return to(src, dst, s1.at[k], r1.at[k], member(m, j), 2 * xl + lax.rem(c + dc, 2))

    q_pieces = [q_piece(dj, dc) for dj in range(GROUP) for dc in range(2)]

    def kv_piece(d):
        peer_b = lax.rem(b + d, NB)
        cols = pl.ds(pl.multiple_of((peer_b // 8) * 128, 128), 128)
        return to(keyval.at[:, cols], kvs.at[b], s2.at[d], r2.at[d], peer_b, h)

    def wo_piece(e):
        d, x2 = lax.rem(e, NB), lax.rem(xl + e // NB, 2)
        part = wo_out.at[h, rows(b * 32, 32)]
        return to(wo, part, s3.at[e], r3.at[e], lax.rem(b + d, NB), 2 * x2 + c)

    def wo_relay(e):
        d, x2 = lax.rem(e, NB), lax.rem(xl + e // NB, 2)
        part = wo_out.at[2 * x2 + c, rows(lax.rem(b + NB - d, NB) * 32, 32)]
        return to(part, part, s4.at[e], r4.at[e], b, sib)

    for item in q_pieces:
        item.start()
    own_cols = pl.ds(pl.multiple_of(y * 128, 128), 128)
    own = [
        pltpu.make_async_copy(keyval.at[:, own_cols], kvs.at[b], ls.at[1]),
        pltpu.make_async_copy(wo, wo_out.at[h, rows(b * 32, 32)], ls.at[2]),
        to(wo, wo_out.at[h, rows(b * 32, 32)], s4.at[0], r4.at[0], b, sib),
    ]
    for item in own:
        item.start()
    times(1, NB, lambda d: kv_piece(d).start())
    times(1, 2 * NB, lambda e: wo_piece(e).start())
    send_rows(crows, c_out, b, c, h, s5, r5, ls.at[3], "start")
    for item in q_pieces:
        item.wait()
    own[0].wait()
    q_keep = pltpu.make_async_copy(qg, q_out, ls.at[4])
    q_keep.start()
    for i in range(GROUP):
        pad_queries(qg[i].astype(F32), qp, i)
    acc[...] = jnp.zeros_like(acc)
    accm[...] = jnp.zeros_like(accm)
    vt[64:80] = jnp.ones((16, 512), BF16)

    def pair(dp):
        p = lax.rem(b // 2 + 16 - dp, 16)
        for kb in (2 * p, 2 * p + 1):

            @pl.when(kb != b)
            def _():
                kv_piece(lax.rem(b + NB - kb, NB)).wait_recv()

        vt[0:64] = (
            kvs[pl.ds(2 * p, 2)].reshape(512, 128).astype(F32).T[64:128].astype(BF16)
        )

        def scores(i):
            keys = kvs[pl.ds(2 * p, 2)].reshape(512, 128)
            return jnp.exp(lax.dot_general(keys, qp[i], NT, preferred_element_type=F32))

        def inside(i):
            acc[i] += jnp.dot(vt[...], scores(i).astype(BF16), preferred_element_type=F32)

        def edge(i, qb):
            low, high = limits(query_positions((1, 1024), 1, qb), e0, e1, total)
            kpos = key_positions((512, 1), 0, 2 * p, c)
            expo = jnp.where((kpos >= low) & (kpos < high), scores(i), 0.0)
            accm[i] += jnp.dot(vt[...], expo.astype(BF16), preferred_element_type=F32)

        on_pair(p, m, inside, edge)

    times(0, 16, pair)
    for i in range(GROUP):
        pos = query_positions((1, 1024), 1, member(m, i))
        acc[i] = accm[i] + jnp.where((pos >= e0) & (pos < e1), acc[i], 0.0)
    swap = to(acc, peer, s6.at[0], r6.at[0], b, sib)
    swap.start()
    kv_keep = pltpu.make_async_copy(kvs, kv_out, ls.at[5])
    kv_keep.start()

    def relay(e):
        wo_piece(e).wait_recv()
        wo_relay(e).start()

    times(1, 2 * NB, relay)
    swap.wait()

    def ctx_piece(dj, dx):
        j = lax.rem(y + dj, GROUP)
        x2 = lax.rem(xl + dx, 2)
        cols = pl.ds(pl.multiple_of((4 * xl + y) * 128, 128), 128)
        src, dst = ctx.at[j, rows(c * 256 + x2 * 128, 128)], ctx_out.at[:, cols]
        k = 2 * dj + dx
        if k == 0:
            return pltpu.make_async_copy(src, dst, ls.at[6])
        return to(src, dst, s7.at[k], r7.at[k], member(m, j), 2 * x2 + c)

    ctx_pieces = [ctx_piece(dj, dx) for dj in range(GROUP) for dx in range(2)]
    for i in range(GROUP):
        both = acc[i] + peer[i]
        inverse = 1.0 / both[64:65]
        wide = both[0:64] * inverse
        flat = jnp.concatenate([wide[:, 0:512], wide[:, 512:1024]], axis=0).T
        wide_out[i] = flat
        ctx[i] = flat.astype(BF16)
        spread = jnp.broadcast_to(inverse, (64, 1024))
        inv_out[i] = jnp.concatenate([spread[:, 0:512], spread[:, 512:1024]], axis=0).T
    for item in ctx_pieces:
        item.start()
    for item in ctx_pieces:
        item.wait()
    own[1].wait()
    own[2].wait()
    times(1, NB, lambda d: kv_piece(d).wait_send())
    times(1, 2 * NB, lambda e: wo_piece(e).wait_send())
    times(1, 2 * NB, lambda e: wo_relay(e).wait())
    send_rows(crows, c_out, b, c, h, s5, r5, ls.at[3], "wait")
    q_keep.wait()
    kv_keep.wait()


def send_rows(src, dst, b, c, h, send, recv, local, what):
    odd = lax.rem(b + c, 2)

    def piece(d):
        k = lax.rem(b // 2 + d, 16)
        return to(src.at[k], dst.at[b // 2], send.at[d], recv.at[d], 2 * k + odd, h)

    def act(d):
        if what == "start":
            piece(d).start()
        else:
            piece(d).wait()

    times(1, 16, act)
    same = pltpu.make_async_copy(src.at[b // 2], dst.at[b // 2], local)

    @pl.when(c == 0)
    def _():
        if what == "start":
            same.start()
        else:
            same.wait()

    @pl.when(c == 1)
    def _():
        act(0)


def greet_rows(bar, b, c, h, sib):
    odd = lax.rem(b + c, 2)
    times(1, 16, lambda d: signal(bar, 2 * lax.rem(b // 2 + d, 16) + odd, h))
    signal(bar, b, sib)

    @pl.when(c == 1)
    def _():
        signal(bar, 2 * (b // 2) + odd, h)

    pl.semaphore_wait(bar, 16 + c)


def dispatch_kernel(mixed, gates, pick, out, gates_out, both_out, gates_both, tok, gt, stage, gstage, s1, r1, s2, r2, sx, rx, ls):
    b, xl, c, _, _ = place()
    h = 2 * xl + c
    sib = 2 * xl + 1 - c
    greet_rows(pltpu.get_barrier_semaphore(), b, c, h, sib)
    odd = lax.rem(b + c, 2)
    near = [
        to(mixed, tok.at[rows(c * 128, 128)], sx.at[0], rx.at[0], b, sib),
        to(gates, gt.at[rows(c * 128, 128)], sx.at[1], rx.at[1], b, sib),
    ]
    for item in near:
        item.start()
    tok[rows(c * 128, 128)] = mixed[...]
    gt[rows(c * 128, 128)] = gates[...]
    for item in near:
        item.wait()

    def each(d):
        k = lax.rem(b // 2 + d, 16)
        stage[k] = jnp.dot(pick[k], tok[...], preferred_element_type=F32).astype(BF16)
        piece = to(stage.at[k], out.at[b // 2], s1.at[d], r1.at[d], 2 * k + odd, h)
        if_remote(d, c, piece.start)

    times(1, 17, each)
    same = pltpu.make_async_copy(stage.at[b // 2], out.at[b // 2], ls.at[0])
    pl.when(c == 0)(same.start)
    high = gt[...].astype(BF16)
    rest = gt[...] - high.astype(F32)
    mid = rest.astype(BF16)
    low = (rest - mid.astype(F32)).astype(BF16)
    lane = lax.broadcasted_iota(jnp.int32, (80, 128), 1)

    def each_gate(d):
        k = lax.rem(b // 2 + d, 16)
        mine = pick[k]
        spread = (
            jnp.dot(mine, high, preferred_element_type=F32)
            + jnp.dot(mine, mid, preferred_element_type=F32)
            + jnp.dot(mine, low, preferred_element_type=F32)
        )
        column = jnp.sum(jnp.where(lane == 2 * k + odd, spread, 0.0), axis=1, keepdims=True)
        wide = jnp.concatenate([jnp.broadcast_to(column, (80, 128)), jnp.zeros((48, 128), F32)])
        gstage[k] = wide.T[0:8]
        piece = to(gstage.at[k], gates_out.at[b // 2], s2.at[d], r2.at[d], 2 * k + odd, h)
        if_remote(d, c, piece.start)

    times(1, 17, each_gate)
    same_gate = pltpu.make_async_copy(gstage.at[b // 2], gates_out.at[b // 2], ls.at[1])
    pl.when(c == 0)(same_gate.start)
    both_out[...] = tok[...]
    gates_both[...] = gt[...]

    def finish(d):
        k = lax.rem(b // 2 + d, 16)
        one = to(stage.at[k], out.at[b // 2], s1.at[d], r1.at[d], 2 * k + odd, h)
        two = to(gstage.at[k], gates_out.at[b // 2], s2.at[d], r2.at[d], 2 * k + odd, h)
        if_remote(d, c, one.wait)
        if_remote(d, c, two.wait)

    times(1, 17, finish)
    pl.when(c == 0)(same.wait)
    pl.when(c == 0)(same_gate.wait)


def if_remote(d, c, act):
    pl.when((d < 16) | (c == 1))(act)


def return_kernel(rg, gg, pick, pick_t, mg_out, gg_out, land, gland, mgs, ggs, s1, r1, s2, r2, sx, rx, ls):
    b, xl, c, _, _ = place()
    h = 2 * xl + c
    sib = 2 * xl + 1 - c
    greet_rows(pltpu.get_barrier_semaphore(), b, c, h, sib)
    send_rows(gg, gland, b, c, h, s2, r2, ls.at[1], "start")
    send_rows(rg, land, b, c, h, s1, r1, ls.at[0], "start")
    send_rows(gg, gland, b, c, h, s2, r2, ls.at[1], "wait")

    def each(k):
        column = jnp.concatenate([gland[k], jnp.zeros((120, 128), F32)]).T[0:80, 0:1]
        ggs[pl.ds(k, 1)] = jnp.sum(pick[k].astype(F32) * column, axis=0, keepdims=True)

    for k in range(16):
        each(k)
    send_rows(rg, land, b, c, h, s1, r1, ls.at[0], "wait")
    mgs[...] = jnp.dot(pick_t[...], land[...].reshape(1280, 1024), preferred_element_type=F32)
    away = rows((1 - c) * 128, 128)
    home = rows(c * 128, 128)
    near = [
        to(mgs.at[away], mg_out.at[1], sx.at[0], rx.at[0], b, sib),
        to(ggs.at[:, away], gg_out.at[1], sx.at[1], rx.at[1], b, sib),
        pltpu.make_async_copy(mgs.at[home], mg_out.at[0], ls.at[2]),
        pltpu.make_async_copy(ggs.at[:, home], gg_out.at[0], ls.at[3]),
    ]
    for item in near:
        item.start()
    for item in near:
        item.wait()


def backward_kernel(
    info, cg, q_ref, kv_ref, wide_ref, inv_ref, eo, wo_mine, wo_other, ex_mine, ex_other,
    dq_out, dkv_out, eo_out, wo_out, ex_out,
    cgs, qp, gp, gi, qt, gt, gti, dt, di, dqs, dkvt, stage, dq_acc,
    wo_in, wo_sum, ex_in, ex_sum, ex_cross, ex_all,
    s1, r1, s2, r2, s3, r3, s4, r4, s5, r5, sx, rx, ls,
):
    b, xl, c, y, m = place()
    h = 2 * xl + c
    sib = 2 * xl + 1 - c
    over = 2 * (1 - xl) + c
    e0, e1, total = info[0], info[1], info[2]
    bar = pltpu.get_barrier_semaphore()
    for dj in range(GROUP):
        j = member(m, lax.rem(y + dj, GROUP))
        signal(bar, j, 2 * (1 - xl) + 1 - c)
        signal(bar, j, 2 * xl + 1 - c)
    times(1, NB, lambda d: signal(bar, lax.rem(b + d, NB), h))
    times(0, NB, lambda d: signal(bar, lax.rem(b + d, NB), over))
    pl.semaphore_wait(bar, 2 * NB - 1 + 2 * GROUP)

    turns = [(dj, dx, dc) for dj in range(GROUP) for dx in range(2) for dc in range(2)]
    cg_pieces = []
    for k, (dj, dx, dc) in enumerate(turns):
        j = lax.rem(y + dj, GROUP)
        x2 = lax.rem(xl + dx, 2)
        cols = pl.ds(pl.multiple_of((4 * x2 + j) * 128, 128), 128)
        src, dst = cg.at[:, cols], cgs.at[y, rows(c * 256 + xl * 128, 128)]
        if k == 0:
            cg_pieces.append(pltpu.make_async_copy(src, dst, ls.at[0]))
        else:
            head = 2 * x2 + lax.rem(c + dc, 2)
            cg_pieces.append(to(src, dst, s1.at[k], r1.at[k], member(m, j), head))
    for item in cg_pieces:
        item.start()
    wo_swap = to(wo_other, wo_in, sx.at[0], rx.at[0], b, sib)
    wo_swap.start()
    ex_swap = to(ex_other, ex_in, sx.at[1], rx.at[1], b, sib)
    ex_swap.start()
    for i in range(GROUP):
        both = q_ref[i].astype(F32)
        pad_queries(both, qp, i)
        turned = both.T
        qt[i] = jnp.concatenate([turned[0:64], turned[64:128]], axis=1).astype(BF16)
    dq_acc[...] = jnp.zeros_like(dq_acc)
    wo_swap.wait()
    wo_sum[...] = (wo_mine[...].astype(F32) + wo_in[...].astype(F32)).astype(BF16)
    ex_swap.wait()
    ex_sum[...] = (ex_mine[...].astype(F32) + ex_in[...].astype(F32)).astype(BF16)
    cross = to(ex_sum, ex_cross, sx.at[2], rx.at[2], b, over)
    cross.start()

    def wo_piece(e):
        d, x2 = lax.rem(e, NB), lax.rem(xl + e // NB, 2)
        peer_b = lax.rem(b + d, NB)
        part = wo_sum.at[x2, rows(peer_b * 32, 32)]
        return to(part, wo_out.at[xl, b], s3.at[e], r3.at[e], peer_b, 2 * x2 + c)

    for item in cg_pieces:
        item.wait()
    wo_own = pltpu.make_async_copy(wo_sum.at[xl, rows(b * 32, 32)], wo_out.at[xl, b], ls.at[1])
    wo_own.start()
    send_rows(eo, eo_out, b, c, h, s2, r2, ls.at[2], "start")
    times(1, 2 * NB, lambda e: wo_piece(e).start())
    left = lax.broadcasted_iota(jnp.int32, (512, 128), 1) < 64
    for i in range(GROUP):
        scaled = cgs[i].astype(F32) * inv_ref[i]
        pos = query_positions((512, 1), 0, member(m, i))
        middle = (pos >= e0) & (pos < e1)
        terms = scaled * wide_ref[i]
        one = jnp.sum(jnp.where(left, terms, 0.0), axis=1, keepdims=True)
        two = jnp.sum(jnp.where(left, 0.0, terms), axis=1, keepdims=True)
        top = jnp.where(left, 0.0, pltpu.roll(scaled, 64, 1))
        low = jnp.where(left, 0.0, scaled)
        for part, val, term in ((0, top, one), (512, low, two)):
            span = pl.ds(part, 512)
            gp[i, span] = val.astype(BF16)
            gi[i, span] = jnp.where(middle, val, 0.0).astype(BF16)
            dt[i, span] = jnp.broadcast_to(term, (512, 128))
            di[i, span] = jnp.broadcast_to(jnp.where(middle, term, 0.0), (512, 128))
            lanes = pl.ds(part, 512)
            gt[i, :, lanes] = val.T[64:128].astype(BF16)
            gti[i, :, lanes] = jnp.where(middle, val, 0.0).T[64:128].astype(BF16)

    def dkv_piece(kb, slot):
        return to(stage.at[kb], dkv_out.at[b], s4.at[kb], r4.at[slot], kb, h)

    def pair(dp):
        p = lax.rem(b // 2 + 1 + dp, 16)
        dkvt[...] = jnp.zeros_like(dkvt)
        keys = kv_ref[pl.ds(2 * p, 2)].reshape(512, 128)

        def step(i, expo, g, gturn, dots):
            prob = lax.dot_general(g[i], keys, NT, preferred_element_type=F32)
            term = jnp.concatenate([dots[i]] * 4, axis=1)
            score_grad = (expo * (prob - term)).astype(BF16)
            dq_acc[i] += jnp.dot(score_grad, keys, preferred_element_type=F32)
            dkvt[0:64] += jnp.dot(qt[i], score_grad, preferred_element_type=F32)
            dkvt[64:128] += jnp.dot(gturn[i], expo.astype(BF16), preferred_element_type=F32)

        def scores(i):
            return jnp.exp(lax.dot_general(qp[i], keys, NT, preferred_element_type=F32))

        def inside(i):
            step(i, scores(i), gi, gti, di)

        def edge(i, qb):
            low, high = limits(query_positions((1024, 1), 0, qb), e0, e1, total)
            kpos = key_positions((1, 512), 1, 2 * p, c)
            expo = jnp.where((kpos >= low) & (kpos < high), scores(i), 0.0)
            step(i, expo, gp, gt, dt)

        on_pair(p, m, inside, edge)
        flat = dkvt[...].T.astype(BF16)
        for n in range(2):
            kb = 2 * p + n
            stage[kb] = flat[256 * n : 256 * n + 256]

            @pl.when(kb != b)
            def _():
                dkv_piece(kb, b).start()

    times(0, 16, pair)
    dkv_own = pltpu.make_async_copy(stage.at[b], dkv_out.at[b], ls.at[3])
    dkv_own.start()
    for i in range(GROUP):
        both = jnp.where(left, dq_acc[i, 0:512], pltpu.roll(dq_acc[i, 512:1024], 64, 1))
        dqs[i] = (both * SCALE).astype(BF16)

    def dq_piece(dj, dc):
        j = lax.rem(y + dj, GROUP)
        c2 = lax.rem(c + dc, 2)
        cols = pl.ds(pl.multiple_of(y * 128, 128), 128)
        src, dst = dqs.at[j, rows(c2 * 256, 256)], dq_out.at[c, :, cols]
        k = 2 * dj + dc
        if k == 0:
            return pltpu.make_async_copy(src, dst, ls.at[4])
        return to(src, dst, s5.at[k], r5.at[k], member(m, j), 2 * xl + c2)

    dq_pieces = [dq_piece(dj, dc) for dj in range(GROUP) for dc in range(2)]
    for item in dq_pieces:
        item.start()
    cross.wait()
    ex_all[...] = (ex_sum[...].astype(F32) + ex_cross[...].astype(F32)).astype(BF16)
    half = rows(c * 512, 512)
    ex_home = pltpu.make_async_copy(ex_all, ex_out.at[:, half], ls.at[5])
    ex_home.start()
    ex_back = to(ex_all, ex_out.at[:, half], sx.at[3], rx.at[3], b, sib)
    ex_back.start()
    for item in dq_pieces:
        item.wait()
    ex_home.wait()
    ex_back.wait()
    wo_own.wait()
    dkv_own.wait()
    times(1, 2 * NB, lambda e: wo_piece(e).wait())

    def finish(d):
        src = lax.rem(b + d, NB)
        dkv_piece(src, src).wait()

    times(1, NB, finish)
    send_rows(eo, eo_out, b, c, h, s2, r2, ls.at[2], "wait")


def tail_kernel(
    w_mine, w_other, back, mix, small, w_out, back_out, mix_out, small_out,
    w_in, w_sum, w_land, four, many, s1, r1, s2, r2, s3, r3, sx, rx, ls,
):
    b, xl, c, _, _ = place()
    h = 2 * xl + c
    sib = 2 * xl + 1 - c
    over = 2 * (1 - xl) + c
    bar = pltpu.get_barrier_semaphore()
    times(1, NB, lambda d: signal(bar, lax.rem(b + d, NB), h))
    for d in range(1, 4):
        signal(bar, b, lax.rem(h + d, 4))
    pl.semaphore_wait(bar, NB + 2)
    w_swap = to(w_other, w_in, sx.at[0], rx.at[0], b, sib)
    w_swap.start()
    near = [
        to(small, four.at[h], s2.at[d], r2.at[d], b, lax.rem(h + d, 4)) for d in range(1, 4)
    ]
    for item in near:
        item.start()
    swaps = [
        to(back, back_out, sx.at[1], rx.at[1], b, over),
        to(mix, mix_out, sx.at[2], rx.at[2], b, sib),
    ]
    for item in swaps:
        item.start()
    four[h] = small[...]
    w_swap.wait()
    w_sum[...] = (w_mine[...].astype(F32) + w_in[...].astype(F32)).astype(BF16)

    def w_piece(d):
        peer = lax.rem(b + d, NB)
        return to(w_sum.at[peer], w_land.at[b], s1.at[d], r1.at[d], peer, h)

    times(1, NB, lambda d: w_piece(d).start())
    w_land[b] = w_sum[b]
    for item in near:
        item.wait()
    many[b] = four[0] + four[1] + four[2] + four[3]

    def far(d):
        return to(many.at[b], many.at[b], s3.at[d], r3.at[d], lax.rem(b + d, NB), h)

    times(1, NB, lambda d: far(d).start())
    times(1, NB, lambda d: far(d).wait())
    total = many[0]
    for i in range(1, NB):
        total = total + many[i]
    small_out[...] = total
    times(1, NB, lambda d: w_piece(d).wait())
    shard = w_land[0].astype(F32)
    for i in range(1, NB):
        shard = shard + w_land[i].astype(F32)
    w_out[...] = shard
    for item in swaps:
        item.wait()


VM = pl.BlockSpec(memory_space=pltpu.VMEM)
SM = pl.BlockSpec(memory_space=pltpu.SMEM)
ANY = pl.BlockSpec(memory_space=pl.ANY)


def call(kernel, collective_id, ins, outs, scratch, sems, flops, *operands):
    return pl.pallas_call(
        kernel,
        out_shape=[jax.ShapeDtypeStruct(shape, dtype) for shape, dtype, _ in outs],
        in_specs=ins,
        out_specs=[spec for _, _, spec in outs],
        scratch_shapes=[pltpu.VMEM(shape, dtype) for shape, dtype in scratch]
        + [pltpu.SemaphoreType.DMA(n) for n in sems],
        compiler_params=pltpu.CompilerParams(
            collective_id=collective_id,
            has_side_effects=True,
            vmem_limit_bytes=60 * 1024 * 1024,
        ),
        cost_estimate=pl.CostEstimate(
            flops=flops, bytes_accessed=8_000_000, transcendentals=flops // 2000
        ),
    )(*operands)


def limits(pos, e0, e1, total):
    low = jnp.where(pos < e0, 0, jnp.where(pos < e1, e0, e1))
    end = jnp.where(pos < e0, e0, jnp.where(pos < e1, e1, total))
    reach = low + ((pos - low) // BLOCK + 1) * BLOCK
    return low, jnp.minimum(end, reach)


def query_positions(shape, axis, qb):
    r = lax.broadcasted_iota(jnp.int32, shape, axis)
    r = lax.rem(r, 512)
    return 512 * qb + 256 * lax.rem(r // 128, 2) + 128 * (r // 256) + lax.rem(r, 128)


def key_positions(shape, axis, kb, core):
    r = lax.broadcasted_iota(jnp.int32, shape, axis)
    return 512 * (kb + r // 256) + 256 * lax.rem(r // 128, 2) + 128 * core + lax.rem(r, 128)


def rms_scale(values, gain_row):
    return (
        values * lax.rsqrt(jnp.mean(values * values, axis=-1, keepdims=True) + EPSILON) * gain_row
    )


def rotary(values, inside):
    half = values.shape[-1] // 2
    frequency = jnp.power(ROPE_BASE, -2.0 * jnp.arange(half, dtype=F32) / values.shape[-1])
    angles = inside.astype(F32)[:, None] * frequency[None, :]
    cosine, sine = jnp.cos(angles)[:, None, :], jnp.sin(angles)[:, None, :]
    first, second = values[..., :half], values[..., half:]
    return jnp.concatenate(
        [first * cosine - second * sine, second * cosine + first * sine], axis=-1
    )


def head_prep(raw_heads, gain_row, inside):
    return rotary(rms_scale(raw_heads, gain_row), inside)


def from_head(value, bit):
    return lax.ppermute(value, "head", [(i, i ^ bit) for i in range(4)])


def body(
    layer_input,
    attn_gain,
    w_query,
    key_weight,
    value_weight,
    w_output,
    query_gain,
    key_gain,
    ffn_gain,
    router,
    w_gate,
    w_up,
    w_down,
    routes,
    doc_lengths,
    cotangent,
):
    b, xl, c, y, m = place()
    tokens, width = layer_input.shape
    total = tokens * 4 * NB
    ends = jnp.cumsum(doc_lengths)
    info = jnp.stack([ends[0], ends[1], jnp.int32(total), c]).astype(jnp.int32)

    shard = jnp.concatenate(
        [
            w_query,
            key_weight[:, :64],
            value_weight[:, :64],
            key_weight[:, 64:],
            value_weight[:, 64:],
        ],
        axis=1,
    )
    w_full, both_inputs, both_cot, both_routes = call(
        weights_kernel,
        0,
        [ANY] * 4,
        [
            ((2, width, 512), BF16, ANY),
            ((2, tokens, width), BF16, ANY),
            ((2, tokens, width), BF16, ANY),
            ((2, tokens, TOPK), jnp.int32, ANY),
        ],
        [],
        [(NB,)] * 4 + [(3,), (3,), (4,)],
        0,
        shard,
        layer_input,
        cotangent,
        routes,
    )

    routes2 = both_routes.reshape(2 * tokens, TOPK)
    chosen2 = jnp.any(routes2[:, :, None] == jnp.arange(NB, dtype=jnp.int32), axis=1)
    before = jnp.tril(jnp.ones((2 * tokens, 2 * tokens), BF16), -1)
    rank = jnp.dot(before, chosen2.astype(BF16), preferred_element_type=F32).astype(jnp.int32)
    odd = (b + c) % 2

    def of_mine(table):
        pairs = table.reshape(2 * tokens, 16, 2)
        return jnp.where(odd == 0, pairs[:, :, 0], pairs[:, :, 1]).T

    slot = jnp.arange(SLOTS, dtype=jnp.int32)
    at_slot = of_mine(chosen2)[:, None, :] & (of_mine(rank)[:, None, :] == slot[None, :, None])
    pick = at_slot.astype(BF16)
    flat_pick = pick.reshape(16 * SLOTS, 2 * tokens)
    pick_t = flat_pick.T
    cot2 = both_cot.reshape(2 * tokens, width)
    cot_rows = (
        jnp.dot(flat_pick, cot2, preferred_element_type=F32)
        .astype(BF16)
        .reshape(16, SLOTS, width)
    )

    source2 = both_inputs.reshape(2 * tokens, width).astype(F32)
    normed_wide, attn_pull = jax.vjp(rms_scale, source2, attn_gain)
    normed = normed_wide.astype(BF16)
    raw = [jnp.dot(normed, w_full[i], preferred_element_type=F32) for i in range(2)]
    query_raw = jnp.concatenate([raw[0][:, :256], raw[1][:, :256]], axis=1).reshape(-1, 8, 64)
    kv_raw = jnp.concatenate([raw[0][:, 256:], raw[1][:, 256:]], axis=1).reshape(-1, 4, 2, 64)
    t = jnp.arange(2 * tokens, dtype=jnp.int32)
    pos = 512 * b + 256 * (t // 128) + 128 * c + t % 128
    opening = jnp.where(pos < ends[0], 0, jnp.where(pos < ends[1], ends[0], ends[1]))
    inside = pos - opening
    prep = functools.partial(head_prep, inside=inside)
    query_prep, query_pull = jax.vjp(prep, query_raw, query_gain)
    key_prep, key_pull = jax.vjp(prep, kv_raw[:, :, 0], key_gain)
    query = (query_prep.astype(BF16) * SCALE).astype(BF16).reshape(2 * tokens, 512)
    keyval = (
        jnp.stack([key_prep, kv_raw[:, :, 1]], axis=2).astype(BF16).reshape(2 * tokens, 512)
    )
    q_group, kv_all, out_full, up_rows, context, ctx_wide, ctx_inv = call(
        forward_kernel,
        1,
        [SM] + [ANY] * 4,
        [
            ((GROUP, 512, 128), BF16, ANY),
            ((NB, 256, 128), BF16, ANY),
            ((4, width, width // 4), BF16, ANY),
            ((16, SLOTS, width), BF16, ANY),
            ((tokens, width), BF16, ANY),
            ((GROUP, 512, 128), F32, VM),
            ((GROUP, 512, 128), F32, VM),
        ],
        [
            ((GROUP, 512, 128), BF16),
            ((NB, 256, 128), BF16),
            ((GROUP, 1024, 128), BF16),
            ((80, 512), BF16),
            ((GROUP, 80, 1024), F32),
            ((GROUP, 80, 1024), F32),
            ((GROUP, 80, 1024), F32),
            ((GROUP, 512, 128), BF16),
        ],
        [(8,)] * 2 + [(NB,)] * 2 + [(2 * NB,)] * 4 + [(16,)] * 2 + [(1,)] * 2 + [(8,)] * 2 + [(7,)],
        18_000_000_000,
        info,
        query,
        keyval,
        w_output,
        cot_rows,
    )

    source = layer_input.astype(F32)
    projected = [jnp.dot(context, out_full[i], preferred_element_type=F32) for i in range(4)]
    middle = source + jnp.concatenate(projected, axis=1)
    mixed_wide, ffn_pull = jax.vjp(rms_scale, middle, ffn_gain)
    mixed_in = mixed_wide.astype(BF16)
    chosen = jnp.any(routes[:, :, None] == jnp.arange(NB, dtype=jnp.int32), axis=1)
    logits = jnp.dot(mixed_in.astype(F32), router, precision=PRECISE)
    top = jnp.max(jnp.where(chosen, logits, -jnp.inf), axis=1, keepdims=True)
    weight = jnp.where(chosen, jnp.exp(logits - top), 0.0)
    gates = weight / jnp.sum(weight, axis=1, keepdims=True)
    expert_in, gates_in, mixed2, gates2 = call(
        dispatch_kernel,
        2,
        [VM] * 3,
        [
            ((16, SLOTS, width), BF16, ANY),
            ((16, 8, 128), F32, ANY),
            ((2 * tokens, width), BF16, VM),
            ((2 * tokens, 128), F32, VM),
        ],
        [
            ((2 * tokens, width), BF16),
            ((2 * tokens, 128), F32),
            ((16, SLOTS, width), BF16),
            ((16, 8, 128), F32),
        ],
        [(17,)] * 4 + [(2,), (2,), (2,)],
        0,
        mixed_in,
        jnp.pad(gates, ((0, 0), (0, 96))),
        pick,
    )

    expert_in = expert_in.reshape(16 * SLOTS, width)
    gate_rows = gates_in[:, 0, :SLOTS].reshape(16 * SLOTS, 1)
    up_rows = up_rows.reshape(16 * SLOTS, width)
    gate_w, up_w, down_w = w_gate[0], w_up[0], w_down[0]
    gate_pre = jnp.dot(expert_in, gate_w, preferred_element_type=F32)
    up_pre = jnp.dot(expert_in, up_w, preferred_element_type=F32)
    sig = jax.nn.sigmoid(gate_pre)
    activated = gate_pre * sig
    hidden = (activated * up_pre).astype(BF16)
    expert_out = jnp.dot(hidden, down_w, preferred_element_type=F32).astype(BF16)
    upstream_rows = up_rows.astype(F32)
    gate_back_rows = jnp.sum(upstream_rows * expert_out.astype(F32), axis=1)
    out_grad = (gate_rows * upstream_rows).astype(BF16)
    hidden_grad = lax.dot_general(out_grad, down_w, NT, preferred_element_type=F32)
    gate_back = (hidden_grad * up_pre * sig * (1.0 + gate_pre * (1.0 - sig))).astype(BF16)
    up_back = (hidden_grad * activated).astype(BF16)
    rows_grad = lax.dot_general(
        gate_back, gate_w, NT, preferred_element_type=F32
    ) + lax.dot_general(up_back, up_w, NT, preferred_element_type=F32)
    sent_gg = jnp.pad(gate_back_rows.reshape(16, 1, SLOTS), ((0, 0), (0, 7), (0, 128 - SLOTS)))
    mg_parts, gg_parts = call(
        return_kernel,
        3,
        [ANY, ANY, VM, VM],
        [((2, tokens, width), F32, ANY), ((2, 16, tokens), F32, ANY)],
        [
            ((16, SLOTS, width), BF16),
            ((16, 8, 128), F32),
            ((2 * tokens, width), F32),
            ((16, 2 * tokens), F32),
        ],
        [(16,)] * 4 + [(2,), (2,), (4,)],
        0,
        rows_grad.astype(BF16).reshape(16, SLOTS, width),
        sent_gg,
        pick,
        pick_t,
    )

    first, second = jnp.where(odd == 0, gg_parts[0], gg_parts[1]), jnp.where(
        odd == 0, gg_parts[1], gg_parts[0]
    )
    gate_grad = jnp.stack([first, second], axis=1).reshape(NB, tokens).T
    logit_grad = gates * (gate_grad - jnp.sum(gates * gate_grad, axis=1, keepdims=True))
    router_grad = jnp.dot(mixed_in.astype(F32).T, logit_grad, precision=PRECISE)
    router_grad = lax.psum(router_grad, ("blk", "head"))
    mixed_grad = mg_parts[0] + mg_parts[1] + jnp.dot(logit_grad, router.T, precision=PRECISE)
    middle_norm_grad, ffn_gain_grad = ffn_pull(mixed_grad)
    upstream = cotangent.astype(F32)
    middle_grad = upstream + middle_norm_grad
    attn_grad = middle_grad.astype(BF16)
    context_grad = sum(
        lax.dot_general(
            attn_grad[:, 256 * i : 256 * i + 256], out_full[i], NT, preferred_element_type=F32
        )
        for i in range(4)
    ).astype(BF16)
    out_w_parts = [
        lax.dot_general(
            context, attn_grad[:, 256 * i : 256 * i + 256], TN, preferred_element_type=F32
        ).astype(BF16)
        for i in range(4)
    ]
    cores = [jnp.stack([out_w_parts[k], out_w_parts[2 + k]]) for k in range(2)]
    wo_mine = jnp.where(c == 0, cores[0], cores[1])
    wo_other = jnp.where(c == 0, cores[1], cores[0])
    down_w_grad = lax.dot_general(hidden, out_grad, TN, preferred_element_type=F32).astype(BF16)
    gate_w_grad = lax.dot_general(expert_in, gate_back, TN, preferred_element_type=F32)
    up_w_grad = lax.dot_general(expert_in, up_back, TN, preferred_element_type=F32)
    expert_grads = jnp.stack(
        [
            gate_w_grad.astype(BF16),
            up_w_grad.astype(BF16),
            jnp.concatenate([down_w_grad[:, :512], down_w_grad[:, 512:]], axis=0),
        ]
    )
    ex_mine = lax.dynamic_slice_in_dim(expert_grads, 512 * c, 512, axis=1)
    ex_other = lax.dynamic_slice_in_dim(expert_grads, 512 * (1 - c), 512, axis=1)
    dq_parts, dkv_parts, rows_home, wo_parts, ex_sums = call(
        backward_kernel,
        4,
        [SM, ANY, VM, VM, VM, VM, ANY, VM, ANY, VM, ANY],
        [
            ((2, 2 * tokens, 512), BF16, ANY),
            ((NB, 256, 128), BF16, ANY),
            ((16, SLOTS, width), BF16, ANY),
            ((2, NB, 32, 256), BF16, ANY),
            ((3, 1024, 512), BF16, ANY),
        ],
        [
            ((GROUP, 512, 128), BF16),
            ((GROUP, 1024, 128), BF16),
            ((GROUP, 1024, 128), BF16),
            ((GROUP, 1024, 128), BF16),
            ((GROUP, 64, 1024), BF16),
            ((GROUP, 64, 1024), BF16),
            ((GROUP, 64, 1024), BF16),
            ((GROUP, 1024, 128), F32),
            ((GROUP, 1024, 128), F32),
            ((GROUP, 512, 128), BF16),
            ((128, 512), F32),
            ((NB, 256, 128), BF16),
            ((GROUP, 1024, 128), F32),
            ((2, 1024, 256), BF16),
            ((2, 1024, 256), BF16),
            ((3, 512, 512), BF16),
            ((3, 512, 512), BF16),
            ((3, 512, 512), BF16),
            ((3, 512, 512), BF16),
        ],
        [(16,)] * 4 + [(2 * NB,)] * 2 + [(NB,)] * 2 + [(8,)] * 2 + [(4,)] * 2 + [(6,)],
        45_000_000_000,
        info,
        context_grad,
        q_group,
        kv_all,
        ctx_wide,
        ctx_inv,
        expert_out.reshape(16, SLOTS, width),
        wo_mine,
        wo_other,
        ex_mine,
        ex_other,
    )

    query_grad = (dq_parts[0].astype(F32) + dq_parts[1].astype(F32)).astype(BF16)
    dkv_sum = jnp.sum(dkv_parts.reshape(GROUP, 8, 256, 128).astype(F32), axis=1).astype(BF16)
    dkv_sum = dkv_sum.transpose(1, 0, 2).reshape(2 * tokens, 4, 2, 64)
    query_raw_grad, query_gain_grad = query_pull(query_grad.astype(F32).reshape(-1, 8, 64))
    key_raw_grad, key_gain_grad = key_pull(dkv_sum[:, :, 0].astype(F32))
    query_low = query_raw_grad.astype(BF16).reshape(2 * tokens, 512)
    kv_low = jnp.stack([key_raw_grad.astype(BF16), dkv_sum[:, :, 1]], axis=2).reshape(
        2 * tokens, 512
    )
    lows = [
        jnp.concatenate(
            [query_low[:, 256 * i : 256 * i + 256], kv_low[:, 256 * i : 256 * i + 256]], axis=1
        )
        for i in range(2)
    ]
    w_parts = [
        lax.dot_general(normed, lows[i], TN, preferred_element_type=F32).astype(BF16)
        for i in range(2)
    ]
    w_mine = jnp.where(c == 0, w_parts[0], w_parts[1]).reshape(NB, width // NB, 512)
    w_other = jnp.where(c == 0, w_parts[1], w_parts[0]).reshape(NB, width // NB, 512)
    normed_grad = sum(
        lax.dot_general(lows[i], w_full[i], NT, preferred_element_type=F32) for i in range(2)
    )
    norm_back, attn_gain_grad = attn_pull(normed_grad)
    halves = norm_back.reshape(2, tokens, width)
    back_mine = jnp.where(xl == 0, halves[0], halves[1])
    back_other = jnp.where(xl == 0, halves[1], halves[0])
    gates_t = gates2[:, :NB].reshape(2 * tokens, 16, 2)
    gates_t = jnp.where(odd == 0, gates_t[:, :, 0], gates_t[:, :, 1])
    weights = jnp.where(at_slot, gates_t.T[:, None, :], 0.0).reshape(16 * SLOTS, 2 * tokens)
    high = weights.astype(BF16)
    low = (weights - high.astype(F32)).astype(BF16)
    flat_home = rows_home.reshape(16 * SLOTS, width)
    mixture = lax.dot_general(high, flat_home, TN, preferred_element_type=F32) + lax.dot_general(
        low, flat_home, TN, preferred_element_type=F32
    )
    mixture = mixture.reshape(2, tokens, width)
    mix_mine = jnp.where(c == 0, mixture[0], mixture[1])
    mix_other = jnp.where(c == 0, mixture[1], mixture[0])
    smalls = jnp.concatenate(
        [attn_gain_grad, ffn_gain_grad, query_gain_grad, key_gain_grad, jnp.zeros((896,), F32)]
    ).reshape(24, 128)
    w_shard, back_in, mix_in, smalls = call(
        tail_kernel,
        5,
        [VM, ANY, ANY, ANY, VM],
        [
            ((width // NB, 512), F32, VM),
            ((tokens, width), F32, ANY),
            ((tokens, width), F32, ANY),
            ((24, 128), F32, VM),
        ],
        [
            ((NB, width // NB, 512), BF16),
            ((NB, width // NB, 512), BF16),
            ((NB, width // NB, 512), BF16),
            ((4, 24, 128), F32),
            ((NB, 24, 128), F32),
        ],
        [(NB,)] * 2 + [(4,)] * 2 + [(NB,)] * 2 + [(3,)] * 2 + [(1,)],
        0,
        w_mine,
        w_other,
        back_other,
        mix_other,
        smalls,
    )
    input_grad = (middle_grad + back_mine + back_in).astype(BF16)
    layer_output = (middle + mix_mine + mix_in).astype(BF16)
    w_output_grad = jnp.sum(wo_parts.reshape(2 * NB, 32, 256).astype(F32), axis=0)
    smalls = smalls.reshape(-1)
    down_sum = jnp.concatenate([ex_sums[2, :512], ex_sums[2, 512:]], axis=1)
    return (
        layer_output,
        input_grad,
        smalls[:1024],
        w_shard[:, :256],
        jnp.concatenate([w_shard[:, 256:320], w_shard[:, 384:448]], axis=1),
        jnp.concatenate([w_shard[:, 320:384], w_shard[:, 448:512]], axis=1),
        w_output_grad,
        smalls[2048:2112],
        smalls[2112:2176],
        smalls[1024:2048],
        router_grad,
        ex_sums[0].astype(F32)[None],
        ex_sums[1].astype(F32)[None],
        down_sum.astype(F32)[None],
    )


def solution(mesh):
    everyone = P(("blk", "head"), None)
    both = P("blk", "head")
    expert = P("blk", None, None)
    return jax.shard_map(
        body,
        mesh=mesh,
        in_specs=(everyone, P(), both, both, both, both, P(), P(), P(), P())
        + (expert, expert, expert, everyone, P(), everyone),
        out_specs=(everyone, everyone, P(), both, both, both, both, P(), P(), P(), P())
        + (expert, expert, expert),
        check_vma=False,
    )
```

time: 700 us -> 553 us (0.79)
  starting transfers between devices: 82.4 us -> 0.04 us
  waiting for transfers between devices: 39.3 us -> 0.02 us
  other arithmetic: 47.8 us -> 31.6 us
  blocking collectives: 13.1 us -> 0 us
  Pallas kernels: 390 us -> 401 us
    all_to_all x6 -> x0, starting transfers between devices: 67.1 us -> none  [the longest x5 58.7 us: to_experts(): return lax.all_to_all(value, 'blk', split_axis=0, concat_axis=0, tiled=True)]
    all_to_all x6 -> x0, waiting for transfers between devices: 39.2 us -> none  [the longest x5 39.2 us: to_experts(): return lax.all_to_all(value, 'blk', split_axis=0, concat_axis=0, tiled=True)]
    all_to_all x1 -> x0, blocking collectives: 13.1 us -> none  [to_experts(): return lax.all_to_all(value, 'blk', split_axis=0, concat_axis=0, tiled=True)]
    convert_element_type x11 -> x4, other arithmetic: 20.2 us -> 8.2 us  [the longest x1 4.23 us: body(): ex_sums[1].astype(F32)[None]]
    pallas_call x10 -> x6, Pallas kernels: 390 us -> 401 us  [call(): pl.pallas_call(kernel, out_shape=[jax.ShapeDtypeStruct(shape, dtype) for...]
    psum x1, starting transfers between devices: 8.69 us -> 0.04 us  [body(): router_grad = lax.psum(router_grad, ('blk', 'head'))]
  transfers between devices with their start and end apart: 19 -> 1, of which waited for: 3 -> 0; matrix products, arithmetic and copies ran while one was open for 15% -> 11% of each run, Pallas kernels for 37% -> 31%
where the time goes in v2:
time: 553 us; the launch traced here: 545 us
  Pallas kernels  401 us (73%)
  matrix products  66.6 us (12%)
  other arithmetic  31.6 us (6%)
  local copies, waits for them, and re-layouts  29.9 us (5%)
  between operations  16 us (3%)
    pallas_call x6, Pallas kernels, call(): pl.pallas_call(kernel, out_shape=[jax.ShapeDtypeStruct(shape, dtype) for...  401 us
  transfers between devices with their start and end apart: 1, of which 0 were waited for; matrix products, arithmetic and copies ran while one was open for 11% of the time, Pallas kernels for 31%

profile of v2, /device:TPU:4, one launch (start us, length us, event | category | flops | bytes accessed | tf_op | source)
XLA Modules:
  0.0 544.6 jit_solution(5813036797550369621)
XLA Ops:
  7.3 1.5 copy.96.routes
  8.8 0.9 fusion.130
  9.6 1.4 concatenate.48.ws
  11.0 28.4 %shard_map.263 = (bf16[2,1024,512]{2,1,0:T(8,128)(2,1)}, bf16[2,128,1024]{2,1,0:T(8,128)(2,1)}, bf16[2,128,1024]{2,1,0:T(8,128)(2,1)}, s32[2,128,8]{2,1,0:T(8,128)}) custom-call(bf16[32,512]{1,0:T(8,128)(2,1)} %concatenate.48.ws, bf16[128,1024]{1,0:T(8,128)(2,1)} %li.1, bf16[128,1024]{1,0:T(8,128)(2,1)} %cot.1, s32[128,8]{1,0:T(8,128)} %copy.96.routes), custom_call_target="tpu_custom_call" | custom-call | bytes 8000000 | tf_op jit(solution)/shard_map/pallas_call | solution.py:643
  39.4 1.4 fusion.18
  41.3 1.2 fusion.20
  42.6 1.7 fusion.37
  47.1 1.3 fusion.104
  48.7 0.8 copy.102.keyval
  51.4 0.8 copy.101.query
  52.2 1.2 fusion.121
  53.4 2.4 convolution_convert_fusion.1
  55.8 1.9 pad_add_fusion.2.info
  57.7 102.6 %shard_map.264 = (bf16[4,512,128]{2,1,0:T(8,128)(2,1)}, bf16[32,256,128]{2,1,0:T(8,128)(2,1)}, bf16[4,1024,256]{2,1,0:T(8,128)(2,1)}, bf16[16,80,1024]{2,1,0:T(8...) custom-call(s32[4]{0:T(128)} %pad_add_fusion.2.info, ...), custom_call_target="tpu_custom_call" | custom-call | flops 17999998976 | bytes 8000000 | tf_op jit(solution)/shard_map/pallas_call | solution.py:643
  160.3 1.4 fusion.62
  161.8 1.4 fusion.58
  163.1 1.4 fusion.55
  164.5 1.3 fusion.52
  166.3 1.4 select_reduce_fusion
  168.7 53.9 %shard_map.265 = (bf16[16,80,1024]{2,1,0:T(8,128)(2,1)}, f32[16,8,128]{2,1,0:T(8,128)}, bf16[256,1024]{1,0:T(8,128)(2,1)}, f32[256,128]{1,0:T(8,128)}) custom-call(bf16[128,1024]{1,0:T(8,128)(2,1)} %copy-done.10, f32[128,128]{1,0:T(8,128)} %pad.20.gates, bf16[16,80,256]{2,1,0:T(8,128)(2,1)} %get-tuple-element.119.pick), custom_call_target="tpu_custom_call" | custom-call | bytes 8000000 | tf_op jit(solution)/shard_map/pallas_call | solution.py:643
  222.6 0.9 slice_reduce_fusion
  223.5 2.2 fusion
  225.8 1.6 fusion.30
  227.8 1.5 fusion.24
  229.3 4.2 multiply_convert_fusion
  233.5 4.2 fusion.2
  238.4 5.5 %fusion.22 = f32[1280,1024]{1,0:T(8,128)} fusion(bf16[1280,512]{1,0:T(8,128)(2,1)} %get-tuple-element.75, bf16[1,1024,512]{2,1,0:T(8,128)(2,1)} %param.26), kind=kOutput, calls=%fused_computation.66 | convolution fusion | flops 1342177280 | bytes 7602176 | tf_op jit(solution)/shard_map/dot_general | solution.py:877
  243.9 1.2 eq.91
  245.1 2.9 copy.106
  248.6 6.3 %add_convert_fusion = bf16[1280,1024]{1,0:T(8,128)(2,1)} fusion(f32[1280,1024]{1,0:T(8,128)} %fusion.22, bf16[1280,512]{1,0:T(8,128)(2,1)} %get-tuple-element.76, bf16[1,1024,512]{2,1,0:T(8,128)(2,1)} %param.27), kind=kOutput, calls=%fused_computation.6 | convolution fusion | flops 1344798720 | bytes 10223616 | tf_op jit(solution)/shard_map/dot_general | solution.py:879
  255.0 1.1 fusion.43.pick_t
  256.0 49.2 %shard_map.266 = (f32[2,128,1024]{2,1,0:T(8,128)}, f32[2,16,128]{2,1,0:T(8,128)}) custom-call(bf16[16,80,1024]{2,1,0:T(8,128)(2,1)} %bitcast.247, f32[16,8,128]{2,1,0:T(8,128)} %pad.21.gg, bf16[16,80,256]{2,1,0:T(8,128)(2,1)} %get-tuple-element.119.pick, bf16[256,1280]{1,0:T(8,128)(2,1)} %fusion.43.pick_t), custom_call_target="tpu_custom_call" | custom-call | bytes 8000000 | tf_op jit(solution)/shard_map/pallas_call | solution.py:643
  305.2 0.7 select_bitcast_fusion.1
  306.2 1.0 fusion.95
  307.2 4.8 fusion.4
  312.1 2.5 fusion.5
  314.6 2.6 multiply_reduce_fusion.1
  318.0 1.1 fusion.9
  319.2 1.1 fusion.10
  320.3 1.2 fusion.11
  321.4 1.1 fusion.12
  322.5 2.1 fusion.60
  325.3 3.7 convolution_convert_fusion.4
  329.1 1.5 copy-done.5
  331.3 1.0 fusion.13.cg
  332.3 1.9 pad_maximum_fusion
  334.3 2.1 constant_dynamic-slice_fusion
  336.4 1.5 broadcast_select_fusion.2
  337.9 126.3 %shard_map.267 = (bf16[2,256,512]{2,1,0:T(8,128)(2,1)}, bf16[32,256,128]{2,1,0:T(8,128)(2,1)}, bf16[16,80,1024]{2,1,0:T(8,128)(2,1)}, bf16[2,32,32,256]{3,2,1,0:T(8,128)(2,1)}, bf16[3,1024,512]{2,1,0:T(8,128)(2,1)}) custom-call(s32[4]{0:T(128)} %pad_add_fusion.2.info, bf16[128,1024]{1,0:T(8,128)(2,1)} %fusion.13.cg, ...), custom_call_target="tpu_custom_call" | custom-call | flops 44999999488 | bytes 8000000 | tf_op jit(solution)/shard_map/pallas_call | solution.py:643
  464.2 1.1 fusion.73
  469.0 2.7 convolution_bitcast_fusion
  471.7 2.8 fusion.8
  474.5 0.9 slice_select_fusion.1.mix
  478.2 1.8 broadcast_select_fusion
  480.0 0.8 slice_select_fusion.back
  481.5 40.2 %shard_map.268 = (f32[32,512]{1,0:T(8,128)}, f32[128,1024]{1,0:T(8,128)}, f32[128,1024]{1,0:T(8,128)}, f32[24,128]{1,0:T(8,128)}) custom-call(bf16[32,32,512]{2,1,0:T(8,128)(2,1)} %bitcast.262, bf16[32,32,512]{2,1,0:T(8,128)(2,1)} %bitcast.261, f32[128,1024]{1,0:T(8,128)} %slice_select_fusion.back, f32[128,1024]{1,0:T(8,128)} %slice_select_fusion.1.mix, ...), custom_call_target="tpu_custom_call" | custom-call | bytes 8000000 | tf_op jit(solution)/shard_map/pallas_call | solution.py:643
  521.8 0.9 fusion.128
  522.6 1.4 slice.288
  524.0 1.3 fusion.122
  525.3 4.2 slice_convert_fusion
  530.8 0.8 convert_reduce_fusion
  531.6 1.6 maximum_convert_fusion
  533.9 1.2 add_convert_fusion.1
  535.8 1.6 copy.128
  (256 shorter events, 20.4 us)
Async XLA Ops:
  7.2 218.6 %copy-start = (bf16[1,512,1024]{2,1,0:T(8,128)(2,1)S(1)}, bf16[1,512,1024]{2,1,0:T(8,128)(2,1)}, u32[]{:S(2)}) copy-start(bf16[1,512,1024]{2,1,0:T(8,128)(2,1)} %param.28) | copy-start | bytes 3145732
  7.2 528.6 %all-reduce.8.cloned.1.call-start = ((), (), s32[]{:S(2)}) async-start(), calls=%async_computation | async-start | bytes 262144 | tf_op jit(solution)/shard_map/psum | solution.py:906
  39.4 4.8 copy-start.31
  44.7 2.2 copy-start.68
  45.1 3.5 copy-start.54
  46.2 6.0 %copy-start.51 = (pred[256,16,1]{0,1,2:T(8,128)(4,1)}, pred[256,16,1]{0,1,2:T(8,128)(4,1)S(1)}, u32[]{:S(2)}) copy-start(pred[256,16,1]{0,1,2:T(8,128)(4,1)S(1)} %copy.126) | copy-start | bytes 12292
  46.2 2.5 copy-start.46
  48.6 417.0 %copy-start.27 = (f32[256,32]{0,1:T(8,128)}, f32[256,32]{0,1:T(8,128)S(1)}, u32[]{:S(2)}) copy-start(f32[256,32]{0,1:T(8,128)S(1)} %get-tuple-element.131) | copy-start | bytes 98308
  48.6 417.0 %copy-start.29 = (f32[256,32]{0,1:T(8,128)}, f32[256,32]{0,1:T(8,128)S(1)}, u32[]{:S(2)}) copy-start(f32[256,32]{0,1:T(8,128)S(1)} %get-tuple-element.132) | copy-start | bytes 98308
  48.6 2.5 copy-start.66
  49.9 3.5 copy-start.33
  160.3 4.2 copy-start.2
  160.3 5.5 %copy-start.61 = (s32[128,8]{0,1:T(8,128)S(1)}, s32[128,8]{0,1:T(8,128)}, u32[]{:S(2)}) copy-start(s32[128,8]{0,1:T(8,128)} %param.29) | copy-start | bytes 12292
  160.3 5.5 %copy-start.25 = (bf16[128,1024]{1,0:T(8,128)(2,1)S(1)}, bf16[128,1024]{1,0:T(8,128)(2,1)}, u32[]{:S(2)}) copy-start(bf16[128,1024]{1,0:T(8,128)(2,1)} %li.1) | copy-start | bytes 786436
  161.7 4.4 copy-start.48
  166.0 1.8 copy-start.75
  166.0 1.8 copy-start.62
  166.3 2.4 copy-start.10
  225.8 1.7 copy-start.77
  225.8 2.0 copy-start.79
  227.8 1.5 copy-start.24
  229.3 4.2 copy-start.12
  233.5 4.2 copy-start.21
  243.9 4.0 copy-start.52
  248.6 6.3 %copy-start.6 = (s32[1280,256]{0,1:T(8,128)S(1)}, s32[1280,256]{0,1:T(8,128)}, u32[]{:S(2)}) copy-start(s32[1280,256]{0,1:T(8,128)} %copy.106) | copy-start | bytes 3932164
  256.0 50.2 %copy-start.11 = (bf16[128,1024]{1,0:T(8,128)(2,1)S(1)}, bf16[128,1024]{1,0:T(8,128)(2,1)}, u32[]{:S(2)}) copy-start(bf16[128,1024]{1,0:T(8,128)(2,1)} %copy-done.10) | copy-start | bytes 786436
  307.2 4.8 copy-start.20
  307.2 4.8 copy-start.78
  312.0 2.6 copy-start.34
  312.0 2.6 copy-start.49
  312.0 2.6 copy-start.63
  312.1 5.2 copy-start.76
  312.1 5.8 %copy-start.13 = (bf16[128,1024]{1,0:T(8,128)(2,1)S(1)}, bf16[128,1024]{1,0:T(8,128)(2,1)}, u32[]{:S(2)}) copy-start(bf16[128,1024]{1,0:T(8,128)(2,1)} %cot.1) | copy-start | bytes 786436
  317.2 5.3 copy-start.8
  318.0 6.7 %copy-start.59 = (f32[2,128]{1,0:T(2,128)S(1)}, f32[2,128]{1,0:T(2,128)}, u32[]{:S(2)}) copy-start(f32[2,128]{1,0:T(2,128)} %copy-done.58) | copy-start | bytes 3076
  325.3 3.8 copy-start.14
  329.0 1.6 copy-start.5
  334.2 2.1 copy-start.16
  334.2 2.1 copy-start.17
  334.3 2.1 copy-start.18
  334.3 2.1 copy-start.19
  464.2 1.5 copy-start.38
  464.2 1.5 copy-start.67
  465.6 1.7 copy-start.15
  468.8 6.6 %copy-start.22 = (bf16[256,256]{0,1:T(8,128)(2,1)}, bf16[256,256]{0,1:T(8,128)(2,1)S(1)}, u32[]{:S(2)}) copy-start(bf16[256,256]{0,1:T(8,128)(2,1)S(1)} %get-tuple-element.110) | copy-start | bytes 393220
  468.8 7.1 %copy-start.42 = (bf16[256,256]{0,1:T(8,128)(2,1)}, bf16[256,256]{0,1:T(8,128)(2,1)S(1)}, u32[]{:S(2)}) copy-start(bf16[256,256]{0,1:T(8,128)(2,1)S(1)} %get-tuple-element.109) | copy-start | bytes 393220
  471.7 3.7 copy-start.32
  474.5 2.3 copy-start.3
  474.5 1.5 copy-start.41
  474.5 1.5 copy-start.56
  474.5 1.5 copy-start.70
  478.2 2.7 copy-start.57
  478.2 2.7 copy-start.71
  478.2 2.7 copy-start.72
  525.3 4.3 copy-start.65
  525.3 5.4 copy-start.26
  530.7 3.1 copy-start.4
  530.7 3.1 copy-start.9
  530.7 3.1 copy-start.35
  530.7 3.1 copy-start.36
  530.8 3.1 copy-start.50
  530.8 3.1 copy-start.64
  530.8 3.1 copy-start.74
  533.9 3.5 copy-start.1
  (18 other events, 17.8 us)
Sparse Core Ops, SparseCore 0:
  307.3 181.2 all-reduce.7

commit v3 on v2

v3 whole, which is shorter than its diff:
```python
import jax
import jax.numpy as jnp
import numpy as np
from jax import lax
from jax.experimental import pallas as pl
from jax.experimental.pallas import tpu as pltpu
from jax.sharding import PartitionSpec as P

HEAD_SIZE = 64
TOPK = 8
BLOCK = 256
EPSILON = 1e-06
ROPE_BASE = 10000.0
PRECISE = lax.Precision.HIGHEST
SCALE = HEAD_SIZE ** (-0.5)

NB = 32
EARLY = 7
SLOTS = 80
GROUP = 4
MESH_ID = pl.DeviceIdType.MESH
F32 = jnp.float32
BF16 = jnp.bfloat16
NT = (((1,), (1,)), ((), ()))
NN = (((1,), (0,)), ((), ()))
TN = (((0,), (0,)), ((), ()))


def place():
    b = lax.axis_index("blk")
    h = lax.axis_index("head")
    y = b // 8
    r = lax.rem(b, 8)
    m = jnp.where(lax.rem(y, 2) == 0, r, 7 - r)
    return b, h // 2, lax.rem(h, 2), y, m


def member(m, j):
    return 8 * j + m + lax.rem(j, 2) * (7 - 2 * m)


def times(start, n, body):
    def step(i, carry):
        body(i)
        return carry

    lax.fori_loop(start, n, step, 0)


def signal(sem, blk, head):
    pl.semaphore_signal(sem, inc=1, device_id=(blk, head), device_id_type=MESH_ID)


def rows(start, size):
    return pl.ds(pl.multiple_of(start, size), size)


def to(src, dst, send, recv, blk, head):
    return pltpu.make_async_remote_copy(
        src, dst, send, recv, device_id=(blk, head), device_id_type=MESH_ID
    )


def settle(sem, part):
    pltpu.make_async_copy(part, part, sem).wait()


def settle_rows(sem, blocks, c):
    pl.when(c == 0)(lambda: settle(sem, blocks.at[pl.ds(0, 15)]))
    pl.when(c == 1)(lambda: settle(sem, blocks))


def greet_all(bar, b, xl, c, y, m):
    h = 2 * xl + c
    times(1, NB, lambda d: signal(bar, lax.rem(b + d, NB), h))
    times(0, NB, lambda d: signal(bar, lax.rem(b + d, NB), 2 * (1 - xl) + c))
    for dj in range(GROUP):
        j = member(m, lax.rem(y + dj, GROUP))
        signal(bar, j, 2 * xl + 1 - c)
    pl.semaphore_wait(bar, 2 * NB - 1 + GROUP)


def pad_queries(both, qp, i):
    left = lax.broadcasted_iota(jnp.int32, (512, 128), 1) < 64
    qp[i, 0:512] = jnp.where(left, both, 0.0).astype(BF16)
    qp[i, 512:1024] = jnp.where(left, pltpu.roll(both, 64, 1), 0.0).astype(BF16)


def on_pair(p, m, inside, edge):
    def each(i):
        qb = member(m, i)
        whole = (p >= 1) & (2 * p + 1 <= qb - 1)
        pl.when(whole)(lambda: inside(i))
        pl.when(jnp.logical_not(whole) & (2 * p <= qb + 1))(lambda: edge(i, qb))

    times(0, GROUP, each)


def by_head(values, left):
    one = jnp.sum(jnp.where(left, values, 0.0), axis=1, keepdims=True) / HEAD_SIZE
    two = jnp.sum(jnp.where(left, 0.0, values), axis=1, keepdims=True) / HEAD_SIZE
    return jnp.where(left, one, two)


def swapped(values, first):
    return jnp.where(first, pltpu.roll(values, 96, 1), pltpu.roll(values, 32, 1))


def row_scale(values):
    return lax.rsqrt(jnp.mean(values * values, axis=1, keepdims=True) + EPSILON)


def lanes_of(shape):
    lane = lax.broadcasted_iota(jnp.int32, shape, 1)
    return lane < 64, lax.rem(lane, 64) < 32


def slab(j):
    return j // 2, slice(128 * (j % 2), 128 * (j % 2) + 128), slice(
        256 + 128 * (j % 2), 384 + 128 * (j % 2)
    )


def forward_kernel(
    lengths, wq, wk, wvl, wo, li, cot, routes_t, attn_gain, q_gain, k_gain, pace, ffn_gain, router_t,
    w_out, far_out, li_out, q_out, kv_out, c_out,
    pick, raw, normed, wide_out, inv_out, ctx_out, mid_out, mixed_out, gates_out, turn, head_gain, router,
    ws, wv, far, li2, cot2, rt, xs, qs, kvst, qg, kvs, qp, vt, acc, accm, peer, ctx, ctx_in,
    sw, rw, sx, rx, s1, r1, s2, r2, s5, r5, s7, r7, ls,
):
    b, xl, c, y, m = place()
    h = 2 * xl + c
    sib = 2 * xl + 1 - c
    over = 2 * (1 - xl) + c
    odd = lax.rem(b + c, 2)
    e0, e1, total = lengths[0], lengths[0] + lengths[1], 512 * NB
    pairs = jnp.concatenate([wk[...].astype(F32), wvl[...].astype(F32)], axis=1)
    even = jnp.concatenate([pairs[:, 0:64], pairs[:, 128:192]], axis=1)
    other = jnp.concatenate([pairs[:, 64:128], pairs[:, 192:256]], axis=1)
    ws[:, 0:256] = wq[...]
    ws[:, 256:384] = even.astype(BF16)
    ws[:, 384:512] = other.astype(BF16)
    ws[:, 512:768] = wo[...]
    greet_all(pltpu.get_barrier_semaphore(), b, xl, c, y, m)

    def w_first(d):
        part = wv.at[c, rows(b * 32, 32)]
        return to(ws, part, sw.at[0], rw.at[0], lax.rem(b + d, NB), h)

    near = [
        to(routes_t, rt.at[c], sx.at[0], rx.at[0], b, sib),
        to(cot, cot2.at[rows(c * 128, 128)], sx.at[1], rx.at[1], b, sib),
        to(li, li2.at[xl], sx.at[2], rx.at[2], b, over),
    ]
    for item in near:
        item.start()
    times(1, NB, lambda d: w_first(d).start())
    wv[c, rows(b * 32, 32)] = ws[...]
    li2[xl] = li[...]
    cot2[rows(c * 128, 128)] = cot[...]
    rt[c] = routes_t[...]

    near[0].wait()
    both_routes = jnp.concatenate([rt[0], rt[1]], axis=1)
    mine = 2 * lax.broadcasted_iota(jnp.int32, (16, 256), 0) + odd
    chosen = jnp.zeros((16, 256), F32)
    for k in range(TOPK):
        chosen = jnp.where(both_routes[k : k + 1] == mine, 1.0, chosen)
    earlier = lax.broadcasted_iota(jnp.int32, (256, 256), 0) < lax.broadcasted_iota(
        jnp.int32, (256, 256), 1
    )
    rank = jnp.dot(
        chosen.astype(BF16), jnp.where(earlier, 1.0, 0.0).astype(BF16), preferred_element_type=F32
    )
    slot = lax.broadcasted_iota(jnp.int32, (80, 256), 0).astype(F32)
    for k in range(16):
        at = jnp.where(rank[k : k + 1] == slot, chosen[k : k + 1], 0.0)
        pick[k] = at.astype(BF16)
    near[1].wait()
    c_piece = rows_out(xs, c_out, b, xl, c, s5.at[0], lambda d: r5.at[0])
    c_same = pltpu.make_async_copy(xs.at[b // 2], c_out.at[15], ls.at[3])

    def fetch(d):
        k = lax.rem(b // 2 + d, 16)
        xs[k] = jnp.dot(pick[k], cot2[...], preferred_element_type=F32).astype(BF16)
        start_rows(c_piece, d, c, c_same)

    times(1, EARLY, fetch)

    near[2].wait()
    li_keep = pltpu.make_async_copy(li2, li_out, ls.at[7])
    li_keep.start()
    source2 = li2[...].reshape(256, 1024).astype(F32)
    normed[...] = (source2 * row_scale(source2) * attn_gain[...]).astype(BF16)

    settle(rw.at[0], wv.at[c, rows(0, 992)])
    w_sib = to(wv.at[c], wv.at[c], sx.at[3], rx.at[3], b, sib)
    w_sib.start()
    wo_over = to(wv.at[c, :, pl.ds(512, 256)], far.at[c], sx.at[4], rx.at[4], b, over)
    wo_over.start()
    left, first = lanes_of((256, 128))
    t = lax.broadcasted_iota(jnp.int32, (256, 128), 0)
    pos = 512 * b + 256 * (t // 128) + 128 * c + lax.rem(t, 128)
    opening = jnp.where(pos < e0, 0, jnp.where(pos < e1, e0, e1))
    angles = (pos - opening).astype(F32) * pace[...]
    turn[0] = jnp.cos(angles)
    sine = jnp.sin(angles)
    turn[1] = jnp.where(first, -sine, sine)
    head_gain[0:1] = jnp.concatenate([q_gain[...], q_gain[...]], axis=1)
    head_gain[1:2] = jnp.concatenate([k_gain[...], jnp.ones((1, 64), F32)], axis=1)
    router[...] = jnp.zeros_like(router)
    router[0:NB] = router_t[...]
    w_sib.wait()
    w_keep = pltpu.make_async_copy(wv, w_out, ls.at[8])
    w_keep.start()
    for i in range(2):
        raw[i] = jnp.dot(normed[...], wv[i, :, 0:512], preferred_element_type=F32)
    for j in range(GROUP):
        i, q_cols, kv_cols = slab(j)
        span = slice(128 * j, 128 * j + 128)
        u = raw[i, :, q_cols]
        n = u * lax.rsqrt(by_head(u * u, left) + EPSILON) * head_gain[0:1]
        turned = n * turn[0] + swapped(n, first) * turn[1]
        qs[:, span] = (turned.astype(BF16).astype(F32) * SCALE).astype(BF16)
        u = raw[i, :, kv_cols]
        n = u * lax.rsqrt(by_head(u * u, left) + EPSILON) * head_gain[1:2]
        turned = n * turn[0] + swapped(n, first) * turn[1]
        kvst[:, span] = jnp.where(left, turned, u).astype(BF16)

    def q_piece(dj, dc):
        j = lax.rem(y + dj, GROUP)
        cols = pl.ds(pl.multiple_of(j * 128, 128), 128)
        k = 2 * dj + dc
        src, dst = qs.at[:, cols], qg.at[y, rows(c * 256, 256)]
        if k == 0:
            return pltpu.make_async_copy(src, dst, ls.at[0])
        return to(src, dst, s1.at[k], r1.at[k], member(m, j), 2 * xl + lax.rem(c + dc, 2))

    q_pieces = [q_piece(dj, dc) for dj in range(GROUP) for dc in range(2)]

    def kv_piece(d):
        peer_b = lax.rem(b + d, NB)
        cols = pl.ds(pl.multiple_of((peer_b // 8) * 128, 128), 128)
        return to(kvst.at[:, cols], kvs.at[b], s2.at[0], r2.at[d], peer_b, h)

    for item in q_pieces:
        item.start()
    own_cols = pl.ds(pl.multiple_of(y * 128, 128), 128)
    kv_own = pltpu.make_async_copy(kvst.at[:, own_cols], kvs.at[b], ls.at[1])
    kv_own.start()
    times(1, NB, lambda d: kv_piece(d).start())
    times(EARLY, 17, fetch)
    for item in q_pieces:
        item.wait()
    kv_own.wait()
    q_keep = pltpu.make_async_copy(qg, q_out, ls.at[4])
    q_keep.start()
    for i in range(GROUP):
        pad_queries(qg[i].astype(F32), qp, i)
    acc[...] = jnp.zeros_like(acc)
    accm[...] = jnp.zeros_like(accm)
    vt[64:80] = jnp.ones((16, 512), BF16)

    def pair(dp):
        p = lax.rem(b // 2 + 16 - dp, 16)
        for kb in (2 * p, 2 * p + 1):

            @pl.when(kb != b)
            def _():
                kv_piece(lax.rem(b + NB - kb, NB)).wait_recv()

        vt[0:64] = (
            kvs[pl.ds(2 * p, 2)].reshape(512, 128).astype(F32).T[64:128].astype(BF16)
        )

        def scores(i):
            keys = kvs[pl.ds(2 * p, 2)].reshape(512, 128)
            return jnp.exp(lax.dot_general(keys, qp[i], NT, preferred_element_type=F32))

        def inside(i):
            acc[i] += jnp.dot(vt[...], scores(i).astype(BF16), preferred_element_type=F32)

        def edge(i, qb):
            low, high = limits(query_positions((1, 1024), 1, qb), e0, e1, total)
            kpos = key_positions((512, 1), 0, 2 * p, c)
            expo = jnp.where((kpos >= low) & (kpos < high), scores(i), 0.0)
            accm[i] += jnp.dot(vt[...], expo.astype(BF16), preferred_element_type=F32)

        on_pair(p, m, inside, edge)

    times(0, 16, pair)
    for i in range(GROUP):
        pos = query_positions((1, 1024), 1, member(m, i))
        acc[i] = accm[i] + jnp.where((pos >= e0) & (pos < e1), acc[i], 0.0)
    swap = to(acc, peer, sx.at[5], rx.at[5], b, sib)
    swap.start()
    kv_keep = pltpu.make_async_copy(kvs, kv_out, ls.at[5])
    kv_keep.start()
    wo_over.wait()
    far_sib = to(far.at[c], far.at[c], sx.at[6], rx.at[6], b, sib)
    far_sib.start()
    swap.wait()

    def ctx_piece(dj, dx):
        j = lax.rem(y + dj, GROUP)
        x2 = lax.rem(xl + dx, 2)
        cols = pl.ds(pl.multiple_of((4 * xl + y) * 128, 128), 128)
        src, dst = ctx.at[j, rows(c * 256 + x2 * 128, 128)], ctx_in.at[:, cols]
        k = 2 * dj + dx
        if k == 0:
            return pltpu.make_async_copy(src, dst, ls.at[6])
        return to(src, dst, s7.at[k], r7.at[k], member(m, j), 2 * x2 + c)

    ctx_pieces = [ctx_piece(dj, dx) for dj in range(GROUP) for dx in range(2)]
    for i in range(GROUP):
        both = acc[i] + peer[i]
        inverse = 1.0 / both[64:65]
        wide = both[0:64] * inverse
        flat = jnp.concatenate([wide[:, 0:512], wide[:, 512:1024]], axis=0).T
        wide_out[i] = flat
        ctx[i] = flat.astype(BF16)
        spread = jnp.broadcast_to(inverse, (64, 1024))
        inv_out[i] = jnp.concatenate([spread[:, 0:512], spread[:, 512:1024]], axis=0).T
    for item in ctx_pieces:
        item.start()
    far_sib.wait()
    wo_keep = pltpu.make_async_copy(far, far_out, ls.at[2])
    wo_keep.start()
    for item in ctx_pieces:
        item.wait()

    context = ctx_in[...]
    ctx_out[...] = context
    for i in range(2):
        for x2, part in ((xl, wv[i, :, 512:768]), (1 - xl, far[i])):
            cols = rows(512 * x2 + 256 * i, 256)
            mid_out[:, cols] = li[:, cols].astype(F32) + jnp.dot(
                context, part, preferred_element_type=F32
            )
    middle = mid_out[...]
    mixed = (middle * row_scale(middle) * ffn_gain[...]).astype(BF16)
    mixed_out[...] = mixed
    logits = lax.dot_general(
        mixed.astype(F32), router[...], NT, preferred_element_type=F32, precision=PRECISE
    )
    expert = lax.broadcasted_iota(jnp.int32, (128, 128), 0)
    hit = jnp.zeros((128, 128), F32)
    for k in range(TOPK):
        hit = jnp.where(routes_t[k : k + 1] == expert, 1.0, hit)
    hit = hit.T
    top = jnp.max(jnp.where(hit > 0.0, logits, -1e30), axis=1, keepdims=True)
    weight = jnp.where(hit > 0.0, jnp.exp(logits - top), 0.0)
    gates_out[...] = weight / jnp.sum(weight, axis=1, keepdims=True)

    settle(sw.at[0], wv.at[0, rows(0, 992)])
    settle(s2.at[0], kvs.at[pl.ds(0, NB - 1)])
    settle_rows(s5.at[0], xs, c)
    settle_rows(r5.at[0], xs, c)
    pl.when(c == 0)(c_same.wait)
    for item in (li_keep, w_keep, q_keep, kv_keep, wo_keep):
        item.wait()


def row_peer(b, xl, c, k):
    e = 2 * k + lax.rem(b + c, 2)
    apart = lax.rem(b // 4 + e // 4, 2)
    return e, 2 * (xl + apart - 2 * xl * apart) + c


def rows_out(src, dst, b, xl, c, send, recv):
    def piece(d):
        k = lax.rem(b // 2 + d, 16)
        e, head = row_peer(b, xl, c, k)
        return to(src.at[k], dst.at[d - 1], send, recv(d), e, head)

    return piece


def rows_home(src, dst, b, xl, c, send, recv):
    def piece(d):
        k = lax.rem(b // 2 + 16 - d, 16)
        e, head = row_peer(b, xl, c, k)
        return to(src.at[d - 1], dst.at[b // 2], send, recv, e, head)

    return piece


def start_rows(piece, d, c, local):
    pl.when((d < 16) | (c == 1))(lambda: piece(d).start())
    pl.when((d == 16) & (c == 0))(local.start)


def experts_kernel(
    mixed, gates, pick, up_rows, gate_w, up_w, down_w, middle_ref, cot, ffn_gain, router,
    wts_out, eo_out, ex_out, grad_out, low_out, small_out, router_out,
    tok, gt, xs, xl_rows, gs, gl, rs, rl, ggs, ggl, hid, gb, ub, og, mgs, ggt, mg_in, gg_in, gg_all,
    s1, r1, s2, r2, s3, r3, s4, r4, sx, rx, ls,
):
    b, xl, c, _, _ = place()
    h = 2 * xl + c
    sib = 2 * xl + 1 - c
    odd = lax.rem(b + c, 2)
    bar = pltpu.get_barrier_semaphore()

    def greet(d):
        e, head = row_peer(b, xl, c, lax.rem(b // 2 + d, 16))
        signal(bar, e, head)

    times(1, 16, greet)
    signal(bar, b, sib)
    pl.when(c == 1)(lambda: greet(0))
    pl.semaphore_wait(bar, 16 + c)
    near = [
        to(mixed, tok.at[rows(c * 128, 128)], sx.at[0], rx.at[0], b, sib),
        to(gates, gt.at[rows(c * 128, 128)], sx.at[1], rx.at[1], b, sib),
    ]
    for item in near:
        item.start()
    tok[rows(c * 128, 128)] = mixed[...]
    gt[rows(c * 128, 128)] = gates[...]
    near[0].wait()
    x_piece = rows_out(xs, xl_rows, b, xl, c, s1.at[0], lambda d: r1.at[(d - 1) // 4])
    x_same = pltpu.make_async_copy(xs.at[b // 2], xl_rows.at[15], ls.at[0])

    def fetch(d):
        k = lax.rem(b // 2 + d, 16)
        xs[k] = jnp.dot(pick[k], tok[...], preferred_element_type=F32).astype(BF16)
        start_rows(x_piece, d, c, x_same)

    times(1, 17, fetch)
    near[1].wait()
    high = gt[...].astype(BF16)
    rest = gt[...] - high.astype(F32)
    mid = rest.astype(BF16)
    low = (rest - mid.astype(F32)).astype(BF16)
    lane = lax.broadcasted_iota(jnp.int32, (80, 128), 1)
    g_piece = rows_out(gs, gl, b, xl, c, s2.at[0], lambda d: r2.at[(d - 1) // 4])
    g_same = pltpu.make_async_copy(gs.at[b // 2], gl.at[15], ls.at[1])

    def as_row(column):
        wide = jnp.concatenate([jnp.broadcast_to(column, (80, 128)), jnp.zeros((48, 128), F32)])
        return wide.T[0:8]

    def fetch_gate(d):
        k = lax.rem(b // 2 + d, 16)
        mine = pick[k]
        spread = (
            jnp.dot(mine, high, preferred_element_type=F32)
            + jnp.dot(mine, mid, preferred_element_type=F32)
            + jnp.dot(mine, low, preferred_element_type=F32)
        )
        column = jnp.sum(jnp.where(lane == 2 * k + odd, spread, 0.0), axis=1, keepdims=True)
        gs[k] = as_row(column)
        start_rows(g_piece, d, c, g_same)
        weights = mine.astype(F32) * column
        weights_high = weights.astype(BF16)
        wts_out[0, k] = weights_high
        wts_out[1, k] = (weights - weights_high.astype(F32)).astype(BF16)

    times(1, 17, fetch_gate)
    home = rows_home(rs, rl, b, xl, c, s3.at[0], r3.at[0])
    home_same = pltpu.make_async_copy(rs.at[15], rl.at[b // 2], ls.at[2])
    gg_home = rows_home(ggs, ggl, b, xl, c, s4.at[0], r4.at[0])
    gg_same = pltpu.make_async_copy(ggs.at[15], ggl.at[b // 2], ls.at[3])

    def arrived(sem, blocks, g, same):
        @pl.when((g < 3) | (c == 1))
        def _():
            settle(sem.at[g], blocks.at[pl.ds(0, 4)])

        @pl.when((g == 3) & (c == 0))
        def _():
            settle(sem.at[g], blocks.at[pl.ds(0, 3)])
            same.wait()

    def group(g):
        arrived(r1, xl_rows, g, x_same)
        x = xl_rows[pl.ds(4 * g, 4)].reshape(320, 1024)
        u = up_rows[pl.ds(4 * g, 4)].reshape(320, 1024).astype(F32)
        gate_pre = jnp.dot(x, gate_w[0], preferred_element_type=F32)
        up_pre = jnp.dot(x, up_w[0], preferred_element_type=F32)
        sig = jax.nn.sigmoid(gate_pre)
        act = gate_pre * sig
        hidden = (act * up_pre).astype(BF16)
        out = jnp.dot(hidden, down_w[0], preferred_element_type=F32).astype(BF16)
        eo_out[pl.ds(4 * g, 4)] = out.reshape(4, 80, 1024)
        gate_grad = jnp.sum(u * out.astype(F32), axis=1, keepdims=True)
        columns = []
        arrived(r2, gl, g, g_same)
        for n in range(4):
            ggs[4 * g + n] = as_row(gate_grad[80 * n : 80 * n + 80])
            start_rows(gg_home, 4 * g + n + 1, c, gg_same)
            row = jnp.concatenate([gl[4 * g + n], jnp.zeros((120, 128), F32)])
            columns.append(row.T[0:80, 0:1])
        out_grad = (jnp.concatenate(columns) * u).astype(BF16)
        hidden_grad = lax.dot_general(out_grad, down_w[0], NT, preferred_element_type=F32)
        gate_back = (hidden_grad * up_pre * sig * (1.0 + gate_pre * (1.0 - sig))).astype(BF16)
        up_back = (hidden_grad * act).astype(BF16)
        back = lax.dot_general(
            gate_back, gate_w[0], NT, preferred_element_type=F32
        ) + lax.dot_general(up_back, up_w[0], NT, preferred_element_type=F32)
        rs[pl.ds(4 * g, 4)] = back.astype(BF16).reshape(4, 80, 1024)
        for n in range(1, 5):
            start_rows(home, 4 * g + n, c, home_same)
        span = rows(320 * g, 320)
        hid[span] = hidden
        gb[span] = gate_back
        ub[span] = up_back
        og[span] = out_grad

    times(0, 4, group)
    for j in range(4):
        part = slice(256 * j, 256 * j + 256)
        x_turned = xl_rows[:, :, part].reshape(1280, 256)
        ex_out[0, part] = lax.dot_general(x_turned, gb[...], TN, preferred_element_type=F32).astype(BF16)
        ex_out[1, part] = lax.dot_general(x_turned, ub[...], TN, preferred_element_type=F32).astype(BF16)
        half = slice(512 * (j // 2), 512 * (j // 2) + 512)
        turned = hid[:, 256 * (j % 2) : 256 * (j % 2) + 256]
        ex_out[2, part] = lax.dot_general(turned, og[:, half], TN, preferred_element_type=F32).astype(BF16)

    settle_rows(r4.at[0], ggl, c)
    pl.when(c == 0)(gg_same.wait)
    for k in range(16):
        column = jnp.concatenate([ggl[k], jnp.zeros((120, 128), F32)]).T[0:80, 0:1]
        ggt[pl.ds(k, 1)] = jnp.sum(pick[k].astype(F32) * column, axis=0, keepdims=True)
    settle_rows(r3.at[0], rl, c)
    pl.when(c == 0)(home_same.wait)
    mgs[...] = lax.dot_general(
        pick[...].reshape(1280, 256), rl[...].reshape(1280, 1024), TN, preferred_element_type=F32
    )
    away = rows((1 - c) * 128, 128)
    own = rows(c * 128, 128)
    back_near = [
        to(ggt.at[:, away], gg_in, sx.at[3], rx.at[3], b, sib),
        to(mgs.at[away], mg_in, sx.at[2], rx.at[2], b, sib),
    ]
    for item in back_near:
        item.start()
    settle_rows(s1.at[0], xs, c)
    settle_rows(s2.at[0], gs, c)
    settle_rows(s3.at[0], rs, c)
    settle_rows(s4.at[0], ggs, c)
    back_near[0].wait()

    gg_all[...] = jnp.zeros_like(gg_all)
    for k in range(16):
        gg_all[pl.ds(2 * k + odd, 1)] = ggt[pl.ds(k, 1), own]
        gg_all[pl.ds(2 * k + 1 - odd, 1)] = gg_in[pl.ds(k, 1)]
    gate_grad = gg_all[...].T
    own_gates = gates[...]
    logit_grad = own_gates * (
        gate_grad - jnp.sum(own_gates * gate_grad, axis=1, keepdims=True)
    )
    router_out[...] = lax.dot_general(
        logit_grad, mixed[...].astype(F32), TN, preferred_element_type=F32, precision=PRECISE
    )[0:NB]
    routed = jnp.dot(
        logit_grad, router[...], preferred_element_type=F32, precision=PRECISE
    )
    back_near[1].wait()
    mixed_grad = mgs[own] + mg_in[...] + routed
    middle = middle_ref[...]
    scale = row_scale(middle)
    unit = middle * scale
    small_out[...] = jnp.sum(mixed_grad * unit, axis=0, keepdims=True)
    inner = mixed_grad * ffn_gain[...]
    grad = cot[...].astype(F32) + scale * (
        inner - unit * jnp.mean(inner * unit, axis=1, keepdims=True)
    )
    grad_out[...] = grad
    low_out[...] = grad.astype(BF16)


def backward_kernel(
    lengths, attn_grad, context, wv, far, q_ref, kv_ref, wide_ref, inv_ref, eo, ex,
    raw, normed, li2, head_gain, turn, attn_gain, ffn_part, wts, middle, grad, router_part,
    out, in_grad, w_out, wo_grad, small_out, router_out, ex_out,
    cg, cgs, qp, gp, gi, qt, gt, gti, dt, di, dqs, dkvt, stage, dq_acc,
    wo_other, wo_in, wo_sum, ex_in, ex_sum, ex_cross, dq, dkv, home, wo_parts,
    low, w_other, w_in, w_sum, w_land, back, back_in, mix, mix_in, small, four, many,
    r_land, r_four, r_tot,
    s1, r1, s2, r2, s3, r3, s4, r4, s5, r5, s6, r6, s7, r7, s8, r8, s9, r9, sa, ra, sx, rx, ls,
):
    b, xl, c, y, m = place()
    h = 2 * xl + c
    sib = 2 * xl + 1 - c
    over = 2 * (1 - xl) + c
    e0, e1, total = lengths[0], lengths[0] + lengths[1], 512 * NB
    bar = pltpu.get_barrier_semaphore()
    for dj in range(GROUP):
        j = member(m, lax.rem(y + dj, GROUP))
        signal(bar, j, 2 * (1 - xl) + 1 - c)
        signal(bar, j, 2 * xl + 1 - c)
    times(1, NB, lambda d: signal(bar, lax.rem(b + d, NB), h))
    times(0, NB, lambda d: signal(bar, lax.rem(b + d, NB), over))
    pl.semaphore_wait(bar, 2 * NB - 1 + 2 * GROUP)

    ex_swap = to(ex.at[:, rows((1 - c) * 512, 512)], ex_in, sx.at[1], rx.at[1], b, sib)
    ex_swap.start()
    ex_own = pltpu.make_async_copy(ex.at[:, rows(c * 512, 512)], ex_sum, ls.at[1])
    ex_own.start()
    turned_back = jnp.zeros((128, 1024), F32)
    for i in range(2):
        for x2, part in ((xl, wv[i, :, 512:768]), (1 - xl, far[i])):
            turned_back = turned_back + lax.dot_general(
                attn_grad[:, rows(512 * x2 + 256 * i, 256)], part, NT, preferred_element_type=F32
            )
    cg[...] = turned_back.astype(BF16)
    turns = [(dj, dx, dc) for dj in range(GROUP) for dx in range(2) for dc in range(2)]
    cg_pieces = []
    for k, (dj, dx, dc) in enumerate(turns):
        j = lax.rem(y + dj, GROUP)
        x2 = lax.rem(xl + dx, 2)
        cols = pl.ds(pl.multiple_of((4 * x2 + j) * 128, 128), 128)
        src, dst = cg.at[:, cols], cgs.at[y, rows(c * 256 + xl * 128, 128)]
        if k == 0:
            cg_pieces.append(pltpu.make_async_copy(src, dst, ls.at[0]))
        else:
            head = 2 * x2 + lax.rem(c + dc, 2)
            cg_pieces.append(to(src, dst, s1.at[0], r1.at[0], member(m, j), head))
    for item in cg_pieces:
        item.start()

    def tile(n):
        return router_part.at[rows(8 * (n // 8), 8), rows(128 * lax.rem(n, 8), 128)]

    def router_first(d):
        to_b = lax.rem(b + d, NB)
        return to(tile(to_b), r_land.at[b], s8.at[0], r8.at[0], to_b, h)

    times(1, NB, lambda d: router_first(d).start())
    r_land[b] = router_part[rows(8 * (b // 8), 8), rows(128 * lax.rem(b, 8), 128)]

    def out_part(x2, core):
        cols = pl.ds(pl.multiple_of(512 * x2 + 256 * core, 256), 256)
        return lax.dot_general(
            context[...], attn_grad[:, cols], TN, preferred_element_type=F32
        )

    for x2 in range(2):
        wo_other[x2] = out_part(x2, 1 - c).astype(BF16)
    wo_swap = to(wo_other, wo_in, sx.at[0], rx.at[0], b, sib)
    wo_swap.start()
    for i in range(GROUP):
        both = q_ref[i].astype(F32)
        pad_queries(both, qp, i)
        turned = both.T
        qt[i] = jnp.concatenate([turned[0:64], turned[64:128]], axis=1).astype(BF16)
    dq_acc[...] = jnp.zeros_like(dq_acc)
    wo_swap.wait()
    for x2 in range(2):
        wo_sum[x2] = (out_part(x2, c) + wo_in[x2].astype(F32)).astype(BF16)
    ex_swap.wait()
    ex_own.wait()
    ex_sum[...] = (ex_sum[...].astype(F32) + ex_in[...].astype(F32)).astype(BF16)
    cross = to(ex_sum, ex_cross, sx.at[2], rx.at[2], b, over)
    cross.start()

    def wo_piece(e):
        d, x2 = lax.rem(e, NB), lax.rem(xl + e // NB, 2)
        peer_b = lax.rem(b + d, NB)
        part = wo_sum.at[x2, rows(peer_b * 32, 32)]
        return to(part, wo_parts.at[NB * (e // NB) + b], s3.at[0], r3.at[0], peer_b, 2 * x2 + c)

    cg_pieces[0].wait()
    settle(r1.at[0], home.at[pl.ds(0, 3)])
    wo_parts[b] = wo_sum[xl, rows(b * 32, 32)]
    eo_piece = rows_home(eo, home, b, xl, c, s2.at[0], r2.at[0])
    eo_same = pltpu.make_async_copy(eo.at[15], home.at[b // 2], ls.at[2])
    times(1, 17, lambda d: start_rows(eo_piece, d, c, eo_same))
    times(1, 2 * NB, lambda e: wo_piece(e).start())
    left = lax.broadcasted_iota(jnp.int32, (512, 128), 1) < 64
    for i in range(GROUP):
        scaled = cgs[i].astype(F32) * inv_ref[i]
        pos = query_positions((512, 1), 0, member(m, i))
        mid_doc = (pos >= e0) & (pos < e1)
        terms = scaled * wide_ref[i]
        one = jnp.sum(jnp.where(left, terms, 0.0), axis=1, keepdims=True)
        two = jnp.sum(jnp.where(left, 0.0, terms), axis=1, keepdims=True)
        upper = jnp.where(left, 0.0, pltpu.roll(scaled, 64, 1))
        lower = jnp.where(left, 0.0, scaled)
        for part, val, term in ((0, upper, one), (512, lower, two)):
            span = pl.ds(part, 512)
            gp[i, span] = val.astype(BF16)
            gi[i, span] = jnp.where(mid_doc, val, 0.0).astype(BF16)
            dt[i, span] = jnp.broadcast_to(term, (512, 128))
            di[i, span] = jnp.broadcast_to(jnp.where(mid_doc, term, 0.0), (512, 128))
            lanes = pl.ds(part, 512)
            gt[i, :, lanes] = val.T[64:128].astype(BF16)
            gti[i, :, lanes] = jnp.where(mid_doc, val, 0.0).T[64:128].astype(BF16)

    def dkv_piece(kb):
        return to(stage.at[kb], dkv.at[b], s4.at[0], r4.at[0], kb, h)

    def pair(dp):
        p = lax.rem(b // 2 + 1 + dp, 16)
        dkvt[...] = jnp.zeros_like(dkvt)
        keys = kv_ref[pl.ds(2 * p, 2)].reshape(512, 128)

        def step(i, expo, g, gturn, dots):
            prob = lax.dot_general(g[i], keys, NT, preferred_element_type=F32)
            term = jnp.concatenate([dots[i]] * 4, axis=1)
            score_grad = (expo * (prob - term)).astype(BF16)
            dq_acc[i] += jnp.dot(score_grad, keys, preferred_element_type=F32)
            dkvt[0:64] += jnp.dot(qt[i], score_grad, preferred_element_type=F32)
            dkvt[64:128] += jnp.dot(gturn[i], expo.astype(BF16), preferred_element_type=F32)

        def scores(i):
            return jnp.exp(lax.dot_general(qp[i], keys, NT, preferred_element_type=F32))

        def inside(i):
            step(i, scores(i), gi, gti, di)

        def edge(i, qb):
            low, high = limits(query_positions((1024, 1), 0, qb), e0, e1, total)
            kpos = key_positions((1, 512), 1, 2 * p, c)
            expo = jnp.where((kpos >= low) & (kpos < high), scores(i), 0.0)
            step(i, expo, gp, gt, dt)

        on_pair(p, m, inside, edge)
        flat = dkvt[...].T.astype(BF16)
        for n in range(2):
            kb = 2 * p + n
            stage[kb] = flat[256 * n : 256 * n + 256]

            @pl.when(kb != b)
            def _():
                dkv_piece(kb).start()

    times(0, 6, pair)
    settle(r8.at[0], r_land.at[pl.ds(0, NB - 1)])
    part = r_land[0]
    for n in range(1, NB):
        part = part + r_land[n]
    r_four[h] = part
    router_near = [
        to(r_four.at[h], r_four.at[h], s9.at[d], r9.at[d], b, lax.rem(h + d, 4))
        for d in range(1, 4)
    ]
    for item in router_near:
        item.start()
    times(6, 11, pair)
    for item in router_near:
        item.wait()
    r_tot[...] = r_four[0] + r_four[1] + r_four[2] + r_four[3]
    home_tile = (rows(8 * (b // 8), 8), rows(128 * lax.rem(b, 8), 128))
    router_out[home_tile] = r_tot[...]

    def router_last(d):
        return to(r_tot, router_out.at[home_tile], sa.at[0], ra.at[0], lax.rem(b + d, NB), h)

    times(1, NB, lambda d: router_last(d).start())
    times(11, 16, pair)
    dkv[b] = stage[b]
    for i in range(GROUP):
        both = jnp.where(left, dq_acc[i, 0:512], pltpu.roll(dq_acc[i, 512:1024], 64, 1))
        dqs[i] = (both * SCALE).astype(BF16)

    def dq_piece(dj, dc):
        j = lax.rem(y + dj, GROUP)
        c2 = lax.rem(c + dc, 2)
        cols = pl.ds(pl.multiple_of(y * 128, 128), 128)
        src, dst = dqs.at[j, rows(c2 * 256, 256)], dq.at[c, :, cols]
        k = 2 * dj + dc
        if k == 0:
            return pltpu.make_async_copy(src, dst, ls.at[4])
        return to(src, dst, s5.at[k], r5.at[k], member(m, j), 2 * xl + c2)

    dq_pieces = [dq_piece(dj, dc) for dj in range(GROUP) for dc in range(2)]
    for item in dq_pieces:
        item.start()
    cross.wait()
    ex_in[...] = (ex_sum[...].astype(F32) + ex_cross[...].astype(F32)).astype(BF16)
    half = rows(c * 512, 512)
    ex_home = pltpu.make_async_copy(ex_in, ex_out.at[:, half], ls.at[5])
    ex_home.start()
    ex_back = to(ex_in, ex_out.at[:, half], sx.at[3], rx.at[3], b, sib)
    ex_back.start()
    for item in dq_pieces:
        item.wait()
    settle(r4.at[0], dkv.at[pl.ds(0, NB - 1)])

    left, first = lanes_of((256, 128))
    q_gain = jnp.zeros((1, 128), F32)
    k_gain = jnp.zeros((1, 128), F32)

    def unprep(d, u, gain, row):
        turned = d * turn[0] - swapped(d, first) * turn[1]
        scale = lax.rsqrt(by_head(u * u, left) + EPSILON)
        unit = u * scale
        inner = turned * row
        gain = gain + jnp.sum(turned * unit, axis=0, keepdims=True)
        return scale * (inner - unit * by_head(inner * unit, left)), gain

    for j in range(GROUP):
        i, q_cols, kv_cols = slab(j)
        span = slice(128 * j, 128 * j + 128)
        d = (dq[0, :, span].astype(F32) + dq[1, :, span].astype(F32)).astype(BF16).astype(F32)
        got, q_gain = unprep(d, raw[i, :, q_cols], q_gain, head_gain[0:1])
        low[i, :, q_cols] = got.astype(BF16)
        d = dkv[8 * j].astype(F32)
        for n in range(1, 8):
            d = d + dkv[8 * j + n].astype(F32)
        d = d.astype(BF16).astype(F32)
        got, k_gain = unprep(d, raw[i, :, kv_cols], k_gain, head_gain[1:2])
        low[i, :, kv_cols] = jnp.where(left, got, d).astype(BF16)
    w_other[...] = lax.dot_general(
        normed[...], low[1 - c], TN, preferred_element_type=F32
    ).astype(BF16).reshape(NB, 32, 512)
    w_swap = to(w_other, w_in, sx.at[4], rx.at[4], b, sib)
    w_swap.start()
    normed_grad = lax.dot_general(low[0], wv[0, :, 0:512], NT, preferred_element_type=F32) + lax.dot_general(
        low[1], wv[1, :, 0:512], NT, preferred_element_type=F32
    )
    source2 = li2[...].reshape(256, 1024).astype(F32)
    scale = row_scale(source2)
    unit = source2 * scale
    inner = normed_grad * attn_gain[...]
    back[...] = (scale * (inner - unit * jnp.mean(inner * unit, axis=1, keepdims=True))).reshape(
        2, 128, 1024
    )
    back_swap = to(back.at[1 - xl], back_in, sx.at[5], rx.at[5], b, over)
    back_swap.start()
    small[:, 0:1024] = jnp.sum(normed_grad * unit, axis=0, keepdims=True)
    small[:, 1024:2048] = ffn_part[...]
    small[:, 2048:2176] = q_gain
    small[:, 2176:2304] = k_gain
    near = [
        to(small, four.at[h], sx.at[6 + d], rx.at[6 + d], b, lax.rem(h + d, 4)) for d in range(1, 4)
    ]
    for item in near:
        item.start()
    four[h] = small[...]
    mine = lax.dot_general(normed[...], low[c], TN, preferred_element_type=F32)
    w_swap.wait()
    w_sum[...] = (mine.reshape(NB, 32, 512) + w_in[...].astype(F32)).astype(BF16)

    def w_piece(d):
        peer = lax.rem(b + d, NB)
        return to(w_sum.at[peer], w_land.at[b], s6.at[0], r6.at[0], peer, h)

    times(1, NB, lambda d: w_piece(d).start())
    w_land[b] = w_sum[b]
    for item in near:
        item.wait()
    many[b] = four[0] + four[1] + four[2] + four[3]

    def spread(d):
        return to(many.at[b], many.at[b], s7.at[0], r7.at[0], lax.rem(b + d, NB), h)

    times(1, NB, lambda d: spread(d).start())

    settle_rows(r2.at[0], home, c)
    pl.when(c == 0)(eo_same.wait)
    flat = home[...].reshape(1280, 1024)
    mix[...] = (
        lax.dot_general(wts[0].reshape(1280, 256), flat, TN, preferred_element_type=F32)
        + lax.dot_general(wts[1].reshape(1280, 256), flat, TN, preferred_element_type=F32)
    ).reshape(2, 128, 1024)
    mix_swap = to(mix.at[1 - c], mix_in, sx.at[6], rx.at[6], b, sib)
    mix_swap.start()
    settle(r3.at[0], wo_parts.at[pl.ds(0, 2 * NB - 1)])
    total = wo_parts[0].astype(F32)
    for n in range(1, 2 * NB):
        total = total + wo_parts[n].astype(F32)
    wo_grad[...] = total
    back_swap.wait()
    in_grad[...] = (grad[...] + back[xl] + back_in[...]).astype(BF16)
    mix_swap.wait()
    out[...] = (middle[...] + mix[c] + mix_in[...]).astype(BF16)
    settle(r7.at[0], many.at[pl.ds(0, NB - 1)])
    total = many[0]
    for n in range(1, NB):
        total = total + many[n]
    small_out[...] = total
    settle(r6.at[0], w_land.at[pl.ds(0, NB - 1)])
    shard = w_land[0].astype(F32)
    for n in range(1, NB):
        shard = shard + w_land[n].astype(F32)
    w_out[...] = shard
    ex_home.wait()
    ex_back.wait()
    settle(ra.at[0], r_land.at[pl.ds(0, NB - 1)])
    settle(s1.at[0], home.at[pl.ds(0, 3)])
    settle_rows(s2.at[0], home, c)
    settle(s3.at[0], wo_parts.at[pl.ds(0, 2 * NB - 1)])
    settle(s4.at[0], dkv.at[pl.ds(0, NB - 1)])
    settle(s6.at[0], w_land.at[pl.ds(0, NB - 1)])
    settle(s7.at[0], many.at[pl.ds(0, NB - 1)])
    settle(s8.at[0], r_land.at[pl.ds(0, NB - 1)])
    settle(sa.at[0], r_land.at[pl.ds(0, NB - 1)])


VM = pl.BlockSpec(memory_space=pltpu.VMEM)
SM = pl.BlockSpec(memory_space=pltpu.SMEM)
ANY = pl.BlockSpec(memory_space=pl.ANY)


def call(kernel, collective_id, ins, outs, scratch, sems, flops, *operands):
    return pl.pallas_call(
        kernel,
        out_shape=[jax.ShapeDtypeStruct(shape, dtype) for shape, dtype, _ in outs],
        in_specs=ins,
        out_specs=[spec for _, _, spec in outs],
        scratch_shapes=[pltpu.VMEM(shape, dtype) for shape, dtype in scratch]
        + [pltpu.SemaphoreType.DMA(n) for n in sems],
        compiler_params=pltpu.CompilerParams(
            collective_id=collective_id,
            has_side_effects=True,
            vmem_limit_bytes=60 * 1024 * 1024,
        ),
        cost_estimate=pl.CostEstimate(
            flops=flops, bytes_accessed=8_000_000, transcendentals=flops // 2000
        ),
    )(*operands)


def limits(pos, e0, e1, total):
    low = jnp.where(pos < e0, 0, jnp.where(pos < e1, e0, e1))
    end = jnp.where(pos < e0, e0, jnp.where(pos < e1, e1, total))
    reach = low + ((pos - low) // BLOCK + 1) * BLOCK
    return low, jnp.minimum(end, reach)


def query_positions(shape, axis, qb):
    r = lax.broadcasted_iota(jnp.int32, shape, axis)
    r = lax.rem(r, 512)
    return 512 * qb + 256 * lax.rem(r // 128, 2) + 128 * (r // 256) + lax.rem(r, 128)


def key_positions(shape, axis, kb, core):
    r = lax.broadcasted_iota(jnp.int32, shape, axis)
    return 512 * (kb + r // 256) + 256 * lax.rem(r // 128, 2) + 128 * core + lax.rem(r, 128)


def body(
    layer_input,
    attn_gain,
    w_query,
    key_weight,
    value_weight,
    w_output,
    query_gain,
    key_gain,
    ffn_gain,
    router,
    w_gate,
    w_up,
    w_down,
    routes,
    doc_lengths,
    cotangent,
):
    tokens, width = layer_input.shape
    lane = np.arange(128) % (HEAD_SIZE // 2)
    pace = jnp.asarray(ROPE_BASE ** (-2.0 * lane / HEAD_SIZE), F32)[None]
    (
        w_full, w_far, both_inputs, q_group, kv_all, up_rows,
        pick, raw, normed, ctx_wide, ctx_inv, context, middle, mixed_in, gates, turn, head_gain, router_wide,
    ) = call(
        forward_kernel,
        0,
        [SM] + [VM] * 13,
        [
            ((2, width, 768), BF16, ANY),
            ((2, width, width // 4), BF16, ANY),
            ((2, tokens, width), BF16, ANY),
            ((GROUP, 512, 128), BF16, ANY),
            ((NB, 256, 128), BF16, ANY),
            ((16, SLOTS, width), BF16, ANY),
            ((16, SLOTS, 2 * tokens), BF16, VM),
            ((2, 2 * tokens, 512), F32, VM),
            ((2 * tokens, width), BF16, VM),
            ((GROUP, 512, 128), F32, VM),
            ((GROUP, 512, 128), F32, VM),
            ((tokens, width), BF16, VM),
            ((tokens, width), F32, VM),
            ((tokens, width), BF16, VM),
            ((tokens, 128), F32, VM),
            ((2, 2 * tokens, 128), F32, VM),
            ((2, 128), F32, VM),
            ((128, width), F32, VM),
        ],
        [
            ((32, 768), BF16),
            ((2, width, 768), BF16),
            ((2, width, width // 4), BF16),
            ((2, tokens, width), BF16),
            ((2 * tokens, width), BF16),
            ((2, 8, 128), jnp.int32),
            ((16, SLOTS, width), BF16),
            ((2 * tokens, 512), BF16),
            ((2 * tokens, 512), BF16),
            ((GROUP, 512, 128), BF16),
            ((NB, 256, 128), BF16),
            ((GROUP, 1024, 128), BF16),
            ((80, 512), BF16),
            ((GROUP, 80, 1024), F32),
            ((GROUP, 80, 1024), F32),
            ((GROUP, 80, 1024), F32),
            ((GROUP, 512, 128), BF16),
            ((tokens, width), BF16),
        ],
        [(1,)] * 2 + [(7,)] * 2 + [(8,)] * 2 + [(1,), (NB,)] + [(1,)] * 2 + [(8,)] * 2 + [(9,)],
        18_000_000_000,
        doc_lengths,
        w_query,
        key_weight,
        value_weight,
        w_output,
        layer_input,
        cotangent,
        routes.T,
        attn_gain[None],
        query_gain[None],
        key_gain[None],
        pace,
        ffn_gain[None],
        router.T,
    )
    wts, expert_out, ex_grads, middle_grad, attn_grad, ffn_part, router_part = call(
        experts_kernel,
        1,
        [VM] * 11,
        [
            ((2, 16, SLOTS, 2 * tokens), BF16, VM),
            ((16, SLOTS, width), BF16, VM),
            ((3, 1024, 512), BF16, VM),
            ((tokens, width), F32, VM),
            ((tokens, width), BF16, VM),
            ((1, width), F32, VM),
            ((NB, width), F32, VM),
        ],
        [
            ((2 * tokens, width), BF16),
            ((2 * tokens, 128), F32),
            ((16, SLOTS, width), BF16),
            ((16, SLOTS, width), BF16),
            ((16, 8, 128), F32),
            ((16, 8, 128), F32),
            ((16, SLOTS, width), BF16),
            ((16, SLOTS, width), BF16),
            ((16, 8, 128), F32),
            ((16, 8, 128), F32),
            ((16 * SLOTS, 512), BF16),
            ((16 * SLOTS, 512), BF16),
            ((16 * SLOTS, 512), BF16),
            ((16 * SLOTS, width), BF16),
            ((2 * tokens, width), F32),
            ((16, 2 * tokens), F32),
            ((tokens, width), F32),
            ((16, tokens), F32),
            ((128, tokens), F32),
        ],
        [(1,), (4,), (1,), (4,)] + [(1,)] * 4 + [(4,)] * 2 + [(4,)],
        12_000_000_000,
        mixed_in,
        gates,
        pick,
        up_rows,
        w_gate,
        w_up,
        w_down,
        middle,
        cotangent,
        ffn_gain[None],
        router_wide,
    )
    layer_output, input_grad, w_shard, w_output_grad, smalls, router_grad, ex_sums = call(
        backward_kernel,
        2,
        [SM] + [VM] * 8 + [ANY, ANY] + [VM] * 11,
        [
            ((tokens, width), BF16, VM),
            ((tokens, width), BF16, VM),
            ((width // NB, 512), F32, VM),
            ((32, 256), F32, VM),
            ((1, 2304), F32, VM),
            ((NB, width), F32, VM),
            ((3, 1024, 512), BF16, ANY),
        ],
        [
            ((tokens, width), BF16),
            ((GROUP, 512, 128), BF16),
            ((GROUP, 1024, 128), BF16),
            ((GROUP, 1024, 128), BF16),
            ((GROUP, 1024, 128), BF16),
            ((GROUP, 64, 1024), BF16),
            ((GROUP, 64, 1024), BF16),
            ((GROUP, 64, 1024), BF16),
            ((GROUP, 1024, 128), F32),
            ((GROUP, 1024, 128), F32),
            ((GROUP, 512, 128), BF16),
            ((128, 512), F32),
            ((NB, 256, 128), BF16),
            ((GROUP, 1024, 128), F32),
            ((2, 1024, 256), BF16),
            ((2, 1024, 256), BF16),
            ((2, 1024, 256), BF16),
            ((3, 512, 512), BF16),
            ((3, 512, 512), BF16),
            ((3, 512, 512), BF16),
            ((2, 2 * tokens, 512), BF16),
            ((NB, 256, 128), BF16),
            ((16, SLOTS, width), BF16),
            ((2 * NB, 32, 256), BF16),
            ((2, 2 * tokens, 512), BF16),
            ((NB, 32, 512), BF16),
            ((NB, 32, 512), BF16),
            ((NB, 32, 512), BF16),
            ((NB, 32, 512), BF16),
            ((2, tokens, width), F32),
            ((tokens, width), F32),
            ((2, tokens, width), F32),
            ((tokens, width), F32),
            ((1, 2304), F32),
            ((4, 1, 2304), F32),
            ((NB, 1, 2304), F32),
            ((NB, 8, 128), F32),
            ((4, 8, 128), F32),
            ((8, 128), F32),
        ],
        [(1,)] * 8 + [(8,)] * 2 + [(1,)] * 6 + [(4,)] * 2 + [(1,)] * 2 + [(10,)] * 2 + [(6,)],
        45_000_000_000,
        doc_lengths,
        attn_grad,
        context,
        w_full,
        w_far,
        q_group,
        kv_all,
        ctx_wide,
        ctx_inv,
        expert_out,
        ex_grads,
        raw,
        normed,
        both_inputs,
        head_gain,
        turn,
        attn_gain[None],
        ffn_part,
        wts,
        middle,
        middle_grad,
        router_part,
    )
    smalls = smalls[0]
    down_sum = jnp.concatenate([ex_sums[2, :512], ex_sums[2, 512:]], axis=1)
    return (
        layer_output,
        input_grad,
        smalls[:1024],
        w_shard[:, :256],
        jnp.concatenate([w_shard[:, 256:320], w_shard[:, 384:448]], axis=1),
        jnp.concatenate([w_shard[:, 320:384], w_shard[:, 448:512]], axis=1),
        w_output_grad,
        smalls[2048:2112] + smalls[2112:2176],
        smalls[2176:2240],
        smalls[1024:2048],
        router_grad.T,
        ex_sums[0].astype(F32)[None],
        ex_sums[1].astype(F32)[None],
        down_sum.astype(F32)[None],
    )


def solution(mesh):
    everyone = P(("blk", "head"), None)
    both = P("blk", "head")
    expert = P("blk", None, None)
    return jax.shard_map(
        body,
        mesh=mesh,
        in_specs=(everyone, P(), both, both, both, both, P(), P(), P(), P())
        + (expert, expert, expert, everyone, P(), everyone),
        out_specs=(everyone, everyone, P(), both, both, both, both, P(), P(), P(), P())
        + (expert, expert, expert),
        check_vma=False,
    )
```

time: 553 us -> 405 us (0.73)
  matrix products: 66.6 us -> 0 us
  other arithmetic: 31.6 us -> 6.18 us
  local copies, waits for them, and re-layouts: 29.9 us -> 8.53 us
  Pallas kernels: 401 us -> 384 us
  between operations: 16 us -> 1.14 us
    dot_general x34 -> x0, matrix products: 66.6 us -> none  [the longest x1 6.33 us: body(): lax.dot_general(up_back, up_w, NT, preferred_element_type=F32)]
    pallas_call x6 -> x3, Pallas kernels: 401 us -> 384 us  [call(): pl.pallas_call(kernel, out_shape=[jax.ShapeDtypeStruct(shape, dtype) for...]
    convert_element_type x10 -> x0, other arithmetic: 8.73 us -> none  [the longest x1 2.23 us: body(): out_grad = (gate_rows * upstream_rows).astype(BF16)]
  transfers between devices with their start and end apart: 1 -> 0, of which waited for: 0 -> 0; matrix products, arithmetic and copies ran while one was open for 11% -> 0% of each run, Pallas kernels for 31% -> 0%
where the time goes in v3:
time: 405 us; the launch traced here: 400 us
  Pallas kernels  384 us (95%)
  local copies, waits for them, and re-layouts  8.53 us (2%)
  other arithmetic  6.18 us (2%)
    pallas_call x3, Pallas kernels, call(): pl.pallas_call(kernel, out_shape=[jax.ShapeDtypeStruct(shape, dtype) for...  384 us

profile of v3, /device:TPU:4, one launch (start us, length us, event | category | flops | bytes accessed | tf_op | source)
XLA Modules:
  0.0 399.7 jit_solution(5969619847851527170)
XLA Ops:
  0.6 121.9 %shard_map.272 = (bf16[2,1024,768]{2,1,0:T(8,128)(2,1)}, bf16[2,1024,256]{2,1,0:T(8,128)(2,1)}, bf16[2,128,1024]{2,1,0:T(8,128)(2,1)}, bf16[4,512,128]{2,1,0:T(8...) custom-call(s32[3]{0:T(128)} %lengths.3, ...), custom_call_target="tpu_custom_call" | custom-call | flops 17999998976 | bytes 8000000 | tf_op jit(solution)/shard_map/pallas_call | solution.py:900
  122.5 96.6 %shard_map.273 = (bf16[2,16,80,256]{3,2,1,0:T(8,128)(2,1)}, bf16[16,80,1024]{2,1,0:T(8,128)(2,1)}, bf16[3,1024,512]{2,1,0:T(8,128)(2,1)}, f32[128,1024]{1,0:T(8,...) custom-call(bf16[128,1024]{1,0:T(8,128)(2,1)} %get-tuple-element.46.mixed, ...), custom_call_target="tpu_custom_call" | custom-call | flops 12000000000 | bytes 8000000 | tf_op jit(solution)/shard_map/pallas_call | solution.py:900
  219.2 165.3 %shard_map.274 = (bf16[128,1024]{1,0:T(8,128)(2,1)}, bf16[128,1024]{1,0:T(8,128)(2,1)}, f32[32,512]{1,0:T(8,128)}, f32[32,256]{1,0:T(8,128)}, f32[1,2304]{1,0:T(...) custom-call(s32[3]{0:T(128)} %lengths.3, bf16[128,1024]{1,0:T(8,128)(2,1)} %get-tuple-element.52.attn_grad, ...), custom_call_target="tpu_custom_call" | custom-call | flops 44999999488 | bytes 8000000 | tf_op jit(solution)/shard_map/pallas_call | solution.py:900
  384.5 1.3 slice_bitcast_fusion
  385.8 1.3 fusion.2
  387.1 1.4 slice.55
  388.4 0.9 fusion.1
  389.3 0.7 pad_maximum_fusion
  390.0 1.3 fusion
  391.3 0.0 copy-start
  391.3 1.6 maximum_convert_fusion
  392.9 1.1 copy-done
  393.9 0.0 copy-start.2
  393.9 0.0 copy-start.1
  393.9 0.0 copy-start.4
  393.9 0.0 copy-start.3
  393.9 2.6 slice_convert_fusion
  396.5 0.0 copy-done.2
  396.6 0.7 copy.35
  397.3 0.0 copy-done.1
  397.3 0.7 copy.36
  398.0 0.0 copy-done.4
  398.0 0.6 copy.37
  398.6 0.0 copy-done.3
  398.6 0.7 copy.38
Async XLA Ops:
  391.3 2.6 copy-start
  393.9 2.6 copy-start.2
  393.9 3.3 copy-start.1
  393.9 4.0 %copy-start.4 = (f32[32,256]{1,0:T(8,128)S(1)}, f32[32,256]{1,0:T(8,128)}, u32[]{:S(2)}) copy-start(f32[32,256]{1,0:T(8,128)} %get-tuple-element.112) | copy-start | bytes 98308
  393.9 4.6 %copy-start.3 = (f32[32,1024]{1,0:T(8,128)S(1)}, f32[32,1024]{1,0:T(8,128)}, u32[]{:S(2)}) copy-start(f32[32,1024]{1,0:T(8,128)} %get-tuple-element.76) | copy-start | bytes 393220
